TPU v7x, 32 devices: a whole 2x2x4 slice. The times are simulated.
32 devices in a mesh: dp: 4 (over y, x), tensor: 8 (over z, core).
Axes of the slice: x: 2, y: 2, z: 4, core: 2. Of those that a mesh axis runs over, the one named last changes fastest.
Arguments:
- tokens: bfloat16 [1024, 4096], P(('dp', 'tensor')), may hold values from -6 to 6
- cotangent: bfloat16 [1024, 4096], P(('dp', 'tensor')), may hold values from -6 to 6
- gate_up: bfloat16 [2, 4096, 14336], P(None, 'dp', 'tensor'), may hold values from -0.09375 to 0.09375
- down_weight: bfloat16 [14336, 4096], P('tensor'), may hold values from -0.046875 to 0.046875
- first_code: bfloat16 [2, 4096, 14336], P(None, 'dp', 'tensor'), may hold values from -1 to 1
- first_scale: float32 [2, 256, 112], P(None, 'dp', 'tensor'), may hold values from 0.05 to 0.5
- second_code: bfloat16 [2, 4096, 14336], P(None, 'dp', 'tensor'), may hold values from 0.049804688 to 1
- second_scale: float32 [2, 256, 112], P(None, 'dp', 'tensor'), may hold values from 0.005 to 0.05
Outputs:
- input_grad: bfloat16 [1024, 4096], P(('dp', 'tensor'))
- new_gate_up: bfloat16 [2, 4096, 14336], P(None, 'dp', 'tensor')
- new_first_code: bfloat16 [2, 4096, 14336], P(None, 'dp', 'tensor')
- new_first_scale: float32 [2, 256, 112], P(None, 'dp', 'tensor')
- new_second_code: bfloat16 [2, 4096, 14336], P(None, 'dp', 'tensor')
- new_second_scale: float32 [2, 256, 112], P(None, 'dp', 'tensor')
All inputs are finite; a program needn't handle non-finite values. Where the computation divides by a largest or mean magnitude, that divisor is 1e-20 or more.
Results may differ from a plain program's by a relative error of at most 0.023.
Values may be sent and summed in bfloat16 or wider, within the bound.
No kernel may reach another device: no remote copies, remote signals or barrier semaphores. Data moves between devices by JAX's collectives and lax.ppermute only.
A program may use at most 256 MiB of HBM per device.

v0:
```python
import jax
import jax.numpy as jnp
from jax import lax
from jax.sharding import PartitionSpec as P

learning_rate = 0.003
beta_first = 0.9
beta_second = 0.95


def dequantize(code, scale):
    shape = code.shape
    blocks = code.astype(jnp.float32).reshape(shape[0], shape[1] // 16, 16, shape[2] // 128, 128)
    return (blocks * scale[:, :, None, :, None]).reshape(shape)


def requantize(state):
    shape = state.shape
    blocks = state.reshape(shape[0], shape[1] // 16, 16, shape[2] // 128, 128)
    peak = jnp.max(jnp.abs(blocks), axis=(2, 4)) + 1e-06
    code = (blocks / peak[:, :, None, :, None]).reshape(shape).astype(jnp.bfloat16)
    return (code, peak)


def shards(
    tokens, cotangent, gate_up, down_weight, first_code, first_scale, second_code, second_scale
):
    weights = lax.all_gather(gate_up, "dp", axis=1, tiled=True)
    group_tokens = lax.all_gather(tokens, "tensor", axis=0, tiled=True)
    pre = jnp.einsum("td,kdf->tkf", group_tokens, weights, preferred_element_type=jnp.float32)
    gate = pre[:, 0]
    upper = pre[:, 1]
    hidden_grad = lax.dot_general(
        lax.all_gather(cotangent, "tensor", axis=0, tiled=True),
        down_weight,
        (((1,), (1,)), ((), ())),
        preferred_element_type=jnp.float32,
    )
    sigma = jax.nn.sigmoid(gate)
    gate_grad = hidden_grad * upper * sigma * (1.0 + gate * (1.0 - sigma))
    upper_grad = hidden_grad * gate * sigma
    pre_grad = jnp.stack([gate_grad, upper_grad], axis=1).astype(jnp.bfloat16)
    own_rows = gate_up.shape[1]
    group_size = group_tokens.shape[0]
    columns = lax.all_to_all(group_tokens, "dp", split_axis=1, concat_axis=0, tiled=True)
    initial = jnp.zeros((own_rows, 2, gate_up.shape[2]), jnp.float32)
    total = initial
    piece = lax.all_gather(pre_grad, "dp", axis=0, tiled=True)
    for block in range(piece.shape[0] // group_size):
        rows = lax.dynamic_slice_in_dim(columns, block * group_size, group_size, 0)
        grads = piece[block * group_size : (block + 1) * group_size]
        partial_value = jnp.einsum(
            "td,tkf->dkf", rows, grads, preferred_element_type=jnp.float32
        ).astype(jnp.bfloat16)
        partial_value = lax.optimization_barrier(partial_value)
        total = total + partial_value.astype(jnp.float32)
    total_tokens = tokens.shape[0] * lax.axis_size("dp") * lax.axis_size("tensor")
    grad = jnp.transpose(total, (1, 0, 2)) / jnp.sqrt(jnp.float32(total_tokens))
    rows = pre_grad
    input_grad = lax.psum_scatter(
        jnp.einsum("tkf,kdf->td", rows, weights, preferred_element_type=jnp.float32).astype(
            jnp.bfloat16
        ),
        "tensor",
        scatter_dimension=0,
        tiled=True,
    )
    first = beta_first * dequantize(first_code, first_scale) + (1.0 - beta_first) * grad
    second = beta_second * dequantize(second_code, second_scale) + (1.0 - beta_second) * grad * grad
    updated = (
        gate_up.astype(jnp.float32) - learning_rate * first / (jnp.sqrt(second) + 1e-08)
    ).astype(jnp.bfloat16)
    code_one, scale_one = requantize(first)
    code_two, scale_two = requantize(second)
    return (input_grad, updated, code_one, scale_one, code_two, scale_two)


def solution(mesh):
    placed = (
        P(("dp", "tensor"), None),
        P(("dp", "tensor"), None),
        P(None, "dp", "tensor"),
        P("tensor", None),
        P(None, "dp", "tensor"),
        P(None, "dp", "tensor"),
        P(None, "dp", "tensor"),
        P(None, "dp", "tensor"),
    )
    return jax.shard_map(
        shards,
        mesh=mesh,
        in_specs=placed,
        out_specs=(
            P(("dp", "tensor"), None),
            P(None, "dp", "tensor"),
            P(None, "dp", "tensor"),
            P(None, "dp", "tensor"),
            P(None, "dp", "tensor"),
            P(None, "dp", "tensor"),
        ),
        check_vma=False,
    )
```

profile of v0, /device:TPU:0, one launch (start us, length us, event | category | flops | bytes accessed | tf_op | source)
XLA Modules:
  0.0 775.6 jit_solution(624773020471606972)
XLA Ops:
  7.2 0.0 all-gather.7.cloned.1.call-start
  7.2 0.7 all-gather.7.cloned.1.call-update
  7.9 0.0 all-gather.9.cloned.1.call-start
  7.9 0.7 all-gather.9.cloned.1.call-update
  8.6 0.0 all-gather.5.cloned.1.call-start
  8.7 0.7 all-gather.5.cloned.1.call-update
  9.4 0.0 all-gather.11.cloned.1.call-start
  9.4 32.0 %all-gather.7.cloned.1.call-done = bf16[256,4096]{1,0:T(8,128)(2,1)} async-done(((bf16[32,4096]{1,0:T(8,128)(2,1)}), bf16[256,4096]{1,0:T(8,128)(2,1)}) %all-gather.7.cloned.1.call-update) | async-done | bytes 2097168 | tf_op jit(solution)/shard_map/all_gather | solution.py:29
  41.4 263.7 %all-gather.9.cloned.1.call-done = bf16[2,4096,1792]{2,1,0:T(8,128)(2,1)} async-done(((bf16[2,1024,1792]{2,1,0:T(8,128)(2,1)}), bf16[2,4096,1792]{2,1,0:T(8,128)(2,1)}) %all-gather.9.cloned.1.call-update) | async-done | bytes 29360144 | tf_op jit(solution)/shard_map/all_gather | solution.py:28
  305.1 15.4 %fusion.1 = f32[256,2,1792]{2,0,1:T(8,128)} fusion(bf16[2,4096,1792]{2,1,0:T(8,128)(2,1)} %all-gather.9.cloned.1.call-done, bf16[256,4096]{1,0:T(8,128)(2,1)} %all-gather.7.cloned.1.call-done), kind=kOutput, calls=%fused_computation.13 | convolution fusion | flops 7516192768 | bytes 35127296 | tf_op jit(solution)/shard_map/td,kdf->tkf/dot_general | solution.py:30
  320.5 15.4 %all-gather.5.cloned.1.call-done = bf16[256,4096]{1,0:T(8,128)(2,1)} async-done(((bf16[32,4096]{1,0:T(8,128)(2,1)}), bf16[256,4096]{1,0:T(8,128)(2,1)}) %all-gather.5.cloned.1.call-update) | async-done | bytes 2097168 | tf_op jit(solution)/shard_map/all_gather | solution.py:34
  335.8 11.3 %fusion.12 = (bf16[256,1,1792]{2,0,1:T(8,128)(2,1)S(1)}, bf16[256,1,1792]{2,0,1:T(8,128)(2,1)S(1)}) fusion(f32[256,2,1792]{2,0,1:T(8,128)} %fusion.1, bf16[256,4096]{1,0:T(8,128)(2,1)} %all-gather.5.cloned.1.call-done, bf16[1792,4096]{1,0:T(8,128)(2,1)} %param.11), kind=kOutput, calls=%fused_computation.29 | convolution fusion | flops 3764060160 | bytes 22282240 | tf_op jit(solution)/shard_map/dot_general | solution.py:33
  347.1 0.0 copy-start.2
  347.1 1.5 pad_maximum_fusion
  348.6 0.0 all-gather.11.cloned.1.call-update
  348.7 0.0 copy-start.3
  348.7 10.3 %copy.50 = bf16[2,1024,1792]{1,2,0:T(8,128)(2,1)} copy(bf16[2,1024,1792]{2,1,0:T(8,128)(2,1)} %param.10) | data formatting | bytes 14680064 | tf_op args[2]
  359.0 0.0 copy-done.2
  359.0 0.0 copy-done.3
  359.0 0.1 copy.52
  359.1 6.8 mul.86
  365.9 16.9 %mul.87 = f32[2,1024,1792]{2,1,0:T(8,128)} reshape(f32[2,64,16,14,128]{4,3,2,1,0:T(8,128)} %mul.86) | data formatting | bytes 29360128 | tf_op jit(solution)/shard_map/mul | solution.py:14
  382.8 14.5 %copy.53 = f32[2,1024,1792]{1,2,0:T(8,128)} copy(f32[2,1024,1792]{2,1,0:T(8,128)} %mul.87) | data formatting | bytes 29360128 | tf_op jit(solution)/shard_map/mul | solution.py:14
  397.2 0.0 copy-start.4
  397.2 9.9 %copy.51 = bf16[2,1024,1792]{1,2,0:T(8,128)(2,1)} copy(bf16[2,1024,1792]{2,1,0:T(8,128)(2,1)} %param.12) | data formatting | bytes 14680064 | tf_op args[4]
  407.1 0.0 copy-done.4
  407.1 0.1 copy.60
  407.2 6.8 mul.96
  414.1 16.9 %mul.97 = f32[2,1024,1792]{2,1,0:T(8,128)} reshape(f32[2,64,16,14,128]{4,3,2,1,0:T(8,128)} %mul.96) | data formatting | bytes 29360128 | tf_op jit(solution)/shard_map/mul | solution.py:14
  431.0 14.5 %copy.61 = f32[2,1024,1792]{1,2,0:T(8,128)} copy(f32[2,1024,1792]{2,1,0:T(8,128)} %mul.97) | data formatting | bytes 29360128 | tf_op jit(solution)/shard_map/mul | solution.py:14
  445.5 0.0 copy-start.1
  445.5 10.1 %copy.59 = bf16[2,1024,1792]{1,2,0:T(8,128)(2,1)} copy(bf16[2,1024,1792]{2,1,0:T(8,128)(2,1)} %param.14) | data formatting | bytes 14680064 | tf_op args[6]
  455.6 0.0 copy-done.1
  455.6 1.5 copy.77
  457.1 3.7 all-to-all-start
  460.9 0.0 reduce-scatter.2.cloned.1.call-start
  460.9 14.9 %fusion = bf16[256,4096]{1,0:T(8,128)(2,1)} fusion(bf16[2,4096,1792]{2,1,0:T(8,128)(2,1)} %all-gather.9.cloned.1.call-done, bf16[256,1,1792]{2,0,1:T(8,128)(2,1)} %copy-done.2, bf16[256,1,1792]{2,0,1:T(8,128)(2,1)S(1)} %get-tuple-element.33), kind=kOutput, calls=%fused_computation.11 | convolution fusion | flops 7518158848 | bytes 33292288 | tf_op jit(solution)/shard_map/tkf,kdf->td/dot_general | solution.py:61
  475.7 0.0 reduce-scatter.2.cloned.1.call-update
  475.8 10.5 %all-to-all-done = bf16[256,4,1024]{2,0,1:T(8,128)(2,1)S(1)} async-done(((bf16[256,4,1024]{2,0,1:T(8,128)(2,1)}), bf16[256,4,1024]{2,0,1:T(8,128)(2,1)S(1)}, u32[]{:S(2)}, u32[]{:S(2)}) %all-to-all-start) | async-done | bytes 2097184 | tf_op jit(solution)/shard_map/all_to_all | solution.py:45
  486.3 0.0 all-gather.11.cloned.1.call-done
  486.3 6.8 convert_bitcast_fusion
  493.1 0.0 copy-done
  493.1 5.2 convert_bitcast_fusion.1
  498.3 5.2 convert_bitcast_fusion.2
  503.4 5.1 convert_bitcast_fusion.3
  508.5 45.5 %fusion.14 = (f32[2,1024,1792]{1,2,0:T(8,128)}, f32[2,1024,1792]{1,2,0:T(8,128)}, f32[2,1024,1792]{1,2,0:T(8,128)}, f32[2,1024,1792]{1,2,0:T(8,128)}) fusion(bf16[1024,2,1792]{0,2,1:T(8,128)(2,1)} %convert_bitcast_fusion, bf16[1024,2,1792]{0,2,1:T(8,128)(2,1)} %convert_bitcast_fusion.1, bf16[1024,2,1792]{0,2,1:T(8,128)(2,1)} %convert_bitcast_fusion.2, ...), kind=kLoop, calls=%fused_computation.37 | loop fusion | flops 77070336 | bytes 132120576 | tf_op jit(solution)/shard_map/abs | solution.py:20
  554.1 14.3 %copy.64 = f32[2,1024,1792]{2,1,0:T(8,128)} copy(f32[2,1024,1792]{1,2,0:T(8,128)} %get-tuple-element.28) | data formatting | bytes 29360128 | tf_op jit(solution)/shard_map/abs | solution.py:20
  568.4 16.9 %abs.15 = f32[2,64,16,14,128]{4,3,2,1,0:T(8,128)} reshape(f32[2,1024,1792]{2,1,0:T(8,128)} %copy.64) | data formatting | bytes 29360128 | tf_op jit(solution)/shard_map/abs | solution.py:20
  585.3 6.7 reduce_max.19
  592.0 0.7 copy.70
  592.7 6.9 div.41
  599.6 16.9 %div.42 = f32[2,1024,1792]{2,1,0:T(8,128)} reshape(f32[2,64,16,14,128]{4,3,2,1,0:T(8,128)} %div.41) | data formatting | bytes 29360128 | tf_op jit(solution)/shard_map/div | solution.py:21
  616.4 14.3 %copy.65 = f32[2,1024,1792]{1,2,0:T(8,128)} copy(f32[2,1024,1792]{2,1,0:T(8,128)} %div.42) | data formatting | bytes 29360128 | tf_op jit(solution)/shard_map/div | solution.py:21
  630.8 14.3 %copy.62 = f32[2,1024,1792]{2,1,0:T(8,128)} copy(f32[2,1024,1792]{1,2,0:T(8,128)} %get-tuple-element.26) | data formatting | bytes 29360128 | tf_op jit(solution)/shard_map/abs | solution.py:20
  645.1 16.9 %abs.13 = f32[2,64,16,14,128]{4,3,2,1,0:T(8,128)} reshape(f32[2,1024,1792]{2,1,0:T(8,128)} %copy.62) | data formatting | bytes 29360128 | tf_op jit(solution)/shard_map/abs | solution.py:20
  662.0 6.7 reduce_max.18
  668.7 0.7 copy.68
  669.4 6.9 div.38
  676.3 16.9 %div.39 = f32[2,1024,1792]{2,1,0:T(8,128)} reshape(f32[2,64,16,14,128]{4,3,2,1,0:T(8,128)} %div.38) | data formatting | bytes 29360128 | tf_op jit(solution)/shard_map/div | solution.py:21
  693.1 14.3 %copy.63 = f32[2,1024,1792]{1,2,0:T(8,128)} copy(f32[2,1024,1792]{2,1,0:T(8,128)} %div.39) | data formatting | bytes 29360128 | tf_op jit(solution)/shard_map/div | solution.py:21
  707.4 31.4 %divide_convert_fusion = (bf16[2,1024,1792]{1,2,0:T(8,128)(2,1)}, bf16[2,1024,1792]{1,2,0:T(8,128)(2,1)}, bf16[2,1024,1792]{1,2,0:T(8,128)(2,1)}) fusion(f32[2,1024,1792]{1,2,0:T(8,128)} %get-tuple-element.29, f32[2,1024,1792]{1,2,0:T(8,128)} %copy.65, f32[2,1024,1792]{1,2,0:T(8,128)} %get-tuple-element.27, bf16[2,1024,1792]{1,2,0:T(8,128)(2,1)} %copy.50, ...), kind=kLoop, calls=%fused_computation.2 | loop fusion | flops 36700160 | bytes 88080384 | tf_op jit(solution)/shard_map/convert_element_type | solution.py:21
  738.8 9.9 %copy.66 = bf16[2,1024,1792]{2,1,0:T(8,128)(2,1)} copy(bf16[2,1024,1792]{1,2,0:T(8,128)(2,1)} %get-tuple-element.31) | data formatting | bytes 14680064
  748.7 9.9 %copy.67 = bf16[2,1024,1792]{2,1,0:T(8,128)(2,1)} copy(bf16[2,1024,1792]{1,2,0:T(8,128)(2,1)} %get-tuple-element.32) | data formatting | bytes 14680064
  758.6 9.9 %copy.69 = bf16[2,1024,1792]{2,1,0:T(8,128)(2,1)} copy(bf16[2,1024,1792]{1,2,0:T(8,128)(2,1)} %get-tuple-element.30) | data formatting | bytes 14680064
  (4 shorter events, 0.0 us)
Async XLA Ops:
  7.2 34.3 %all-gather.7.cloned.1.call-start = ((), (), s32[]{:S(2)}) async-start(), calls=%async_computation.3 | async-start | bytes 2359296 | tf_op jit(solution)/shard_map/all_gather | solution.py:29
  7.9 297.2 %all-gather.9.cloned.1.call-start = ((), (), s32[]{:S(2)}) async-start(), calls=%async_computation.4 | async-start | bytes 36700160 | tf_op jit(solution)/shard_map/all_gather | solution.py:28
  8.6 327.2 %all-gather.5.cloned.1.call-start = ((), (), s32[]{:S(2)}) async-start(), calls=%async_computation.2 | async-start | bytes 2359296 | tf_op jit(solution)/shard_map/all_gather | solution.py:34
  9.4 476.9 %all-gather.11.cloned.1.call-start = ((), (), s32[]{:S(2)}) async-start(), calls=%async_computation.6 | async-start | bytes 9175040 | tf_op jit(solution)/shard_map/all_gather | solution.py:48
  347.1 11.9 %copy-start.2 = (bf16[256,1,1792]{2,0,1:T(8,128)(2,1)}, bf16[256,1,1792]{2,0,1:T(8,128)(2,1)S(1)}, u32[]{:S(2)}) copy-start(bf16[256,1,1792]{2,0,1:T(8,128)(2,1)S(1)} %get-tuple-element.34) | copy-start | bytes 2752516
  348.7 10.3 %copy-start.3 = (f32[2,64,14]{1,0,2:T(2,128)S(1)}, f32[2,64,14]{1,0,2:T(2,128)}, u32[]{:S(2)}) copy-start(f32[2,64,14]{1,0,2:T(2,128)} %param.13) | copy-start | bytes 21508
  397.2 9.9 %copy-start.4 = (f32[2,64,14]{1,0,2:T(2,128)S(1)}, f32[2,64,14]{1,0,2:T(2,128)}, u32[]{:S(2)}) copy-start(f32[2,64,14]{1,0,2:T(2,128)} %param.15) | copy-start | bytes 21508
  445.5 10.1 %copy-start.1 = (bf16[256,4096]{1,0:T(8,128)(2,1)S(1)}, bf16[256,4096]{1,0:T(8,128)(2,1)}, u32[]{:S(2)}) copy-start(bf16[256,4096]{1,0:T(8,128)(2,1)} %all-gather.7.cloned.1.call-done) | copy-start | bytes 6291460
  457.1 29.2 %all-to-all-start = ((bf16[256,4,1024]{2,0,1:T(8,128)(2,1)}), bf16[256,4,1024]{2,0,1:T(8,128)(2,1)S(1)}, u32[]{:S(2)}, u32[]{:S(2)}) async-start(bf16[256,4,1024]{2,0,1:T(8,128)(2,1)} %bitcast.76), calls=%async_computation.1 | async-start | bytes 4194304 | tf_op jit(solution)/shard_map/all_to_all | solution.py:45
  460.9 307.7 %reduce-scatter.2.cloned.1.call-start = ((), (), s32[]{:S(2)}) async-start(), calls=%async_computation.5 | async-start | bytes 2359296 | tf_op jit(solution)/shard_map/reduce_scatter | solution.py:60
  486.3 6.8 copy-start
Sparse Core Ops, SparseCore 0:
  9.6 31.7 all-gather.6
  43.3 261.7 all-gather.8
  306.7 29.0 all-gather.4
  348.8 78.3 all-gather.10
  475.9 36.0 reduce-scatter.1
where the time goes:
time: 789 us; the launch traced here: 776 us
  waiting for transfers between devices  324 us (41%)
  local copies, waits for them, and re-layouts  278 us (35%)
  other arithmetic  91.8 us (12%)
  matrix products  63.7 us (8%)
  between operations  14.3 us (2%)
    all_gather x1, waiting for transfers between devices, shards(): weights = lax.all_gather(gate_up, 'dp', axis=1, tiled=True)  264 us
    mul x6, local copies, waits for them, and re-layouts, dequantize(): return (blocks * scale[:, :, None, :, None]).reshape(shape)  76.4 us
    div x6, local copies, waits for them, and re-layouts, requantize(): blocks / peak[:, :, None, :, None]  76.1 us
    abs x4, local copies, waits for them, and re-layouts, requantize(): peak = jnp.max(jnp.abs(blocks), axis=(2, 4)) + 1e-06  62.4 us
    unnamed x20, local copies, waits for them, and re-layouts  61.7 us
    abs x1, other arithmetic, requantize(): peak = jnp.max(jnp.abs(blocks), axis=(2, 4)) + 1e-06  45.5 us
    all_gather x1, waiting for transfers between devices, shards(): group_tokens = lax.all_gather(tokens, 'tensor', axis=0, tiled=True)  32 us
    convert_element_type x1, other arithmetic, requantize(): (blocks / peak[:, :, None, :, None]).reshape(shape).astype(jnp.bfloat16)  31.4 us
  transfers between devices with their start and end apart: 6, of which 4 were waited for; matrix products, arithmetic and copies ran while one was open for 54% of the time, Pallas kernels for 0%

commit v1 on v0

v1 whole, which is shorter than its diff:
```python
import functools

import jax
import jax.numpy as jnp
from jax import lax
from jax.experimental import pallas as pl
from jax.experimental.pallas import tpu as pltpu
from jax.sharding import PartitionSpec as P

learning_rate = 0.003
beta_first = 0.9
beta_second = 0.95
f32 = jnp.float32
bf16 = jnp.bfloat16


def swap(value, mask):
    return lax.ppermute(value, "dp", [(p, p ^ mask) for p in range(lax.axis_size("dp"))])


def pair(value):
    return lax.ppermute(value, "tensor", [(p, p ^ 1) for p in range(lax.axis_size("tensor"))])


def ring(value):
    size = lax.axis_size("tensor")
    return lax.ppermute(value, "tensor", [(p, (p + 2) % size) for p in range(size)])


def adam_kernel(parts, total_tokens, *refs):
    token_refs = refs[:parts]
    grad_refs = refs[parts : 2 * parts]
    weight_ref, first_ref, first_scale_ref, second_ref, second_scale_ref = refs[2 * parts : 2 * parts + 5]
    out_weight, out_first, out_first_scale, out_second, out_second_scale, total = refs[-6:]
    value = None
    for token_ref, grad_ref in zip(token_refs, grad_refs):
        term = jnp.dot(token_ref[...], grad_ref[0], preferred_element_type=f32)
        value = term if value is None else value + term
    total[...] = value
    rows, columns = total.shape
    step = 8
    inverse = 1.0 / (float(total_tokens) ** 0.5)

    def body(at, carry):
        span = pl.ds(pl.multiple_of(at * step * 16, step * 16), step * 16)
        blocks = pl.ds(pl.multiple_of(at * step, step), step)
        shape = (step, 16, columns)
        grad = (total[span, :] * inverse).reshape(shape)
        first = first_ref[0, span, :].astype(f32).reshape(shape) * first_scale_ref[0, blocks][:, None, :]
        second = second_ref[0, span, :].astype(f32).reshape(shape) * second_scale_ref[0, blocks][:, None, :]
        first = beta_first * first + (1.0 - beta_first) * grad
        second = beta_second * second + (1.0 - beta_second) * grad * grad
        weight = weight_ref[0, span, :].astype(f32).reshape(shape)
        weight = weight - learning_rate * first / (jnp.sqrt(second) + 1e-08)
        out_weight[0, span, :] = weight.reshape(step * 16, columns).astype(bf16)
        for state, code_ref, scale_ref in ((first, out_first, out_first_scale), (second, out_second, out_second_scale)):
            peak = jnp.max(jnp.abs(state), axis=1)
            peaks = []
            for c in range(columns // 128):
                top = jnp.max(peak[:, c * 128 : (c + 1) * 128], axis=1, keepdims=True) + 1e-06
                peaks.append(jnp.broadcast_to(top, (step, 128)))
            peak = jnp.concatenate(peaks, axis=1)
            scale_ref[0, blocks] = peak
            code = state * (1.0 / peak)[:, None, :]
            code_ref[0, span, :] = code.reshape(step * 16, columns).astype(bf16)
        return carry

    lax.fori_loop(0, rows // (step * 16), body, 0)


def adam(parts, weight, first, first_scale, second, second_scale, outs, chunk, width, total_tokens):
    rows = weight.shape[1]
    tile = min(512, rows)
    n = len(parts)
    big = pl.BlockSpec((1, tile, width), lambda k, r: (k, r, chunk))
    scale = pl.BlockSpec((1, tile // 16, width), lambda k, r: (k, r, chunk))
    specs = [pl.BlockSpec((tile, t.shape[1]), lambda k, r: (r, 0)) for t, _, _ in parts]
    for _, g, at in parts:
        specs.append(pl.BlockSpec((1, g.shape[1], width), lambda k, r, at=at: (k, 0, at)))
    specs += [big, big, scale, big, scale]
    operands = [t for t, _, _ in parts] + [g for _, g, _ in parts] + [weight, first, first_scale, second, second_scale]
    aliases = {}
    if outs is not None:
        aliases = {len(operands) + i: i for i in range(5)}
        specs += [pl.BlockSpec(memory_space=pl.ANY)] * 5
        operands += list(outs)
    elements = 2 * rows * width
    return pl.pallas_call(
        functools.partial(adam_kernel, n, total_tokens),
        grid=(2, rows // tile),
        in_specs=specs,
        out_specs=[big, big, scale, big, scale],
        out_shape=[
            jax.ShapeDtypeStruct(weight.shape, bf16),
            jax.ShapeDtypeStruct(weight.shape, bf16),
            jax.ShapeDtypeStruct(first_scale.shape, f32),
            jax.ShapeDtypeStruct(weight.shape, bf16),
            jax.ShapeDtypeStruct(first_scale.shape, f32),
        ],
        input_output_aliases=aliases,
        scratch_shapes=[pltpu.VMEM((tile, width), f32)],
        compiler_params=pltpu.CompilerParams(vmem_limit_bytes=32 << 20),
        cost_estimate=pl.CostEstimate(
            flops=2 * elements * sum(t.shape[1] for t, _, _ in parts) + 40 * elements,
            bytes_accessed=12 * elements,
            transcendentals=2 * elements,
        ),
        name="weight_step",
    )(*operands)


def shards(tokens, cotangent, gate_up, down_weight, first_code, first_scale, second_code, second_scale):
    groups = lax.axis_size("dp")
    bits = groups.bit_length() - 1
    chips = lax.axis_size("tensor") // 2
    me = lax.axis_index("dp")
    own, depth = tokens.shape
    rows, units = gate_up.shape[1:]
    width = 256 if units % 256 == 0 else 128
    chunks = units // width
    total_tokens = own * groups * lax.axis_size("tensor")
    orders = [list(range(bits)), list(reversed(range(bits)))]

    blocks = tokens.reshape(own, groups, rows)
    slots = []
    for s in range(groups):
        block = lax.dynamic_index_in_dim(blocks, me ^ s, 1, keepdims=False)
        slots.append(swap(block, s) if s else block)
    block = jnp.stack(slots)
    token_blocks = []
    grad_blocks = []
    cot = cotangent
    for k in range(chips):
        if k:
            block = ring(block)
        token_blocks.append(jnp.concatenate([block, pair(block)], axis=1))
    for k in range(chips):
        if k:
            cot = ring(cot)
        grad_blocks.append(jnp.concatenate([cot, pair(cot)], axis=0))

    every = tuple(range(chips))
    lead = max(1, (chunks * 4) // 7)
    plan = [((0,), 0, lead)]
    for c in range(lead):
        plan.append((every[1:], c, c + 1))
    for c in range(lead, chunks):
        plan.append((every, c, c + 1))

    cache = {}

    def rows_of(ks):
        if ks not in cache:
            t = jnp.concatenate([token_blocks[k] for k in ks], axis=1)
            c = jnp.concatenate([grad_blocks[k] for k in ks], axis=0)
            flat = t.reshape(-1, rows)
            cache[ks] = (t, c, flat.T)
        return cache[ks]

    expand = lambda scale: jnp.repeat(scale, 128, axis=2)
    first_wide = expand(first_scale)
    second_wide = expand(second_scale)

    def forward(ks, c0, c1):
        t, c, _ = rows_of(ks)
        n = t.shape[1]
        lo, hi = c0 * width, c1 * width
        pre = []
        for k in range(2):
            w = gate_up[k, :, lo:hi]
            dot = lambda pick: jnp.dot(
                jnp.concatenate([t[s] for s in pick], axis=0), w, preferred_element_type=f32
            ).reshape(len(pick), n, hi - lo)
            held = {}
            active = list(range(groups))
            got = {s: [] for s in active}
            for b in orders[k]:
                mask = 1 << b
                send = [s for s in active if s & mask]
                active = [s for s in active if not s & mask]
                out = dot(send)
                for at, s in enumerate(send):
                    for extra in got[s]:
                        out = out.at[at].add(extra.astype(f32)) if len(send) > 1 else out + extra.astype(f32)[None]
                back = swap(out.astype(bf16), mask)
                for at, s in enumerate(send):
                    got[s ^ mask].append(back[at])
            value = dot([0])[0]
            for extra in got[0]:
                value = value + extra.astype(f32)
            pre.append(value)
        gate, upper = pre
        hidden = lax.dot_general(
            c, down_weight[lo:hi], (((1,), (1,)), ((), ())), preferred_element_type=f32
        )
        sigma = jax.nn.sigmoid(gate)
        grads = (
            (hidden * upper * sigma * (1.0 + gate * (1.0 - sigma))).astype(bf16),
            (hidden * gate * sigma).astype(bf16),
        )
        full = []
        for k in range(2):
            held = {0: grads[k]}
            for b in reversed(orders[k]):
                mask = 1 << b
                keys = sorted(held)
                back = swap(jnp.stack([held[s] for s in keys]), mask)
                for at, s in enumerate(keys):
                    held[s ^ mask] = back[at]
            full.append(jnp.concatenate([held[s] for s in range(groups)], axis=0))
        return jnp.stack(full)

    results = [(ks, c0, c1, forward(ks, c0, c1)) for ks, c0, c1 in plan]

    sums = {}
    for ks, c0, c1, g in results:
        term = jnp.einsum(
            "ktf,kdf->td", g, gate_up[:, :, c0 * width : c1 * width], preferred_element_type=f32
        )
        sums[ks] = term if ks not in sums else sums[ks] + term
    partial = [None] * chips
    for ks, value in sums.items():
        value = value.reshape(groups, len(ks), 2, own, rows)
        for at, k in enumerate(ks):
            part = value[:, at]
            partial[k] = part if partial[k] is None else partial[k] + part
    moving = None
    for k in every[1:] + (0,):
        mine = partial[k][:, 0] + pair(partial[k][:, 1].astype(bf16)).astype(f32)
        if moving is not None:
            mine = mine + ring(moving).astype(f32)
        moving = mine.astype(bf16)
    final = [moving[0]] + [swap(moving[s], s) for s in range(1, groups)]
    final = jnp.stack(final)
    final = jnp.stack([lax.dynamic_index_in_dim(final, me ^ a, 0, keepdims=False) for a in range(groups)], axis=1)
    input_grad = final.reshape(own, depth)

    outs = None
    for chunk in range(chunks):
        parts = []
        for ks, c0, c1, g in results:
            if c0 <= chunk < c1:
                parts.append((rows_of(ks)[2], g, chunk - c0))
        outs = adam(
            parts, gate_up, first_code, first_wide, second_code, second_wide, outs, chunk, width, total_tokens
        )
    updated, code_one, scale_one, code_two, scale_two = outs
    return (input_grad, updated, code_one, scale_one[:, :, ::128], code_two, scale_two[:, :, ::128])


def solution(mesh):
    placed = (
        P(("dp", "tensor"), None),
        P(("dp", "tensor"), None),
        P(None, "dp", "tensor"),
        P("tensor", None),
        P(None, "dp", "tensor"),
        P(None, "dp", "tensor"),
        P(None, "dp", "tensor"),
        P(None, "dp", "tensor"),
    )
    return jax.shard_map(
        shards,
        mesh=mesh,
        in_specs=placed,
        out_specs=(
            P(("dp", "tensor"), None),
            P(None, "dp", "tensor"),
            P(None, "dp", "tensor"),
            P(None, "dp", "tensor"),
            P(None, "dp", "tensor"),
            P(None, "dp", "tensor"),
        ),
        check_vma=False,
    )
```

time: 789 us -> 341 us (0.43)
  waiting for transfers between devices: 324 us -> 54.5 us
  local copies, waits for them, and re-layouts: 278 us -> 47 us
  starting transfers between devices: 3.89 us -> 88.6 us
  other arithmetic: 91.8 us -> 11 us
  Pallas kernels: 0 us -> 57.5 us
  between operations: 14.3 us -> 2.72 us
  matrix products: 63.7 us -> 74 us
    all_gather x4 -> x0, waiting for transfers between devices: 311 us -> none  [the longest x1 264 us: shards(): weights = lax.all_gather(gate_up, 'dp', axis=1, tiled=True)]
    ppermute x0 -> x91, starting transfers between devices: none -> 88.6 us  [the longest x70 75.8 us: swap(): lax.ppermute(value, 'dp', [(p, p ^ mask) for p in range(lax.axis_size('dp...]
    mul x6 -> x0, local copies, waits for them, and re-layouts: 76.4 us -> none  [dequantize(): return (blocks * scale[:, :, None, :, None]).reshape(shape)]
    div x6 -> x0, local copies, waits for them, and re-layouts: 76.1 us -> none  [requantize(): blocks / peak[:, :, None, :, None]]
    abs x4 -> x0, local copies, waits for them, and re-layouts: 62.4 us -> none  [requantize(): peak = jnp.max(jnp.abs(blocks), axis=(2, 4)) + 1e-06]
    pallas_call x0 -> x7, Pallas kernels: none -> 57.5 us  [adam(): pl.pallas_call(functools.partial(adam_kernel, n, total_tokens), grid=(2,...]
    ppermute x0 -> x91, waiting for transfers between devices: none -> 54.5 us  [the longest x70 36.1 us: swap(): lax.ppermute(value, 'dp', [(p, p ^ mask) for p in range(lax.axis_size('dp...]
    abs x1 -> x0, other arithmetic: 45.5 us -> none  [requantize(): peak = jnp.max(jnp.abs(blocks), axis=(2, 4)) + 1e-06]
  transfers between devices with their start and end apart: 6 -> 91, of which waited for: 4 -> 23; matrix products, arithmetic and copies ran while one was open for 54% -> 34% of each run, Pallas kernels for 0% -> 17%
where the time goes in v1:
time: 341 us; the launch traced here: 335 us
  starting transfers between devices  88.6 us (26%)
  matrix products  74 us (22%)
  Pallas kernels  57.5 us (17%)
  waiting for transfers between devices  54.5 us (16%)
  local copies, waits for them, and re-layouts  47 us (14%)
  other arithmetic  11 us (3%)
    ppermute x70, starting transfers between devices, swap(): lax.ppermute(value, 'dp', [(p, p ^ mask) for p in range(lax.axis_size('dp...  75.8 us
    pallas_call x7, Pallas kernels, adam(): pl.pallas_call(functools.partial(adam_kernel, n, total_tokens), grid=(2,...  57.5 us
    dot_general x48, matrix products, forward(): jnp.dot(jnp.concatenate([t[s] for s in pick], axis=0), w, preferred_eleme...  47.1 us
    ppermute x70, waiting for transfers between devices, swap(): lax.ppermute(value, 'dp', [(p, p ^ mask) for p in range(lax.axis_size('dp...  36.1 us
    unnamed x125, local copies, waits for them, and re-layouts  20 us
    ppermute x9, waiting for transfers between devices, ring(): lax.ppermute(value, 'tensor', [(p, (p + 2) % size) for p in range(size)])  17.3 us
    dot_general x8, matrix products, forward(): lax.dot_general(c, down_weight[lo:hi], (((1,), (1,)), ((), ())), preferre...  16.6 us
    ppermute x9, starting transfers between devices, ring(): lax.ppermute(value, 'tensor', [(p, (p + 2) % size) for p in range(size)])  11.1 us
  transfers between devices with their start and end apart: 91, of which 23 were waited for; matrix products, arithmetic and copies ran while one was open for 34% of the time, Pallas kernels for 17%

profile of v1, /device:TPU:0, one launch (start us, length us, event | category | flops | bytes accessed | tf_op | source)
XLA Modules:
  0.0 335.4 jit_solution(10914354515079991468)
XLA Ops:
  1.2 2.6 collective-permute-start.13
  5.6 1.6 collective-permute-start.1
  7.1 1.6 collective-permute-start.2
  14.8 1.6 collective-permute-start.19
  16.4 1.6 collective-permute-start.15
  19.0 1.8 constant_dynamic-update-slice_fusion.21
  20.9 2.9 fusion.36
  23.8 2.8 fusion.39
  27.2 1.5 collective-permute-start.5
  28.7 2.1 copy.115
  31.8 1.7 constant_dynamic-update-slice_fusion.27
  33.5 1.6 collective-permute-start.17
  35.1 1.9 constant_dynamic-update-slice_fusion.20
  37.0 1.8 constant_dynamic-update-slice_fusion.19
  39.0 2.2 fusion.137
  41.8 2.1 fusion.134
  43.9 1.5 collective-permute-start.6
  45.3 1.7 collective-permute-start.23
  48.7 6.1 %multiply_convert_fusion.3 = (bf16[64,1024]{1,0:T(8,128)(2,1)S(1)}, f32[64,1024]{1,0:T(8,128)S(1)}) fusion(f32[64,1024]{1,0:T(8,128)S(1)} %fusion.57, bf16[1792,4096]{1,0:T(8,128)(2,1)} %param.11, bf16[32,4096]{1,0:T(8,128)(2,1)S(1)} %copy-done.33, bf16[32,4096]{1,0:T(8,128)(2,1)S(1)} %copy-done.30), kind=kOutput, calls=%fused_computation.355 | convolution fusion | flops 538312704 | bytes 9568256 | tf_op jit(solution)/shard_map/dot_general | solution.py:193
  55.5 1.4 fusion.119
  56.9 1.6 collective-permute-start.9
  62.6 1.5 collective-permute-start.10
  81.6 2.4 fusion.2
  90.1 2.8 copy.116
  92.9 4.1 %copy.119 = bf16[1024,1024]{0,1:T(8,128)(2,1)} copy(bf16[1024,1024]{1,0:T(8,128)(2,1)} %bitcast.746) | data formatting | bytes 4194304 | tf_op jit(solution)/shard_map/reshape | solution.py:156
  97.0 1.5 collective-permute-start.60
  98.5 1.4 fusion.153
  101.0 1.4 fusion.151
  103.6 1.4 fusion.149
  106.0 1.4 fusion.147
  108.7 1.4 fusion.152
  112.5 1.5 collective-permute-start.27
  115.3 1.5 collective-permute-start.43
  117.1 2.9 collective-permute-done.33
  121.0 1.7 collective-permute-done.41
  125.5 1.9 collective-permute-done.35
  127.4 1.4 collective-permute-start.75
  129.2 3.9 %collective-permute-done.43 = bf16[2,256,256]{2,1,0:T(8,128)(2,1)S(1)} collective-permute-done((bf16[2,256,256]{2,1,0:T(8,128)(2,1)S(1)}, bf16[2,256,256]{2,1,0:T(8,128)(2,1)S(1)}, u32[]{:S(2)}, u32[]{:S(2)}) %collective-permute-start.43) | collective-permute-done | bytes 262176 | tf_op jit(solution)/shard_map/ppermute | solution.py:18
  134.5 3.2 collective-permute-done.77
  139.1 2.6 multiply_convert_fusion.4
  143.7 2.4 multiply_convert_fusion.5
  148.3 2.4 multiply_convert_fusion.6
  150.8 1.7 collective-permute-done.53
  165.1 2.9 collective-permute-done.44
  169.8 3.1 collective-permute-done.36
  183.9 1.5 collective-permute-start.54
  186.1 3.3 collective-permute-done.54
  197.4 3.6 %collective-permute-done.29 = bf16[1,256,256]{2,1,0:T(8,128)(2,1)S(1)} collective-permute-done((bf16[1,256,256]{2,1,0:T(8,128)(2,1)S(1)}, bf16[1,256,256]{2,1,0:T(8,128)(2,1)S(1)}, u32[]{:S(2)}, u32[]{:S(2)}) %collective-permute-start.29) | collective-permute-done | bytes 131104 | tf_op jit(solution)/shard_map/ppermute | solution.py:18
  208.0 1.8 collective-permute-done.73
  227.9 8.2 %weight_step.7 = (bf16[2,1024,1792]{2,1,0:T(8,128)(2,1)}, bf16[2,1024,1792]{2,1,0:T(8,128)(2,1)}, f32[2,64,1792]{2,1,0:T(8,128)S(1)}, bf16[2,1024,1792]{2,1,0:T(8,128)(2,1)}, f32[2,64,1792]{2,1,0:T(8,128)S(1)}) custom-call(bf16[1024,256]{1,0:T(8,128)(2,1)S(1)} %bitcast.740, bf16[1024,768]{1,0:T(8,128)(2,1)S(1)} %bitcast.733, ...), custom_call_target="tpu_custom_call" | custom-call | flops 1094713344 | bytes 6291456 | tf_op jit(solution)/shard_map/weight_step/pallas_call | solution.py:88
  236.1 8.2 %weight_step.8 = (bf16[2,1024,1792]{2,1,0:T(8,128)(2,1)}, bf16[2,1024,1792]{2,1,0:T(8,128)(2,1)}, f32[2,64,1792]{2,1,0:T(8,128)S(1)}, bf16[2,1024,1792]{2,1,0:T(8,128)(2,1)}, f32[2,64,1792]{2,1,0:T(8,128)S(1)}) custom-call(bf16[1024,256]{1,0:T(8,128)(2,1)S(1)} %bitcast.741, ...), custom_call_target="tpu_custom_call", output_to_operand_aliasing={{0}: (9, {}), {1}: (10, {}), {2}: (11, {}), {3}: (12, {}), ... | custom-call | flops 1094713344 | bytes 6291456 | tf_op jit(solution)/shard_map/weight_step/pallas_call | solution.py:88
  244.3 8.2 %weight_step.9 = (bf16[2,1024,1792]{2,1,0:T(8,128)(2,1)}, bf16[2,1024,1792]{2,1,0:T(8,128)(2,1)}, f32[2,64,1792]{2,1,0:T(8,128)S(1)}, bf16[2,1024,1792]{2,1,0:T(8,128)(2,1)}, f32[2,64,1792]{2,1,0:T(8,128)S(1)}) custom-call(bf16[1024,256]{1,0:T(8,128)(2,1)S(1)} %bitcast.742, ...), custom_call_target="tpu_custom_call", output_to_operand_aliasing={{0}: (9, {}), {1}: (10, {}), {2}: (11, {}), {3}: (12, {}), ... | custom-call | flops 1094713344 | bytes 6291456 | tf_op jit(solution)/shard_map/weight_step/pallas_call | solution.py:88
  252.6 8.4 %weight_step.10 = (bf16[2,1024,1792]{2,1,0:T(8,128)(2,1)}, bf16[2,1024,1792]{2,1,0:T(8,128)(2,1)}, f32[2,64,1792]{2,1,0:T(8,128)S(1)}, bf16[2,1024,1792]{2,1,0:T(8,128)(2,1)}, f32[2,64,1792]{2,1,0:T(8,128)S(1)}) custom-call(bf16[1024,256]{1,0:T(8,128)(2,1)S(1)} %bitcast.743, ...), custom_call_target="tpu_custom_call", output_to_operand_aliasing={{0}: (9, {}), {1}: (10, {}), {2}: (11, {}), {3}: (12, {}), ... | custom-call | flops 1094713344 | bytes 6291456 | tf_op jit(solution)/shard_map/weight_step/pallas_call | solution.py:88
  271.6 3.1 fusion.273
  274.8 1.9 fusion.154
  279.2 1.6 collective-permute-start.85
  281.2 8.2 %collective-permute-done.85 = bf16[4,32,1024]{2,1,0:T(8,128)(2,1)S(1)} collective-permute-done((bf16[4,32,1024]{2,1,0:T(8,128)(2,1)S(1)}, bf16[4,32,1024]{2,1,0:T(8,128)(2,1)S(1)}, u32[]{:S(2)}, u32[]{:S(2)}) %collective-permute-start.85) | collective-permute-done | bytes 262176 | tf_op jit(solution)/shard_map/ppermute | solution.py:27
  289.8 9.0 %collective-permute-done.86 = bf16[4,32,1024]{2,1,0:T(8,128)(2,1)S(1)} collective-permute-done((bf16[4,32,1024]{2,1,0:T(8,128)(2,1)S(1)}, bf16[4,32,1024]{2,1,0:T(8,128)(2,1)S(1)}, u32[]{:S(2)}, u32[]{:S(2)}) %collective-permute-start.86) | collective-permute-done | bytes 262176 | tf_op jit(solution)/shard_map/ppermute | solution.py:27
  299.0 8.2 %weight_step.11 = (bf16[2,1024,1792]{2,1,0:T(8,128)(2,1)}, bf16[2,1024,1792]{2,1,0:T(8,128)(2,1)}, f32[2,64,1792]{2,1,0:T(8,128)S(1)}, bf16[2,1024,1792]{2,1,0:T(8,128)(2,1)}, f32[2,64,1792]{2,1,0:T(8,128)S(1)}) custom-call(bf16[1024,1024]{1,0:T(8,128)(2,1)S(1)} %bitcast.737, ...), custom_call_target="tpu_custom_call", output_to_operand_aliasing={{0}: (7, {}), {1}: (8, {}), {2}: (9, {}), {3}: (10, {}), {4... | custom-call | flops 1094713344 | bytes 6291456 | tf_op jit(solution)/shard_map/weight_step/pallas_call | solution.py:88
  307.2 8.2 %weight_step.12 = (bf16[2,1024,1792]{2,1,0:T(8,128)(2,1)}, bf16[2,1024,1792]{2,1,0:T(8,128)(2,1)}, f32[2,64,1792]{2,1,0:T(8,128)S(1)}, bf16[2,1024,1792]{2,1,0:T(8,128)(2,1)}, f32[2,64,1792]{2,1,0:T(8,128)S(1)}) custom-call(bf16[1024,1024]{1,0:T(8,128)(2,1)S(1)} %bitcast.738, ...), custom_call_target="tpu_custom_call", output_to_operand_aliasing={{0}: (7, {}), {1}: (8, {}), {2}: (9, {}), {3}: (10, {}), {4... | custom-call | flops 1094713344 | bytes 6291456 | tf_op jit(solution)/shard_map/weight_step/pallas_call | solution.py:88
  315.6 1.5 collective-permute-start.90
  319.2 8.2 %weight_step.13 = (bf16[2,1024,1792]{2,1,0:T(8,128)(2,1)}, bf16[2,1024,1792]{2,1,0:T(8,128)(2,1)}, f32[2,64,1792]{2,1,0:T(8,128)S(1)}, bf16[2,1024,1792]{2,1,0:T(8,128)(2,1)}, f32[2,64,1792]{2,1,0:T(8,128)S(1)}) custom-call(bf16[1024,1024]{1,0:T(8,128)(2,1)S(1)} %bitcast.739, ...), custom_call_target="tpu_custom_call", output_to_operand_aliasing={{0}: (7, {}), {1}: (8, {}), {2}: (9, {}), {3}: (10, {}), {4... | custom-call | flops 1094713344 | bytes 6291456 | tf_op jit(solution)/shard_map/weight_step/pallas_call | solution.py:88
  329.2 1.5 slice.570
  331.4 1.5 slice.571
  (413 shorter events, 140.7 us)
Async XLA Ops:
  0.7 17.6 %collective-permute-start = (bf16[32,4096]{1,0:T(8,128)(2,1)}, bf16[32,4096]{1,0:T(8,128)(2,1)S(1)}, u32[]{:S(2)}, u32[]{:S(2)}) collective-permute-start(bf16[32,4096]{1,0:T(8,128)(2,1)} %param.9), channel_id=1, source_target_pairs={{0,1},{1,0},{2,3},{3,2},{4,5},{5,4},{6,7},{7,6},{8,9},{9,8},{10,11... | collective-permute-start | bytes 786440 | tf_op jit(solution)/shard_map/ppermute | solution.py:22
  1.2 15.2 %collective-permute-start.13 = (bf16[32,4096]{1,0:T(8,128)(2,1)}, bf16[32,4096]{1,0:T(8,128)(2,1)}, u32[]{:S(2)}, u32[]{:S(2)}) collective-permute-start(bf16[32,4096]{1,0:T(8,128)(2,1)} %param.9), channel_id=1, source_target_pairs={{0,2},{1,3},{2,4},{3,5},{4,6},{5,7},{6,0},{7,1},{8,10},{9,11},{10,... | collective-permute-start | bytes 786440 | tf_op jit(solution)/shard_map/ppermute | solution.py:27
  5.6 7.5 %collective-permute-start.1 = (bf16[32,1024]{1,0:T(8,128)(2,1)S(1)}, bf16[32,1024]{1,0:T(8,128)(2,1)S(1)}, u32[]{:S(2)}, u32[]{:S(2)}) collective-permute-start(bf16[32,1024]{1,0:T(8,128)(2,1)S(1)} %bitcast.823), channel_id=1, source_target_pairs={{0,8},{8,0},{16,24},{24,16},{1,9},{9,1},{17,25},{25,17},{2,10},{10... | collective-permute-start | bytes 196616 | tf_op jit(solution)/shard_map/ppermute | solution.py:18
  14.8 16.0 %collective-permute-start.19 = (bf16[4,32,1024]{2,1,0:T(8,128)(2,1)}, bf16[4,32,1024]{2,1,0:T(8,128)(2,1)}, u32[]{:S(2)}, u32[]{:S(2)}) collective-permute-start(bf16[4,32,1024]{2,1,0:T(8,128)(2,1)} %get-tuple-element.168), channel_id=1, source_target_pairs={{0,2},{1,3},{2,4},{3,5},{4,6},{5,7},{6,0},{7,1},{8,10},{9,11},{10,... | collective-permute-start | bytes 786440 | tf_op jit(solution)/shard_map/ppermute | solution.py:27
  16.4 17.1 %collective-permute-start.15 = (bf16[32,4096]{1,0:T(8,128)(2,1)}, bf16[32,4096]{1,0:T(8,128)(2,1)}, u32[]{:S(2)}, u32[]{:S(2)}) collective-permute-start(bf16[32,4096]{1,0:T(8,128)(2,1)} %collective-permute-done.13), channel_id=1, source_target_pairs={{0,2},{1,3},{2,4},{3,5},{4,6},{5,7},{6,0},{7,1},{8,10},{9,11},{10,... | collective-permute-start | bytes 786440 | tf_op jit(solution)/shard_map/ppermute | solution.py:27
  18.0 15.5 %collective-permute-start.14 = (bf16[32,4096]{1,0:T(8,128)(2,1)}, bf16[32,4096]{1,0:T(8,128)(2,1)}, u32[]{:S(2)}, u32[]{:S(2)}) collective-permute-start(bf16[32,4096]{1,0:T(8,128)(2,1)} %collective-permute-done.13), channel_id=1, source_target_pairs={{0,1},{1,0},{2,3},{3,2},{4,5},{5,4},{6,7},{7,6},{8,9},{9,8},{10,11... | collective-permute-start | bytes 786440 | tf_op jit(solution)/shard_map/ppermute | solution.py:22
  26.6 12.2 %collective-permute-start.7 = (bf16[2,64,1024]{2,1,0:T(8,128)(2,1)}, bf16[2,64,1024]{2,1,0:T(8,128)(2,1)}, u32[]{:S(2)}, u32[]{:S(2)}) collective-permute-start(bf16[2,64,1024]{2,1,0:T(8,128)(2,1)} %fusion.39), channel_id=1, source_target_pairs={{0,8},{8,0},{16,24},{24,16},{1,9},{9,1},{17,25},{25,17},{2,10},{10... | collective-permute-start | bytes 786440 | tf_op jit(solution)/shard_map/ppermute | solution.py:18
  27.2 14.0 %collective-permute-start.5 = (bf16[2,64,1024]{2,1,0:T(8,128)(2,1)}, bf16[2,64,1024]{2,1,0:T(8,128)(2,1)}, u32[]{:S(2)}, u32[]{:S(2)}) collective-permute-start(bf16[2,64,1024]{2,1,0:T(8,128)(2,1)} %fusion.36), channel_id=1, source_target_pairs={{0,16},{8,24},{16,0},{24,8},{1,17},{9,25},{17,1},{25,9},{2,18},{10... | collective-permute-start | bytes 786440 | tf_op jit(solution)/shard_map/ppermute | solution.py:18
  30.8 13.0 %collective-permute-start.21 = (bf16[4,32,1024]{2,1,0:T(8,128)(2,1)}, bf16[4,32,1024]{2,1,0:T(8,128)(2,1)S(1)}, u32[]{:S(2)}, u32[]{:S(2)}) collective-permute-start(bf16[4,32,1024]{2,1,0:T(8,128)(2,1)} %collective-permute-done.19), channel_id=1, source_target_pairs={{0,2},{1,3},{2,4},{3,5},{4,6},{5,7},{6,0},{7,1},{8,10},{9,11},{10,... | collective-permute-start | bytes 786440 | tf_op jit(solution)/shard_map/ppermute | solution.py:27
  33.5 11.8 %collective-permute-start.20 = (bf16[4,32,1024]{2,1,0:T(8,128)(2,1)}, bf16[4,32,1024]{2,1,0:T(8,128)(2,1)S(1)}, u32[]{:S(2)}, u32[]{:S(2)}) collective-permute-start(bf16[4,32,1024]{2,1,0:T(8,128)(2,1)} %collective-permute-done.19), channel_id=1, source_target_pairs={{0,1},{1,0},{2,3},{3,2},{4,5},{5,4},{6,7},{7,6},{8,9},{9,8},{10,11... | collective-permute-start | bytes 786440 | tf_op jit(solution)/shard_map/ppermute | solution.py:22
  33.5 23.4 %collective-permute-start.17 = (bf16[32,4096]{1,0:T(8,128)(2,1)}, bf16[32,4096]{1,0:T(8,128)(2,1)S(1)}, u32[]{:S(2)}, u32[]{:S(2)}) collective-permute-start(bf16[32,4096]{1,0:T(8,128)(2,1)} %collective-permute-done.15), channel_id=1, source_target_pairs={{0,2},{1,3},{2,4},{3,5},{4,6},{5,7},{6,0},{7,1},{8,10},{9,11},{10,... | collective-permute-start | bytes 786440 | tf_op jit(solution)/shard_map/ppermute | solution.py:27
  38.8 19.7 %collective-permute-start.16 = (bf16[32,4096]{1,0:T(8,128)(2,1)}, bf16[32,4096]{1,0:T(8,128)(2,1)S(1)}, u32[]{:S(2)}, u32[]{:S(2)}) collective-permute-start(bf16[32,4096]{1,0:T(8,128)(2,1)} %collective-permute-done.15), channel_id=1, source_target_pairs={{0,1},{1,0},{2,3},{3,2},{4,5},{5,4},{6,7},{7,6},{8,9},{9,8},{10,11... | collective-permute-start | bytes 786440 | tf_op jit(solution)/shard_map/ppermute | solution.py:22
  43.9 10.9 %collective-permute-start.6 = (bf16[1,64,1024]{2,1,0:T(8,128)(2,1)S(1)}, bf16[1,64,1024]{2,1,0:T(8,128)(2,1)S(1)}, u32[]{:S(2)}, u32[]{:S(2)}) collective-permute-start(bf16[1,64,1024]{2,1,0:T(8,128)(2,1)S(1)} %fusion.134), channel_id=1, source_target_pairs={{0,8},{8,0},{16,24},{24,16},{1,9},{9,1},{17,25},{25,17},{2,10},{10... | collective-permute-start | bytes 393224 | tf_op jit(solution)/shard_map/ppermute | solution.py:18
  45.3 18.8 %collective-permute-start.23 = (bf16[4,32,1024]{2,1,0:T(8,128)(2,1)S(1)}, bf16[4,32,1024]{2,1,0:T(8,128)(2,1)S(1)}, u32[]{:S(2)}, u32[]{:S(2)}) collective-permute-start(bf16[4,32,1024]{2,1,0:T(8,128)(2,1)S(1)} %collective-permute-done.21), channel_id=1, source_target_pairs={{0,2},{1,3},{2,4},{3,5},{4,6},{5,7},{6,0},{7,1},{8,10},{9,11},{10,... | collective-permute-start | bytes 786440 | tf_op jit(solution)/shard_map/ppermute | solution.py:27
  47.2 16.9 %collective-permute-start.22 = (bf16[4,32,1024]{2,1,0:T(8,128)(2,1)S(1)}, bf16[4,32,1024]{2,1,0:T(8,128)(2,1)S(1)}, u32[]{:S(2)}, u32[]{:S(2)}) collective-permute-start(bf16[4,32,1024]{2,1,0:T(8,128)(2,1)S(1)} %collective-permute-done.21), channel_id=1, source_target_pairs={{0,1},{1,0},{2,3},{3,2},{4,5},{5,4},{6,7},{7,6},{8,9},{9,8},{10,11... | collective-permute-start | bytes 786440 | tf_op jit(solution)/shard_map/ppermute | solution.py:22
  60.8 19.7 %collective-permute-start.12 = (bf16[2,64,1024]{2,1,0:T(8,128)(2,1)S(1)}, bf16[2,64,1024]{2,1,0:T(8,128)(2,1)S(1)}, u32[]{:S(2)}, u32[]{:S(2)}) collective-permute-start(bf16[2,64,1024]{2,1,0:T(8,128)(2,1)S(1)} %pad_maximum_fusion.17), channel_id=1, source_target_pairs={{0,16},{8,24},{16,0},{24,8},{1,17},{9,25},{17,1},{25,9},{2,18},{10... | collective-permute-start | bytes 786440 | tf_op jit(solution)/shard_map/ppermute | solution.py:18
  62.6 18.9 %collective-permute-start.10 = (bf16[2,64,1024]{2,1,0:T(8,128)(2,1)S(1)}, bf16[2,64,1024]{2,1,0:T(8,128)(2,1)S(1)}, u32[]{:S(2)}, u32[]{:S(2)}) collective-permute-start(bf16[2,64,1024]{2,1,0:T(8,128)(2,1)S(1)} %pad_maximum_fusion.16), channel_id=1, source_target_pairs={{0,8},{8,0},{16,24},{24,16},{1,9},{9,1},{17,25},{25,17},{2,10},{10... | collective-permute-start | bytes 786440 | tf_op jit(solution)/shard_map/ppermute | solution.py:18
  78.7 18.3 %collective-permute-start.50 = (bf16[2,192,256]{2,1,0:T(8,128)(2,1)}, bf16[2,192,256]{2,1,0:T(8,128)(2,1)}, u32[]{:S(2)}, u32[]{:S(2)}) collective-permute-start(bf16[2,192,256]{2,1,0:T(8,128)(2,1)} %convolution_convert_fusion.13), channel_id=1, source_target_pairs={{0,16},{8,24},{16,0},{24,8},{1,17},{9,25},{17,1},{25,9},{2,18},{10... | collective-permute-start | bytes 589832 | tf_op jit(solution)/shard_map/ppermute | solution.py:18
  85.0 14.9 %collective-permute-start.58 = (bf16[2,192,256]{2,1,0:T(8,128)(2,1)}, bf16[2,192,256]{2,1,0:T(8,128)(2,1)}, u32[]{:S(2)}, u32[]{:S(2)}) collective-permute-start(bf16[2,192,256]{2,1,0:T(8,128)(2,1)} %convolution_convert_fusion.11), channel_id=1, source_target_pairs={{0,16},{8,24},{16,0},{24,8},{1,17},{9,25},{17,1},{25,9},{2,18},{10... | collective-permute-start | bytes 589832 | tf_op jit(solution)/shard_map/ppermute | solution.py:18
  87.5 15.0 %collective-permute-start.66 = (bf16[2,192,256]{2,1,0:T(8,128)(2,1)}, bf16[2,192,256]{2,1,0:T(8,128)(2,1)}, u32[]{:S(2)}, u32[]{:S(2)}) collective-permute-start(bf16[2,192,256]{2,1,0:T(8,128)(2,1)} %convolution_convert_fusion.9), channel_id=1, source_target_pairs={{0,16},{8,24},{16,0},{24,8},{1,17},{9,25},{17,1},{25,9},{2,18},{10... | collective-permute-start | bytes 589832 | tf_op jit(solution)/shard_map/ppermute | solution.py:18
  88.1 17.0 %collective-permute-start.74 = (bf16[2,192,256]{2,1,0:T(8,128)(2,1)}, bf16[2,192,256]{2,1,0:T(8,128)(2,1)}, u32[]{:S(2)}, u32[]{:S(2)}) collective-permute-start(bf16[2,192,256]{2,1,0:T(8,128)(2,1)} %convolution_convert_fusion.7), channel_id=1, source_target_pairs={{0,16},{8,24},{16,0},{24,8},{1,17},{9,25},{17,1},{25,9},{2,18},{10... | collective-permute-start | bytes 589832 | tf_op jit(solution)/shard_map/ppermute | solution.py:18
  89.5 18.0 %collective-permute-start.52 = (bf16[2,192,256]{2,1,0:T(8,128)(2,1)}, bf16[2,192,256]{2,1,0:T(8,128)(2,1)}, u32[]{:S(2)}, u32[]{:S(2)}) collective-permute-start(bf16[2,192,256]{2,1,0:T(8,128)(2,1)} %convolution_convert_fusion.12), channel_id=1, source_target_pairs={{0,8},{8,0},{16,24},{24,16},{1,9},{9,1},{17,25},{25,17},{2,10},{10... | collective-permute-start | bytes 589832 | tf_op jit(solution)/shard_map/ppermute | solution.py:18
  97.0 13.2 %collective-permute-start.60 = (bf16[2,192,256]{2,1,0:T(8,128)(2,1)}, bf16[2,192,256]{2,1,0:T(8,128)(2,1)S(1)}, u32[]{:S(2)}, u32[]{:S(2)}) collective-permute-start(bf16[2,192,256]{2,1,0:T(8,128)(2,1)} %convolution_convert_fusion.10), channel_id=1, source_target_pairs={{0,8},{8,0},{16,24},{24,16},{1,9},{9,1},{17,25},{25,17},{2,10},{10... | collective-permute-start | bytes 589832 | tf_op jit(solution)/shard_map/ppermute | solution.py:18
  100.0 12.5 %collective-permute-start.68 = (bf16[2,192,256]{2,1,0:T(8,128)(2,1)}, bf16[2,192,256]{2,1,0:T(8,128)(2,1)S(1)}, u32[]{:S(2)}, u32[]{:S(2)}) collective-permute-start(bf16[2,192,256]{2,1,0:T(8,128)(2,1)} %convolution_convert_fusion.8), channel_id=1, source_target_pairs={{0,8},{8,0},{16,24},{24,16},{1,9},{9,1},{17,25},{25,17},{2,10},{10... | collective-permute-start | bytes 589832 | tf_op jit(solution)/shard_map/ppermute | solution.py:18
  102.5 11.8 %collective-permute-start.76 = (bf16[2,192,256]{2,1,0:T(8,128)(2,1)}, bf16[2,192,256]{2,1,0:T(8,128)(2,1)S(1)}, u32[]{:S(2)}, u32[]{:S(2)}) collective-permute-start(bf16[2,192,256]{2,1,0:T(8,128)(2,1)} %convolution_convert_fusion.6), channel_id=1, source_target_pairs={{0,8},{8,0},{16,24},{24,16},{1,9},{9,1},{17,25},{25,17},{2,10},{10... | collective-permute-start | bytes 589832 | tf_op jit(solution)/shard_map/ppermute | solution.py:18
  105.1 10.2 %collective-permute-start.25 = (bf16[2,256,256]{2,1,0:T(8,128)(2,1)}, bf16[2,256,256]{2,1,0:T(8,128)(2,1)S(1)}, u32[]{:S(2)}, u32[]{:S(2)}) collective-permute-start(bf16[2,256,256]{2,1,0:T(8,128)(2,1)} %convolution_convert_fusion.5), channel_id=1, source_target_pairs={{0,16},{8,24},{16,0},{24,8},{1,17},{9,25},{17,1},{25,9},{2,18},{10... | collective-permute-start | bytes 786440 | tf_op jit(solution)/shard_map/ppermute | solution.py:18
  107.5 12.4 %collective-permute-start.33 = (bf16[2,256,256]{2,1,0:T(8,128)(2,1)S(1)}, bf16[2,256,256]{2,1,0:T(8,128)(2,1)S(1)}, u32[]{:S(2)}, u32[]{:S(2)}) collective-permute-start(bf16[2,256,256]{2,1,0:T(8,128)(2,1)S(1)} %copy-done.41), channel_id=1, source_target_pairs={{0,16},{8,24},{16,0},{24,8},{1,17},{9,25},{17,1},{25,9},{2,18},{10... | collective-permute-start | bytes 786440 | tf_op jit(solution)/shard_map/ppermute | solution.py:18
  110.2 12.5 %collective-permute-start.41 = (bf16[2,256,256]{2,1,0:T(8,128)(2,1)S(1)}, bf16[2,256,256]{2,1,0:T(8,128)(2,1)S(1)}, u32[]{:S(2)}, u32[]{:S(2)}) collective-permute-start(bf16[2,256,256]{2,1,0:T(8,128)(2,1)S(1)} %copy-done.40), channel_id=1, source_target_pairs={{0,16},{8,24},{16,0},{24,8},{1,17},{9,25},{17,1},{25,9},{2,18},{10... | collective-permute-start | bytes 786440 | tf_op jit(solution)/shard_map/ppermute | solution.py:18
  112.5 11.3 %collective-permute-start.27 = (bf16[2,256,256]{2,1,0:T(8,128)(2,1)S(1)}, bf16[2,256,256]{2,1,0:T(8,128)(2,1)S(1)}, u32[]{:S(2)}, u32[]{:S(2)}) collective-permute-start(bf16[2,256,256]{2,1,0:T(8,128)(2,1)S(1)} %copy-done.39), channel_id=1, source_target_pairs={{0,8},{8,0},{16,24},{24,16},{1,9},{9,1},{17,25},{25,17},{2,10},{10... | collective-permute-start | bytes 786440 | tf_op jit(solution)/shard_map/ppermute | solution.py:18
  114.3 13.1 %collective-permute-start.35 = (bf16[2,256,256]{2,1,0:T(8,128)(2,1)S(1)}, bf16[2,256,256]{2,1,0:T(8,128)(2,1)S(1)}, u32[]{:S(2)}, u32[]{:S(2)}) collective-permute-start(bf16[2,256,256]{2,1,0:T(8,128)(2,1)S(1)} %copy-done.38), channel_id=1, source_target_pairs={{0,8},{8,0},{16,24},{24,16},{1,9},{9,1},{17,25},{25,17},{2,10},{10... | collective-permute-start | bytes 786440 | tf_op jit(solution)/shard_map/ppermute | solution.py:18
  115.3 17.8 %collective-permute-start.43 = (bf16[2,256,256]{2,1,0:T(8,128)(2,1)S(1)}, bf16[2,256,256]{2,1,0:T(8,128)(2,1)S(1)}, u32[]{:S(2)}, u32[]{:S(2)}) collective-permute-start(bf16[2,256,256]{2,1,0:T(8,128)(2,1)S(1)} %convolution_convert_fusion), channel_id=1, source_target_pairs={{0,8},{8,0},{16,24},{24,16},{1,9},{9,1},{17,25},{25,17},{2,10},{10... | collective-permute-start | bytes 786440 | tf_op jit(solution)/shard_map/ppermute | solution.py:18
  119.9 40.5 %collective-permute-start.51 = (bf16[1,192,256]{2,1,0:T(8,128)(2,1)S(1)}, bf16[1,192,256]{2,1,0:T(8,128)(2,1)S(1)}, u32[]{:S(2)}, u32[]{:S(2)}) collective-permute-start(bf16[1,192,256]{2,1,0:T(8,128)(2,1)S(1)} %fusion.153), channel_id=1, source_target_pairs={{0,8},{8,0},{16,24},{24,16},{1,9},{9,1},{17,25},{25,17},{2,10},{10... | collective-permute-start | bytes 294920 | tf_op jit(solution)/shard_map/ppermute | solution.py:18
  122.7 39.8 %collective-permute-start.59 = (bf16[1,192,256]{2,1,0:T(8,128)(2,1)S(1)}, bf16[1,192,256]{2,1,0:T(8,128)(2,1)S(1)}, u32[]{:S(2)}, u32[]{:S(2)}) collective-permute-start(bf16[1,192,256]{2,1,0:T(8,128)(2,1)S(1)} %fusion.151), channel_id=1, source_target_pairs={{0,8},{8,0},{16,24},{24,16},{1,9},{9,1},{17,25},{25,17},{2,10},{10... | collective-permute-start | bytes 294920 | tf_op jit(solution)/shard_map/ppermute | solution.py:18
  123.8 34.1 %collective-permute-start.67 = (bf16[1,192,256]{2,1,0:T(8,128)(2,1)S(1)}, bf16[1,192,256]{2,1,0:T(8,128)(2,1)S(1)}, u32[]{:S(2)}, u32[]{:S(2)}) collective-permute-start(bf16[1,192,256]{2,1,0:T(8,128)(2,1)S(1)} %fusion.149), channel_id=1, source_target_pairs={{0,8},{8,0},{16,24},{24,16},{1,9},{9,1},{17,25},{25,17},{2,10},{10... | collective-permute-start | bytes 294920 | tf_op jit(solution)/shard_map/ppermute | solution.py:18
  127.4 28.4 %collective-permute-start.75 = (bf16[1,192,256]{2,1,0:T(8,128)(2,1)S(1)}, bf16[1,192,256]{2,1,0:T(8,128)(2,1)S(1)}, u32[]{:S(2)}, u32[]{:S(2)}) collective-permute-start(bf16[1,192,256]{2,1,0:T(8,128)(2,1)S(1)} %fusion.147), channel_id=1, source_target_pairs={{0,8},{8,0},{16,24},{24,16},{1,9},{9,1},{17,25},{25,17},{2,10},{10... | collective-permute-start | bytes 294920 | tf_op jit(solution)/shard_map/ppermute | solution.py:18
  152.5 25.9 %collective-permute-start.26 = (bf16[1,256,256]{2,1,0:T(8,128)(2,1)S(1)}, bf16[1,256,256]{2,1,0:T(8,128)(2,1)S(1)}, u32[]{:S(2)}, u32[]{:S(2)}) collective-permute-start(bf16[1,256,256]{2,1,0:T(8,128)(2,1)S(1)} %fusion.145), channel_id=1, source_target_pairs={{0,8},{8,0},{16,24},{24,16},{1,9},{9,1},{17,25},{25,17},{2,10},{10... | collective-permute-start | bytes 393224 | tf_op jit(solution)/shard_map/ppermute | solution.py:18
  155.8 24.2 %collective-permute-start.34 = (bf16[1,256,256]{2,1,0:T(8,128)(2,1)S(1)}, bf16[1,256,256]{2,1,0:T(8,128)(2,1)S(1)}, u32[]{:S(2)}, u32[]{:S(2)}) collective-permute-start(bf16[1,256,256]{2,1,0:T(8,128)(2,1)S(1)} %fusion.143), channel_id=1, source_target_pairs={{0,8},{8,0},{16,24},{24,16},{1,9},{9,1},{17,25},{25,17},{2,10},{10... | collective-permute-start | bytes 393224 | tf_op jit(solution)/shard_map/ppermute | solution.py:18
  157.9 19.1 %collective-permute-start.42 = (bf16[1,256,256]{2,1,0:T(8,128)(2,1)S(1)}, bf16[1,256,256]{2,1,0:T(8,128)(2,1)S(1)}, u32[]{:S(2)}, u32[]{:S(2)}) collective-permute-start(bf16[1,256,256]{2,1,0:T(8,128)(2,1)S(1)} %fusion.141), channel_id=1, source_target_pairs={{0,8},{8,0},{16,24},{24,16},{1,9},{9,1},{17,25},{25,17},{2,10},{10... | collective-permute-start | bytes 393224 | tf_op jit(solution)/shard_map/ppermute | solution.py:18
  160.4 14.3 %collective-permute-start.28 = (bf16[1,256,256]{2,1,0:T(8,128)(2,1)S(1)}, bf16[1,256,256]{2,1,0:T(8,128)(2,1)S(1)}, u32[]{:S(2)}, u32[]{:S(2)}) collective-permute-start(bf16[1,256,256]{2,1,0:T(8,128)(2,1)S(1)} %fusion.144), channel_id=1, source_target_pairs={{0,16},{8,24},{16,0},{24,8},{1,17},{9,25},{17,1},{25,9},{2,18},{10... | collective-permute-start | bytes 393224 | tf_op jit(solution)/shard_map/ppermute | solution.py:18
  172.9 9.9 %collective-permute-start.80 = (bf16[1,192,256]{2,1,0:T(8,128)(2,1)S(1)}, bf16[1,192,256]{2,1,0:T(8,128)(2,1)S(1)}, u32[]{:S(2)}, u32[]{:S(2)}) collective-permute-start(bf16[1,192,256]{2,1,0:T(8,128)(2,1)S(1)} %bitcast.790), channel_id=1, source_target_pairs={{0,8},{8,0},{16,24},{24,16},{1,9},{9,1},{17,25},{25,17},{2,10},{10... | collective-permute-start | bytes 294920 | tf_op jit(solution)/shard_map/ppermute | solution.py:18
  177.0 8.4 %collective-permute-start.72 = (bf16[1,192,256]{2,1,0:T(8,128)(2,1)S(1)}, bf16[1,192,256]{2,1,0:T(8,128)(2,1)S(1)}, u32[]{:S(2)}, u32[]{:S(2)}) collective-permute-start(bf16[1,192,256]{2,1,0:T(8,128)(2,1)S(1)} %bitcast.802), channel_id=1, source_target_pairs={{0,8},{8,0},{16,24},{24,16},{1,9},{9,1},{17,25},{25,17},{2,10},{10... | collective-permute-start | bytes 294920 | tf_op jit(solution)/shard_map/ppermute | solution.py:18
  180.1 12.7 %collective-permute-start.64 = (bf16[1,192,256]{2,1,0:T(8,128)(2,1)S(1)}, bf16[1,192,256]{2,1,0:T(8,128)(2,1)S(1)}, u32[]{:S(2)}, u32[]{:S(2)}) collective-permute-start(bf16[1,192,256]{2,1,0:T(8,128)(2,1)S(1)} %bitcast.798), channel_id=1, source_target_pairs={{0,8},{8,0},{16,24},{24,16},{1,9},{9,1},{17,25},{25,17},{2,10},{10... | collective-permute-start | bytes 294920 | tf_op jit(solution)/shard_map/ppermute | solution.py:18
  181.6 10.0 %collective-permute-start.62 = (bf16[1,192,256]{2,1,0:T(8,128)(2,1)S(1)}, bf16[1,192,256]{2,1,0:T(8,128)(2,1)S(1)}, u32[]{:S(2)}, u32[]{:S(2)}) collective-permute-start(bf16[1,192,256]{2,1,0:T(8,128)(2,1)S(1)} %bitcast.804), channel_id=1, source_target_pairs={{0,16},{8,24},{16,0},{24,8},{1,17},{9,25},{17,1},{25,9},{2,18},{10... | collective-permute-start | bytes 294920 | tf_op jit(solution)/shard_map/ppermute | solution.py:18
  182.8 7.6 %collective-permute-start.56 = (bf16[1,192,256]{2,1,0:T(8,128)(2,1)S(1)}, bf16[1,192,256]{2,1,0:T(8,128)(2,1)S(1)}, u32[]{:S(2)}, u32[]{:S(2)}) collective-permute-start(bf16[1,192,256]{2,1,0:T(8,128)(2,1)S(1)} %bitcast.794), channel_id=1, source_target_pairs={{0,8},{8,0},{16,24},{24,16},{1,9},{9,1},{17,25},{25,17},{2,10},{10... | collective-permute-start | bytes 294920 | tf_op jit(solution)/shard_map/ppermute | solution.py:18
  185.4 10.1 %collective-permute-start.47 = (bf16[1,256,256]{2,1,0:T(8,128)(2,1)S(1)}, bf16[1,256,256]{2,1,0:T(8,128)(2,1)S(1)}, u32[]{:S(2)}, u32[]{:S(2)}) collective-permute-start(bf16[1,256,256]{2,1,0:T(8,128)(2,1)S(1)} %bitcast.768), channel_id=1, source_target_pairs={{0,8},{8,0},{16,24},{24,16},{1,9},{9,1},{17,25},{25,17},{2,10},{10... | collective-permute-start | bytes 393224 | tf_op jit(solution)/shard_map/ppermute | solution.py:18
  190.5 15.7 %collective-permute-start.39 = (bf16[1,256,256]{2,1,0:T(8,128)(2,1)S(1)}, bf16[1,256,256]{2,1,0:T(8,128)(2,1)S(1)}, u32[]{:S(2)}, u32[]{:S(2)}) collective-permute-start(bf16[1,256,256]{2,1,0:T(8,128)(2,1)S(1)} %bitcast.772), channel_id=1, source_target_pairs={{0,8},{8,0},{16,24},{24,16},{1,9},{9,1},{17,25},{25,17},{2,10},{10... | collective-permute-start | bytes 393224 | tf_op jit(solution)/shard_map/ppermute | solution.py:18
  191.6 12.8 %collective-permute-start.37 = (bf16[1,256,256]{2,1,0:T(8,128)(2,1)S(1)}, bf16[1,256,256]{2,1,0:T(8,128)(2,1)S(1)}, u32[]{:S(2)}, u32[]{:S(2)}) collective-permute-start(bf16[1,256,256]{2,1,0:T(8,128)(2,1)S(1)} %bitcast.776), channel_id=1, source_target_pairs={{0,16},{8,24},{16,0},{24,8},{1,17},{9,25},{17,1},{25,9},{2,18},{10... | collective-permute-start | bytes 393224 | tf_op jit(solution)/shard_map/ppermute | solution.py:18
  192.7 10.0 %collective-permute-start.31 = (bf16[1,256,256]{2,1,0:T(8,128)(2,1)S(1)}, bf16[1,256,256]{2,1,0:T(8,128)(2,1)S(1)}, u32[]{:S(2)}, u32[]{:S(2)}) collective-permute-start(bf16[1,256,256]{2,1,0:T(8,128)(2,1)S(1)} %bitcast.770), channel_id=1, source_target_pairs={{0,8},{8,0},{16,24},{24,16},{1,9},{9,1},{17,25},{25,17},{2,10},{10... | collective-permute-start | bytes 393224 | tf_op jit(solution)/shard_map/ppermute | solution.py:18
  195.5 25.6 %collective-permute-start.81 = (bf16[2,192,256]{2,1,0:T(8,128)(2,1)S(1)}, bf16[2,192,256]{2,1,0:T(8,128)(2,1)S(1)}, u32[]{:S(2)}, u32[]{:S(2)}) collective-permute-start(bf16[2,192,256]{2,1,0:T(8,128)(2,1)S(1)} %pad_maximum_fusion.32), channel_id=1, source_target_pairs={{0,16},{8,24},{16,0},{24,8},{1,17},{9,25},{17,1},{25,9},{2,18},{10... | collective-permute-start | bytes 589832 | tf_op jit(solution)/shard_map/ppermute | solution.py:18
  201.0 21.3 %collective-permute-start.79 = (bf16[2,192,256]{2,1,0:T(8,128)(2,1)S(1)}, bf16[2,192,256]{2,1,0:T(8,128)(2,1)S(1)}, u32[]{:S(2)}, u32[]{:S(2)}) collective-permute-start(bf16[2,192,256]{2,1,0:T(8,128)(2,1)S(1)} %pad_maximum_fusion.31), channel_id=1, source_target_pairs={{0,8},{8,0},{16,24},{24,16},{1,9},{9,1},{17,25},{25,17},{2,10},{10... | collective-permute-start | bytes 589832 | tf_op jit(solution)/shard_map/ppermute | solution.py:18
  202.8 7.0 %collective-permute-start.73 = (bf16[2,192,256]{2,1,0:T(8,128)(2,1)S(1)}, bf16[2,192,256]{2,1,0:T(8,128)(2,1)S(1)}, u32[]{:S(2)}, u32[]{:S(2)}) collective-permute-start(bf16[2,192,256]{2,1,0:T(8,128)(2,1)S(1)} %pad_maximum_fusion.30), channel_id=1, source_target_pairs={{0,16},{8,24},{16,0},{24,8},{1,17},{9,25},{17,1},{25,9},{2,18},{10... | collective-permute-start | bytes 589832 | tf_op jit(solution)/shard_map/ppermute | solution.py:18
  215.5 45.6 %collective-permute-start.48 = (bf16[2,256,256]{2,1,0:T(8,128)(2,1)}, bf16[2,256,256]{2,1,0:T(8,128)(2,1)}, u32[]{:S(2)}, u32[]{:S(2)}) collective-permute-start(bf16[2,256,256]{2,1,0:T(8,128)(2,1)} %pad_maximum_fusion.23), channel_id=1, source_target_pairs={{0,16},{8,24},{16,0},{24,8},{1,17},{9,25},{17,1},{25,9},{2,18},{10... | collective-permute-start | bytes 786440 | tf_op jit(solution)/shard_map/ppermute | solution.py:18
  217.6 51.7 %collective-permute-start.46 = (bf16[2,256,256]{2,1,0:T(8,128)(2,1)S(1)}, bf16[2,256,256]{2,1,0:T(8,128)(2,1)}, u32[]{:S(2)}, u32[]{:S(2)}) collective-permute-start(bf16[2,256,256]{2,1,0:T(8,128)(2,1)S(1)} %pad_maximum_fusion.22), channel_id=1, source_target_pairs={{0,8},{8,0},{16,24},{24,16},{1,9},{9,1},{17,25},{25,17},{2,10},{10... | collective-permute-start | bytes 786440 | tf_op jit(solution)/shard_map/ppermute | solution.py:18
  218.8 44.3 %collective-permute-start.40 = (bf16[2,256,256]{2,1,0:T(8,128)(2,1)}, bf16[2,256,256]{2,1,0:T(8,128)(2,1)}, u32[]{:S(2)}, u32[]{:S(2)}) collective-permute-start(bf16[2,256,256]{2,1,0:T(8,128)(2,1)} %pad_maximum_fusion.21), channel_id=1, source_target_pairs={{0,16},{8,24},{16,0},{24,8},{1,17},{9,25},{17,1},{25,9},{2,18},{10... | collective-permute-start | bytes 786440 | tf_op jit(solution)/shard_map/ppermute | solution.py:18
  221.1 43.0 %collective-permute-start.38 = (bf16[2,256,256]{2,1,0:T(8,128)(2,1)}, bf16[2,256,256]{2,1,0:T(8,128)(2,1)}, u32[]{:S(2)}, u32[]{:S(2)}) collective-permute-start(bf16[2,256,256]{2,1,0:T(8,128)(2,1)} %pad_maximum_fusion.20), channel_id=1, source_target_pairs={{0,8},{8,0},{16,24},{24,16},{1,9},{9,1},{17,25},{25,17},{2,10},{10... | collective-permute-start | bytes 786440 | tf_op jit(solution)/shard_map/ppermute | solution.py:18
  222.3 43.0 %collective-permute-start.32 = (bf16[2,256,256]{2,1,0:T(8,128)(2,1)}, bf16[2,256,256]{2,1,0:T(8,128)(2,1)}, u32[]{:S(2)}, u32[]{:S(2)}) collective-permute-start(bf16[2,256,256]{2,1,0:T(8,128)(2,1)} %pad_maximum_fusion.19), channel_id=1, source_target_pairs={{0,16},{8,24},{16,0},{24,8},{1,17},{9,25},{17,1},{25,9},{2,18},{10... | collective-permute-start | bytes 786440 | tf_op jit(solution)/shard_map/ppermute | solution.py:18
  277.2 38.3 %collective-permute-start.49 = (bf16[4,32,1024]{2,1,0:T(8,128)(2,1)S(1)}, bf16[4,32,1024]{2,1,0:T(8,128)(2,1)S(1)}, u32[]{:S(2)}, u32[]{:S(2)}) collective-permute-start(bf16[4,32,1024]{2,1,0:T(8,128)(2,1)S(1)} %fusion.268), channel_id=1, source_target_pairs={{0,1},{1,0},{2,3},{3,2},{4,5},{5,4},{6,7},{7,6},{8,9},{9,8},{10,11... | collective-permute-start | bytes 786440 | tf_op jit(solution)/shard_map/ppermute | solution.py:22
  279.2 10.2 %collective-permute-start.85 = (bf16[4,32,1024]{2,1,0:T(8,128)(2,1)S(1)}, bf16[4,32,1024]{2,1,0:T(8,128)(2,1)S(1)}, u32[]{:S(2)}, u32[]{:S(2)}) collective-permute-start(bf16[4,32,1024]{2,1,0:T(8,128)(2,1)S(1)} %fusion.171), channel_id=1, source_target_pairs={{0,2},{1,3},{2,4},{3,5},{4,6},{5,7},{6,0},{7,1},{8,10},{9,11},{10,... | collective-permute-start | bytes 786440 | tf_op jit(solution)/shard_map/ppermute | solution.py:27
  281.1 8.7 %collective-permute-start.82 = (bf16[4,32,1024]{2,1,0:T(8,128)(2,1)S(1)}, bf16[4,32,1024]{2,1,0:T(8,128)(2,1)S(1)}, u32[]{:S(2)}, u32[]{:S(2)}) collective-permute-start(bf16[4,32,1024]{2,1,0:T(8,128)(2,1)S(1)} %fusion.269), channel_id=1, source_target_pairs={{0,1},{1,0},{2,3},{3,2},{4,5},{5,4},{6,7},{7,6},{8,9},{9,8},{10,11... | collective-permute-start | bytes 786440 | tf_op jit(solution)/shard_map/ppermute | solution.py:22
  289.5 9.4 %collective-permute-start.86 = (bf16[4,32,1024]{2,1,0:T(8,128)(2,1)S(1)}, bf16[4,32,1024]{2,1,0:T(8,128)(2,1)S(1)}, u32[]{:S(2)}, u32[]{:S(2)}) collective-permute-start(bf16[4,32,1024]{2,1,0:T(8,128)(2,1)S(1)} %fusion.174), channel_id=1, source_target_pairs={{0,2},{1,3},{2,4},{3,5},{4,6},{5,7},{6,0},{7,1},{8,10},{9,11},{10,... | collective-permute-start | bytes 786440 | tf_op jit(solution)/shard_map/ppermute | solution.py:27
  299.0 16.5 %collective-permute-start.87 = (bf16[4,32,1024]{2,1,0:T(8,128)(2,1)S(1)}, bf16[4,32,1024]{2,1,0:T(8,128)(2,1)S(1)}, u32[]{:S(2)}, u32[]{:S(2)}) collective-permute-start(bf16[4,32,1024]{2,1,0:T(8,128)(2,1)S(1)} %fusion.177), channel_id=1, source_target_pairs={{0,2},{1,3},{2,4},{3,5},{4,6},{5,7},{6,0},{7,1},{8,10},{9,11},{10,... | collective-permute-start | bytes 786440 | tf_op jit(solution)/shard_map/ppermute | solution.py:27
  315.6 17.9 %collective-permute-start.90 = (bf16[32,1024]{1,0:T(8,128)(2,1)S(1)}, bf16[32,1024]{1,0:T(8,128)(2,1)S(1)}, u32[]{:S(2)}, u32[]{:S(2)}) collective-permute-start(bf16[32,1024]{1,0:T(8,128)(2,1)S(1)} %get-tuple-element.125), channel_id=1, source_target_pairs={{0,24},{8,16},{16,8},{24,0},{1,25},{9,17},{17,9},{25,1},{2,26},{10... | collective-permute-start | bytes 196616 | tf_op jit(solution)/shard_map/ppermute | solution.py:18
  317.2 16.4 %collective-permute-start.89 = (bf16[32,1024]{1,0:T(8,128)(2,1)S(1)}, bf16[32,1024]{1,0:T(8,128)(2,1)S(1)}, u32[]{:S(2)}, u32[]{:S(2)}) collective-permute-start(bf16[32,1024]{1,0:T(8,128)(2,1)S(1)} %get-tuple-element.126), channel_id=1, source_target_pairs={{0,16},{8,24},{16,0},{24,8},{1,17},{9,25},{17,1},{25,9},{2,18},{10... | collective-permute-start | bytes 196616 | tf_op jit(solution)/shard_map/ppermute | solution.py:18
  318.2 15.3 %collective-permute-start.88 = (bf16[32,1024]{1,0:T(8,128)(2,1)S(1)}, bf16[32,1024]{1,0:T(8,128)(2,1)}, u32[]{:S(2)}, u32[]{:S(2)}) collective-permute-start(bf16[32,1024]{1,0:T(8,128)(2,1)S(1)} %get-tuple-element.127), channel_id=1, source_target_pairs={{0,8},{8,0},{16,24},{24,16},{1,9},{9,1},{17,25},{25,17},{2,10},{10... | collective-permute-start | bytes 196616 | tf_op jit(solution)/shard_map/ppermute | solution.py:18
  (79 other events, 529.6 us)

commit v2 on v1

v2 whole, which is shorter than its diff:
```python
import functools

import jax
import jax.numpy as jnp
from jax import lax
from jax.experimental import pallas as pl
from jax.experimental.pallas import tpu as pltpu
from jax.sharding import PartitionSpec as P

learning_rate = 0.003
beta_first = 0.9
beta_second = 0.95
f32 = jnp.float32
bf16 = jnp.bfloat16


def swap(value, mask):
    return lax.ppermute(value, "dp", [(p, p ^ mask) for p in range(lax.axis_size("dp"))])


def pair(value):
    return lax.ppermute(value, "tensor", [(p, p ^ 1) for p in range(lax.axis_size("tensor"))])


def ring(value):
    size = lax.axis_size("tensor")
    return lax.ppermute(value, "tensor", [(p, (p + 2) % size) for p in range(size)])


class Chain:
    def __init__(self):
        self.tokens = []

    def add(self, value):
        self.tokens.append(value)

    def call(self, kernel, in_specs, operands, out_specs, out_shape, name, vmem, flops, read, scratch=(), aliases=None):
        inputs, held, outputs = len(operands), len(self.tokens), len(out_shape)

        def body(*refs):
            kernel(*refs[:inputs], *refs[inputs + held : inputs + held + outputs], *refs[inputs + held + outputs + 1 :])

        anywhere = pl.BlockSpec(memory_space=pl.ANY)
        outs = pl.pallas_call(
            body,
            in_specs=list(in_specs) + [anywhere] * held,
            out_specs=list(out_specs) + [anywhere],
            out_shape=list(out_shape) + [jax.ShapeDtypeStruct((8, 128), f32)],
            input_output_aliases=aliases or {},
            scratch_shapes=list(scratch),
            compiler_params=pltpu.CompilerParams(vmem_limit_bytes=vmem << 20),
            cost_estimate=pl.CostEstimate(flops=flops, bytes_accessed=read, transcendentals=0),
            name=name,
        )(*operands, *self.tokens)
        self.tokens = [outs[-1]]
        return outs[:-1]


in_vmem = pl.BlockSpec(memory_space=pltpu.VMEM)
in_hbm = pl.BlockSpec(memory_space=pltpu.HBM)


def weight_kernel(parts, total_tokens, c0, columns, tile, *refs):
    token_refs = refs[:parts]
    grad_refs = [ref for ref in refs[parts : 2 * parts]]
    sources = refs[2 * parts : 2 * parts + 5]
    targets = refs[-6:-1]
    total = refs[-1]
    starts = [at for at, _ in total_tokens[1]]
    first_gain = (1.0 - beta_first) / float(total_tokens[0]) ** 0.5
    second_gain = (1.0 - beta_second) / float(total_tokens[0])
    group = 8
    rows = sources[0].shape[1]
    lanes = 256 if columns % 256 == 0 else 128

    def work(weight_ref, first_ref, first_scale_ref, second_ref, second_scale_ref, *outs):
        out_weight, out_first, out_first_scale, out_second, out_second_scale = outs
        k, r = pl.program_id(0), pl.program_id(1)
        value = None
        for token_ref, grad_ref, start in zip(token_refs, grad_refs, starts):
            term = lax.dot_general(
                token_ref[:, pl.ds(pl.multiple_of(r * tile, tile), tile)],
                grad_ref[k, :, pl.ds(start, columns)],
                (((0,), (0,)), ((), ())),
                preferred_element_type=f32,
            )
            value = term if value is None else value + term
        total[...] = value

        def body(at, carry):
            base = pl.multiple_of(at * group, group)
            for lane in range(0, columns, lanes):
                side = pl.ds(lane, lanes)
                scale_one = first_scale_ref[0, pl.ds(base, group), side] * beta_first
                scale_two = second_scale_ref[0, pl.ds(base, group), side] * beta_second
                tops_one, tops_two = [], []
                for b in range(group):
                    span = pl.ds(pl.multiple_of(at * group * 16, group * 16) + b * 16, 16)
                    grad = total[span, side]
                    first = first_ref[0, span, side].astype(f32) * scale_one[b : b + 1] + first_gain * grad
                    second = second_ref[0, span, side].astype(f32) * scale_two[b : b + 1] + second_gain * (grad * grad)
                    root = second * lax.rsqrt(second)
                    step = (learning_rate * first) * pl.reciprocal(root + 1e-08, approx=True)
                    out_weight[0, span, side] = (weight_ref[0, span, side].astype(f32) - step).astype(bf16)
                    for state, size, code_ref, tops in (
                        (first, jnp.abs(first), out_first, tops_one),
                        (second, second, out_second, tops_two),
                    ):
                        peak = jnp.max(size, axis=0, keepdims=True)
                        wide = []
                        for c in range(0, lanes, 128):
                            top = jnp.max(peak[:, c : c + 128], axis=1, keepdims=True) + 1e-06
                            wide.append(jnp.broadcast_to(top, (1, 128)))
                        peak = jnp.concatenate(wide, axis=1)
                        tops.append(peak)
                        inverse = pl.reciprocal(peak, approx=True)
                        inverse = inverse * (2.0 - peak * inverse)
                        code_ref[0, span, side] = (state * inverse).astype(bf16)
                out_first_scale[0, pl.ds(base, group), side] = jnp.concatenate(tops_one, axis=0)
                out_second_scale[0, pl.ds(base, group), side] = jnp.concatenate(tops_two, axis=0)
            return carry

        lax.fori_loop(0, tile // (group * 16), body, 0)

    big = pl.BlockSpec((1, tile, columns), lambda k, r: (k, r, 0))
    scale = pl.BlockSpec((1, tile // 16, columns), lambda k, r: (k, r, 0))
    specs = [big, big, scale, big, scale]
    cut = lambda ref: ref.at[:, :, pl.ds(c0, columns)]
    pltpu.emit_pipeline(work, grid=(2, rows // tile), in_specs=specs, out_specs=specs)(
        *[cut(ref) for ref in sources], *[cut(ref) for ref in targets]
    )


def weight_step(chain, parts, weight, first, first_scale, second, second_scale, outs, c0, columns, total_tokens):
    rows = weight.shape[1]
    tile = min(512, rows)
    n = len(parts)
    operands = [t for t, _, _ in parts] + [g for _, g, _ in parts] + [weight, first, first_scale, second, second_scale]
    specs = [in_vmem] * (2 * n) + [in_hbm] * 5
    aliases = {}
    if outs is not None:
        aliases = {len(operands) + i: i for i in range(5)}
        specs += [in_hbm] * 5
        operands += list(outs)
    elements = 2 * rows * columns
    kernel = functools.partial(weight_kernel, n, (total_tokens, [(at, 0) for _, _, at in parts]), c0, columns, tile)
    return chain.call(
        kernel,
        specs,
        operands,
        [in_hbm] * 5,
        [jax.ShapeDtypeStruct(v.shape, v.dtype) for v in (weight, first, first_scale, second, second_scale)],
        "weight_step",
        20,
        2 * elements * sum(t.shape[0] for t, _, _ in parts) + 40 * elements,
        12 * elements,
        scratch=[pltpu.VMEM((tile, columns), f32)],
        aliases=aliases,
    )


def pre_kernel(c0, count, width, token_ref, weight_ref, send_ref, keep_ref):
    n = token_ref.shape[0] // 4
    depth = weight_ref.shape[1]

    def work(block):
        k, c = pl.program_id(0), pl.program_id(1)
        value = jnp.dot(token_ref[...], block[0], preferred_element_type=f32)
        span = pl.ds(pl.multiple_of(c * n, n), n)
        send_ref[k, span] = value[3 * n :].astype(bf16)
        for slot in range(3):
            keep_ref[slot, k, span] = value[slot * n : (slot + 1) * n]

    spec = pl.BlockSpec((1, depth, width), lambda k, c: (k, 0, c))
    pltpu.emit_pipeline(work, grid=(2, count), in_specs=[spec])(weight_ref.at[:, :, pl.ds(c0 * width, count * width)])


def partial_pre(chain, tokens, weight, c0, c1, width):
    rows, depth = tokens.shape
    n = rows // 4
    count = c1 - c0
    return chain.call(
        functools.partial(pre_kernel, c0, count, width),
        [in_vmem, in_hbm],
        [tokens, weight],
        [in_vmem, in_vmem],
        [jax.ShapeDtypeStruct((2, count * n, width), bf16), jax.ShapeDtypeStruct((3, 2, count * n, width), f32)],
        "partial_pre",
        8,
        4 * rows * depth * count * width,
        4 * depth * count * width,
    )


def hidden_kernel(c0, count, width, grad_ref, down_ref, out_ref):
    n, depth = grad_ref.shape

    def work(block):
        c = pl.program_id(0)
        out_ref[pl.ds(pl.multiple_of(c * n, n), n)] = lax.dot_general(
            grad_ref[...], block[...], (((1,), (1,)), ((), ())), preferred_element_type=f32
        )

    spec = pl.BlockSpec((width, depth), lambda c: (c, 0))
    pltpu.emit_pipeline(work, grid=(count,), in_specs=[spec])(down_ref.at[pl.ds(c0 * width, count * width)])


def hidden_grad(chain, cot, down, c0, c1, width):
    rows, depth = cot.shape
    count = c1 - c0
    (out,) = chain.call(
        functools.partial(hidden_kernel, c0, count, width),
        [in_vmem, in_hbm],
        [cot, down],
        [in_vmem],
        [jax.ShapeDtypeStruct((count * rows, width), f32)],
        "hidden_grad",
        8,
        2 * rows * depth * count * width,
        2 * depth * count * width,
    )
    return out


def step_kernel(has, offsets, *refs):
    refs = list(refs)
    take = lambda: refs.pop(0)
    counts = {0: 1, 1: 3, 2: 4, 3: 2}
    inputs = {s: [take() for _ in range(counts[s])] for s in has}
    out_x, out_y = take(), take()
    if 0 in has:
        (send,) = inputs[0]
        at, size, _ = offsets[0]
        out_x[pl.ds(at, size)] = send[0]
        out_y[pl.ds(at, size)] = send[1]
    if 1 in has:
        keep, got_x, got_y = inputs[1]
        at, size, start = offsets[1]
        span = pl.ds(start, size)
        out_x[pl.ds(at, size)] = keep[1, 0].astype(bf16)
        out_x[pl.ds(at + size, size)] = (keep[1, 1] + got_y[span].astype(f32)).astype(bf16)
        out_y[pl.ds(at, size)] = (keep[2, 0] + got_x[span].astype(f32)).astype(bf16)
        out_y[pl.ds(at + size, size)] = keep[2, 1].astype(bf16)
    if 2 in has:
        keep, hidden, got_x, got_y = inputs[2]
        at, size, start = offsets[2]
        own = take()
        gate = keep[0, 0] + got_x[pl.ds(start, size)].astype(f32) + got_y[pl.ds(start, size)].astype(f32)
        upper = (
            keep[0, 1] + got_x[pl.ds(start + size, size)].astype(f32) + got_y[pl.ds(start + size, size)].astype(f32)
        )
        grad = hidden[...]
        sigma = jax.nn.sigmoid(gate)
        first = (grad * upper * sigma * (1.0 + gate * (1.0 - sigma))).astype(bf16)
        second = (grad * gate * sigma).astype(bf16)
        own[0] = first
        own[1] = second
        for out in (out_x, out_y):
            out[pl.ds(at, size)] = first
            out[pl.ds(at + size, size)] = second
    if 3 in has:
        got_x, got_y = inputs[3]
        at, size, start = offsets[3]
        out_x[pl.ds(at, size)] = got_y[pl.ds(start, size)]
        out_y[pl.ds(at, size)] = got_x[pl.ds(start + size, size)]


def gather_kernel(offset_one, offset_two, size, n, own, x_one, y_one, x_two, y_two, out):
    width = own.shape[2]
    for c in range(size // n):
        columns = pl.ds(c * width, width)
        rows = c * n
        for k in range(2):
            at = offset_one + k * size + rows
            out[k, pl.ds(0, n), columns] = own[k, pl.ds(rows, n)]
            out[k, pl.ds(n, n), columns] = x_one[pl.ds(at, n)]
            out[k, pl.ds(2 * n, n), columns] = y_one[pl.ds(at, n)]
        out[0, pl.ds(3 * n, n), columns] = x_two[pl.ds(offset_two + rows, n)]
        out[1, pl.ds(3 * n, n), columns] = y_two[pl.ds(offset_two + rows, n)]


class Exchange:
    def __init__(self, chain, units, lag, own_rows, width):
        self.chain, self.units, self.lag, self.width, self.own_rows = chain, units, lag, width, own_rows
        self.sends, self.keeps, self.hidden = {}, {}, {}
        self.got, self.place, self.own = {}, {}, {}

    def rows_in(self, u):
        return 2 * self.own_rows * len(self.units[u][0])

    def size_of(self, u):
        return (self.units[u][2] - self.units[u][1]) * self.rows_in(u)

    def stages(self, m):
        return {s: m - s * self.lag for s in range(4) if (m - s * self.lag) in self.units}

    def step(self, m):
        stages, lag = self.stages(m), self.lag
        pieces = (1, 2, 2, 1)
        offsets, at, operands = {}, 0, []
        for s, u in stages.items():
            size = self.size_of(u)
            offsets[s] = (at, size, self.place[u, s - 1] if s else 0)
            self.place[u, s] = at
            at += pieces[s] * size
            if s == 0:
                operands += [self.sends[u]]
            elif s == 1:
                operands += [self.keeps[u], *self.got[m - lag]]
            elif s == 2:
                operands += [self.keeps[u], self.hidden[u], *self.got[m - lag]]
            else:
                operands += [*self.got[m - lag]]
        shapes = [jax.ShapeDtypeStruct((at, self.width), bf16)] * 2
        if 2 in stages:
            shapes.append(jax.ShapeDtypeStruct((2, self.size_of(stages[2]), self.width), bf16))
        outs = self.chain.call(
            functools.partial(step_kernel, tuple(stages), offsets),
            [in_vmem] * len(operands),
            operands,
            [in_vmem] * len(shapes),
            shapes,
            "exchange_step",
            4,
            8 * at * self.width,
            8 * at * self.width,
        )
        self.got[m] = (swap(outs[0], 1), swap(outs[1], 2))
        if 2 in stages:
            self.own[stages[2]] = outs[2]

    def gather(self, u):
        n, columns = self.rows_in(u), (self.units[u][2] - self.units[u][1]) * self.width
        (out,) = self.chain.call(
            functools.partial(gather_kernel, self.place[u, 2], self.place[u, 3], self.size_of(u), n),
            [in_vmem] * 5,
            [self.own[u], *self.got[u + 2 * self.lag], *self.got[u + 3 * self.lag]],
            [in_vmem],
            [jax.ShapeDtypeStruct((2, 4 * n, columns), bf16)],
            "pre_grad",
            4,
            0,
            16 * n * columns,
        )
        return out


def shards(tokens, cotangent, gate_up, down_weight, first_code, first_scale, second_code, second_scale):
    groups = lax.axis_size("dp")
    bits = groups.bit_length() - 1
    chips = lax.axis_size("tensor") // 2
    me = lax.axis_index("dp")
    own, depth = tokens.shape
    rows, units = gate_up.shape[1:]
    width = 256 if units % 256 == 0 else 128
    chunks = units // width
    total_tokens = own * groups * lax.axis_size("tensor")
    orders = [list(range(bits)), list(reversed(range(bits)))]
    every = tuple(range(chips))
    rest = every[1:]
    staged = groups == 4 and chips == 4 and chunks >= 4

    blocks = tokens.reshape(own, groups, rows)
    slots = []
    for s in range(groups):
        block = lax.dynamic_index_in_dim(blocks, me ^ s, 1, keepdims=False)
        slots.append(swap(block, s) if s else block)
    block = jnp.stack(slots)
    def around(value, axis):
        moved, found = value, []
        for _ in rest:
            moved = ring(moved)
            found.append(moved)
        result = [jnp.concatenate([value, pair(value)], axis=axis)]
        if found:
            other = pair(jnp.stack(found))
            result += [jnp.concatenate([v, other[at]], axis=axis) for at, v in enumerate(found)]
        return result

    token_blocks = around(block, 1)
    grad_blocks = around(cotangent, 0)

    if staged:
        last = chunks - max(1, (chunks * 2) // 7)
        plan = {0: ((0,), 0, last)}
        at = 4
        for c in range(0, last, 2):
            plan[at] = (rest, c, min(c + 2, last))
            at += 1
        plan[at] = (every[1:3], last, chunks)
        plan[at + 1] = ((every[3], 0), last, chunks)
    else:
        plan = {c: (every, c, c + 1) for c in range(chunks)}

    cache = {}

    def rows_of(ks):
        if ks not in cache:
            t = jnp.concatenate([token_blocks[k] for k in ks], axis=1)
            c = jnp.concatenate([grad_blocks[k] for k in ks], axis=0)
            cache[ks] = (t, c, t.reshape(-1, rows))
        return cache[ks]

    expand = lambda scale: jnp.repeat(scale, 128, axis=2)
    first_wide = expand(first_scale)
    second_wide = expand(second_scale)

    def forward(ks, c0, c1):
        t, c, _ = rows_of(ks)
        n = t.shape[1]
        lo, hi = c0 * width, c1 * width
        pre = []
        for k in range(2):
            w = gate_up[k, :, lo:hi]
            dot = lambda pick: jnp.dot(
                jnp.concatenate([t[s] for s in pick], axis=0), w, preferred_element_type=f32
            ).reshape(len(pick), n, hi - lo)
            active = list(range(groups))
            got = {s: [] for s in active}
            for b in orders[k]:
                mask = 1 << b
                send = [s for s in active if s & mask]
                active = [s for s in active if not s & mask]
                out = dot(send)
                for at, s in enumerate(send):
                    for extra in got[s]:
                        out = out.at[at].add(extra.astype(f32)) if len(send) > 1 else out + extra.astype(f32)[None]
                back = swap(out.astype(bf16), mask)
                for at, s in enumerate(send):
                    got[s ^ mask].append(back[at])
            value = dot([0])[0]
            for extra in got[0]:
                value = value + extra.astype(f32)
            pre.append(value)
        gate, upper = pre
        hidden = lax.dot_general(
            c, down_weight[lo:hi], (((1,), (1,)), ((), ())), preferred_element_type=f32
        )
        sigma = jax.nn.sigmoid(gate)
        grads = (
            (hidden * upper * sigma * (1.0 + gate * (1.0 - sigma))).astype(bf16),
            (hidden * gate * sigma).astype(bf16),
        )
        full = []
        for k in range(2):
            held = {0: grads[k]}
            for b in reversed(orders[k]):
                mask = 1 << b
                keys = sorted(held)
                back = swap(jnp.stack([held[s] for s in keys]), mask)
                for at, s in enumerate(keys):
                    held[s ^ mask] = back[at]
            full.append(jnp.concatenate([held[s] for s in range(groups)], axis=0))
        return jnp.stack(full)

    product = lambda g, c0, c1: jnp.einsum(
        "ktf,kdf->td", g, gate_up[:, :, c0 * width : c1 * width], preferred_element_type=f32
    )
    sums = {}

    def add_input_grad(u, g):
        ks, c0, c1 = plan[u]
        term = product(g, c0, c1)
        sums[ks] = term if ks not in sums else sums[ks] + term
        return sums[ks]

    def split(ks):
        value = sums[ks].reshape(groups, len(ks), 2, own, rows)
        return {k: value[:, at] for at, k in enumerate(ks)}

    grads = {}
    if staged:
        chain = Chain()
        lag = 2
        exchange = Exchange(chain, plan, lag, own, width)
        steps = [m for m in range(max(plan) + 3 * lag + 1) if exchange.stages(m)]
        sources = (gate_up, first_code, first_wide, second_code, second_wide)
        result = [None]

        def start(u):
            exchange.sends[u], exchange.keeps[u] = partial_pre(chain, rows_of(plan[u][0])[2], gate_up, *plan[u][1:], width)

        def hidden(u):
            exchange.hidden[u] = hidden_grad(chain, rows_of(plan[u][0])[1], down_weight, *plan[u][1:], width)

        def finish(u):
            grads[u] = exchange.gather(u)

        def inputs(u):
            chain.add(add_input_grad(u, grads[u]))

        def update(c0, c1):
            parts = []
            for u, (ks, a, b) in plan.items():
                if a <= c0 and c1 <= b:
                    parts.append((rows_of(ks)[2], grads[u], (c0 - a) * width))
            result[0] = weight_step(
                chain, parts, *sources, result[0], c0 * width, (c1 - c0) * width, total_tokens
            )

        hidden(0)
        start(0)
        spans = [p[1:] for p in plan.values() if p[0] == rest]
        updated_spans = []
        for place, m in enumerate(steps):
            exchange.step(m)
            if place + 1 < len(steps):
                after = steps[place + 1]
                if after in plan:
                    start(after)
                if after - 2 * lag in plan and after != 2 * lag:
                    hidden(after - 2 * lag)
            if m - 4 * lag in plan:
                finish(m - 4 * lag)
                inputs(m - 4 * lag)
                if plan[m - 4 * lag][1:] in spans[:1]:
                    update(*spans[0])
        left = [u for u in plan if u not in grads]
        for u in left:
            finish(u)
            inputs(u)
            if u == left[-2]:
                for span in spans[1:-1]:
                    update(*span)
        for span in spans[max(1, len(spans) - 1) :]:
            update(*span)
        update(last, chunks)
        outs = result[0]
    else:
        for u, unit in plan.items():
            grads[u] = forward(*unit)
            add_input_grad(u, grads[u])

    partial = [None] * chips
    for ks in sums:
        for k, part in split(ks).items():
            partial[k] = part if partial[k] is None else partial[k] + part
    order = rest + (0,)
    mine = {}
    for at in range(0, chips, 2):
        ks = order[at : at + 2]
        theirs = pair(jnp.stack([partial[k][:, 1] for k in ks]).astype(bf16))
        for spot, k in enumerate(ks):
            mine[k] = partial[k][:, 0] + theirs[spot].astype(f32)
    moving = None
    for k in order:
        value = mine[k]
        if moving is not None:
            value = value + ring(moving).astype(f32)
        moving = value.astype(bf16)
    final = [moving[0]] + [swap(moving[s], s) for s in range(1, groups)]
    final = jnp.stack(final)
    final = jnp.stack([lax.dynamic_index_in_dim(final, me ^ a, 0, keepdims=False) for a in range(groups)], axis=1)
    input_grad = final.reshape(own, depth)

    if not staged:
        chain, outs = Chain(), None
        for c, (ks, c0, c1) in plan.items():
            outs = weight_step(
                chain,
                [(rows_of(ks)[2], grads[c], 0)],
                gate_up,
                first_code,
                first_wide,
                second_code,
                second_wide,
                outs,
                c0 * width,
                (c1 - c0) * width,
                total_tokens,
            )
    updated, code_one, scale_one, code_two, scale_two = outs
    return (input_grad, updated, code_one, scale_one[:, :, ::128], code_two, scale_two[:, :, ::128])


def solution(mesh):
    placed = (
        P(("dp", "tensor"), None),
        P(("dp", "tensor"), None),
        P(None, "dp", "tensor"),
        P("tensor", None),
        P(None, "dp", "tensor"),
        P(None, "dp", "tensor"),
        P(None, "dp", "tensor"),
        P(None, "dp", "tensor"),
    )
    return jax.shard_map(
        shards,
        mesh=mesh,
        in_specs=placed,
        out_specs=(
            P(("dp", "tensor"), None),
            P(None, "dp", "tensor"),
            P(None, "dp", "tensor"),
            P(None, "dp", "tensor"),
            P(None, "dp", "tensor"),
            P(None, "dp", "tensor"),
        ),
        check_vma=False,
    )
```

time: 341 us -> 264 us (0.77); the launches traced: 335 us -> 263 us
  matrix products: 74 us -> 8.79 us
  starting transfers between devices: 88.6 us -> 41.3 us
  waiting for transfers between devices: 54.5 us -> 86.8 us
  Pallas kernels: 57.5 us -> 79.2 us
  local copies, waits for them, and re-layouts: 47 us -> 39 us
  other arithmetic: 11 us -> 6 us
    dot_general x56 -> x0, matrix products: 63.7 us -> none  [the longest x48 47.1 us: forward(): jnp.dot(jnp.concatenate([t[s] for s in pick], axis=0), w, preferred_eleme...]
    ppermute x70 -> x32, starting transfers between devices: 75.8 us -> 32.4 us  [swap(): lax.ppermute(value, 'dp', [(p, p ^ mask) for p in range(lax.axis_size('dp...]
    ppermute x70 -> x32, waiting for transfers between devices: 36.1 us -> 59.4 us  [swap(): lax.ppermute(value, 'dp', [(p, p ^ mask) for p in range(lax.axis_size('dp...]
    pallas_call x7 -> x35, Pallas kernels: 57.5 us -> 79.2 us  [call(): pl.pallas_call(body, in_specs=list(in_specs) + [anywhere] * held, out_spe...]
    unnamed x125 -> x140, local copies, waits for them, and re-layouts: 20 us -> 30.9 us
    reshape x3 -> x0, local copies, waits for them, and re-layouts: 8.95 us -> none  [rows_of(): flat = t.reshape(-1, rows)]
    ppermute x9, waiting for transfers between devices: 17.3 us -> 26.2 us  [ring(): lax.ppermute(value, 'tensor', [(p, (p + 2) % size) for p in range(size)])]
    another operation x40 -> x4, other arithmetic: 6.09 us -> 1.32 us  [the longest x2 1.22 us: around(): other = pair(jnp.stack(found))]
  transfers between devices with their start and end apart: 91 -> 47, of which waited for: 23 -> 20; matrix products, arithmetic and copies ran while one was open for 34% -> 10% of each run, Pallas kernels for 17% -> 29%
where the time goes in v2:
time: 264 us; the launch traced here: 263 us
  waiting for transfers between devices  86.8 us (33%)
  Pallas kernels  79.2 us (30%)
  starting transfers between devices  41.3 us (16%)
  local copies, waits for them, and re-layouts  39 us (15%)
  matrix products  8.79 us (3%)
  other arithmetic  6 us (2%)
    pallas_call x35, Pallas kernels, call(): pl.pallas_call(body, in_specs=list(in_specs) + [anywhere] * held, out_spe...  79.2 us
    ppermute x32, waiting for transfers between devices, swap(): lax.ppermute(value, 'dp', [(p, p ^ mask) for p in range(lax.axis_size('dp...  59.4 us
    ppermute x32, starting transfers between devices, swap(): lax.ppermute(value, 'dp', [(p, p ^ mask) for p in range(lax.axis_size('dp...  32.4 us
    unnamed x140, local copies, waits for them, and re-layouts  30.9 us
    ppermute x9, waiting for transfers between devices, ring(): lax.ppermute(value, 'tensor', [(p, (p + 2) % size) for p in range(size)])  26.2 us
    dot_general x6, matrix products, shards(): jnp.einsum('ktf,kdf->td', g, gate_up[:, :, c0 * width:c1 * width], prefer...  8.79 us
    ppermute x9, starting transfers between devices, ring(): lax.ppermute(value, 'tensor', [(p, (p + 2) % size) for p in range(size)])  8.59 us
  transfers between devices with their start and end apart: 47, of which 20 were waited for; matrix products, arithmetic and copies ran while one was open for 10% of the time, Pallas kernels for 29%

profile of v2, /device:TPU:0, one launch (start us, length us, event | category | flops | bytes accessed | tf_op | source)
XLA Modules:
  0.0 263.1 jit_solution(11928626636946419088)
XLA Ops:
  0.6 3.1 %collective-permute-start.17 = (bf16[32,4096]{1,0:T(8,128)(2,1)}, bf16[32,4096]{1,0:T(8,128)(2,1)S(1)}, u32[]{:S(2)}, u32[]{:S(2)}) collective-permute-start(bf16[32,4096]{1,0:T(8,128)(2,1)} %param.9), channel_id=1, source_target_pairs={{0,2},{1,3},{2,4},{3,5},{4,6},{5,7},{6,0},{7,1},{8,10},{9,11},{10,... | collective-permute-start | bytes 786440 | tf_op jit(solution)/shard_map/ppermute | solution.py:27
  4.9 7.4 %collective-permute-done.17 = bf16[32,4096]{1,0:T(8,128)(2,1)S(1)} collective-permute-done((bf16[32,4096]{1,0:T(8,128)(2,1)}, bf16[32,4096]{1,0:T(8,128)(2,1)S(1)}, u32[]{:S(2)}, u32[]{:S(2)}) %collective-permute-start.17) | collective-permute-done | bytes 262176 | tf_op jit(solution)/shard_map/ppermute | solution.py:27
  13.5 2.4 collective-permute-start.2
  19.5 1.5 collective-permute-done.1
  22.3 1.3 collective-permute-start.3
  23.7 1.6 collective-permute-start.19
  25.3 1.2 pad_maximum_fusion.7.refs_0_
  26.5 5.4 %copy-done = bf16[1792,4096]{1,0:T(8,128)(2,1)S(1)} copy-done((bf16[1792,4096]{1,0:T(8,128)(2,1)S(1)}, bf16[1792,4096]{1,0:T(8,128)(2,1)}, u32[]{:S(2)}) %copy-start) | copy-done | bytes 14680088
  31.9 5.6 %hidden_grad.6 = (f32[320,256]{1,0:T(8,128)S(1)}, f32[8,128]{1,0:T(8,128)S(1)}) custom-call(bf16[64,4096]{1,0:T(8,128)(2,1)S(1)} %pad_maximum_fusion.7.refs_0_, bf16[1792,4096]{1,0:T(8,128)(2,1)S(1)} %copy-done), custom_call_target="tpu_custom_call" | custom-call | flops 671088640 | bytes 10485760 | tf_op jit(solution)/shard_map/hidden_grad/pallas_call | solution.py:44
  37.5 2.1 collective-permute-start.4
  41.0 4.1 %partial_pre.6 = (bf16[2,320,256]{2,1,0:T(8,128)(2,1)S(1)}, f32[3,2,320,256]{3,2,1,0:T(8,128)S(1)}, f32[8,128]{1,0:T(8,128)S(1)}) custom-call(bf16[256,1024]{1,0:T(8,128)(2,1)S(1)} %bitcast.178, bf16[2,1024,1792]{2,1,0:T(8,128)(2,1)S(1)} %bitcast.160, f32[8,128]{1,0:T(8,128)S(1)} %get-tuple-element.116.refs_2_), custom_call_target="tpu_custom_call" | custom-call | flops 1342177280 | bytes 5242880 | tf_op jit(solution)/shard_map/partial_pre/pallas_call | solution.py:44
  45.7 1.5 collective-permute-start.10
  47.8 3.9 %collective-permute-done.9.refs_1_ = bf16[320,256]{1,0:T(8,128)(2,1)S(1)} collective-permute-done((bf16[320,256]{1,0:T(8,128)(2,1)S(1)}, bf16[320,256]{1,0:T(8,128)(2,1)S(1)}, u32[]{:S(2)}, u32[]{:S(2)}) %collective-permute-start.9) | collective-permute-done | bytes 163872 | tf_op jit(solution)/shard_map/ppermute | solution.py:18
  52.1 1.6 collective-permute-start.11
  53.6 1.5 collective-permute-start.12
  55.1 2.0 collective-permute-done.5
  58.4 1.2 collective-permute-done.6
  59.7 2.9 %partial_pre.7 = (bf16[2,384,256]{2,1,0:T(8,128)(2,1)S(1)}, f32[3,2,384,256]{3,2,1,0:T(8,128)S(1)}, f32[8,128]{1,0:T(8,128)S(1)}) custom-call(bf16[768,1024]{1,0:T(8,128)(2,1)S(1)} %bitcast.171, bf16[2,1024,1792]{2,1,0:T(8,128)(2,1)S(1)} %bitcast.160, f32[8,128]{1,0:T(8,128)S(1)} %get-tuple-element.123.refs_2_), custom_call_target="tpu_custom_call" | custom-call | flops 1610612736 | bytes 2097152 | tf_op jit(solution)/shard_map/partial_pre/pallas_call | solution.py:44
  62.9 1.6 collective-permute-start.13
  65.0 2.7 %partial_pre.8 = (bf16[2,384,256]{2,1,0:T(8,128)(2,1)S(1)}, f32[3,2,384,256]{3,2,1,0:T(8,128)S(1)}, f32[8,128]{1,0:T(8,128)S(1)}) custom-call(bf16[768,1024]{1,0:T(8,128)(2,1)S(1)} %bitcast.172, bf16[2,1024,1792]{2,1,0:T(8,128)(2,1)S(1)} %bitcast.160, f32[8,128]{1,0:T(8,128)S(1)} %get-tuple-element.132.refs_2_), custom_call_target="tpu_custom_call" | custom-call | flops 1610612736 | bytes 2097152 | tf_op jit(solution)/shard_map/partial_pre/pallas_call | solution.py:44
  67.7 1.3 collective-permute-start.21
  69.9 1.3 partial_pre.9
  71.2 6.5 %collective-permute-done.13.refs_2_.refs_4_.refs_1_ = bf16[1024,256]{1,0:T(8,128)(2,1)S(1)} collective-permute-done((bf16[1024,256]{1,0:T(8,128)(2,1)S(1)}, bf16[1024,256]{1,0:T(8,128)(2,1)S(1)}, u32[]{:S(2)}, u32[]{:S(2)}) %collective-permute-start.13) | collective-permute-done | bytes 524320 | tf_op jit(solution)/shard_map/ppermute | solution.py:18
  77.7 1.5 collective-permute-done.14.refs_3_.refs_5_.refs_2_
  80.0 1.2 collective-permute-start.16
  81.6 2.2 partial_pre.10
  84.9 2.2 partial_pre.11
  87.1 2.4 hidden_grad.7
  89.5 5.6 %collective-permute-done.15.refs_2_.refs_6_.refs_3_ = bf16[1280,256]{1,0:T(8,128)(2,1)S(1)} collective-permute-done((bf16[1280,256]{1,0:T(8,128)(2,1)S(1)}, bf16[1280,256]{1,0:T(8,128)(2,1)S(1)}, u32[]{:S(2)}, u32[]{:S(2)}) %collective-permute-start.15) | collective-permute-done | bytes 655392 | tf_op jit(solution)/shard_map/ppermute | solution.py:18
  95.2 1.2 collective-permute-done.16.refs_3_.refs_7_.refs_4_
  96.4 1.4 exchange_step.19
  102.1 1.5 collective-permute-start.26
  103.6 2.4 hidden_grad.8
  106.1 1.5 fusion
  107.7 19.2 %collective-permute-done.25.refs_1_.refs_5_ = bf16[1024,256]{1,0:T(8,128)(2,1)S(1)} collective-permute-done((bf16[1024,256]{1,0:T(8,128)(2,1)}, bf16[1024,256]{1,0:T(8,128)(2,1)S(1)}, u32[]{:S(2)}, u32[]{:S(2)}) %collective-permute-start.25) | collective-permute-done | bytes 524320 | tf_op jit(solution)/shard_map/ppermute | solution.py:18
  127.3 1.6 exchange_step.20
  128.9 1.5 collective-permute-start.27
  130.7 1.2 hidden_grad.9
  133.5 1.7 collective-permute-start.30
  137.4 2.4 hidden_grad.10
  139.8 6.9 %collective-permute-done.27.refs_2_.refs_4_.refs_1_ = bf16[1280,256]{1,0:T(8,128)(2,1)S(1)} collective-permute-done((bf16[1280,256]{1,0:T(8,128)(2,1)S(1)}, bf16[1280,256]{1,0:T(8,128)(2,1)S(1)}, u32[]{:S(2)}, u32[]{:S(2)}) %collective-permute-start.27) | collective-permute-done | bytes 655392 | tf_op jit(solution)/shard_map/ppermute | solution.py:18
  146.7 1.5 collective-permute-done.28.refs_3_.refs_5_.refs_2_
  149.9 2.6 hidden_grad.11
  152.5 8.2 %collective-permute-done.29.refs_2_.refs_4_.refs_3_.refs_1_ = bf16[1280,256]{1,0:T(8,128)(2,1)S(1)} collective-permute-done((bf16[1280,256]{1,0:T(8,128)(2,1)S(1)}, bf16[1280,256]{1,0:T(8,128)(2,1)S(1)}, u32[]{:S(2)}, u32[]{:S(2)}) %collective-permute-start.29) | collective-permute-done | bytes 655392 | tf_op jit(solution)/shard_map/ppermute | solution.py:18
  160.7 1.5 collective-permute-done.30.refs_3_.refs_5_.refs_4_.refs_2_
  163.5 1.8 fusion.6.refs_10_
  168.0 11.2 %weight_step.4 = (bf16[2,1024,1792]{2,1,0:T(8,128)(2,1)}, bf16[2,1024,1792]{2,1,0:T(8,128)(2,1)}, f32[2,64,1792]{2,1,0:T(8,128)S(1)}, bf16[2,1024,1792]{2,1,0:T(...) custom-call(bf16[256,1024]{1,0:T(8,128)(2,1)S(1)} %bitcast.179, bf16[768,1024]{1,0:T(8,128)(2,1)S(1)} %bitcast.174, ...), custom_call_target="tpu_custom_call" | custom-call | flops 2189426688 | bytes 12582912 | tf_op jit(solution)/shard_map/weight_step/pallas_call | solution.py:44
  179.2 1.3 collective-permute-start.37
  180.4 1.8 collective-permute-start.38
  182.3 1.8 bitcast_add_fusion.1.refs_3_
  186.7 1.3 fusion.11
  189.2 1.2 slice-done.8
  192.6 11.2 %weight_step.5 = (bf16[2,1024,1792]{2,1,0:T(8,128)(2,1)}, bf16[2,1024,1792]{2,1,0:T(8,128)(2,1)}, f32[2,64,1792]{2,1,0:T(8,128)S(1)}, bf16[2,1024,1792]{2,1,0:T(...) custom-call(bf16[256,1024]{1,0:T(8,128)(2,1)S(1)} %bitcast.180, ...), custom_call_target="tpu_custom_call", output_to_operand_aliasing={{0}: (9, {}), {1}: (10, {}), {2}: (11, {}), {3}: (12, {}), ... | custom-call | flops 2189426688 | bytes 12582912 | tf_op jit(solution)/shard_map/weight_step/pallas_call | solution.py:44
  203.9 1.3 fusion.9
  207.1 7.9 %collective-permute-done.41 = bf16[4,32,1024]{2,1,0:T(8,128)(2,1)S(1)} collective-permute-done((bf16[4,32,1024]{2,1,0:T(8,128)(2,1)S(1)}, bf16[4,32,1024]{2,1,0:T(8,128)(2,1)S(1)}, u32[]{:S(2)}, u32[]{:S(2)}) %collective-permute-start.41) | collective-permute-done | bytes 262176 | tf_op jit(solution)/shard_map/ppermute | solution.py:27
  215.2 8.7 %collective-permute-done.42 = bf16[4,32,1024]{2,1,0:T(8,128)(2,1)S(1)} collective-permute-done((bf16[4,32,1024]{2,1,0:T(8,128)(2,1)S(1)}, bf16[4,32,1024]{2,1,0:T(8,128)(2,1)S(1)}, u32[]{:S(2)}, u32[]{:S(2)}) %collective-permute-start.42) | collective-permute-done | bytes 262176 | tf_op jit(solution)/shard_map/ppermute | solution.py:27
  224.1 7.6 %weight_step.6 = (bf16[2,1024,1792]{2,1,0:T(8,128)(2,1)}, bf16[2,1024,1792]{2,1,0:T(8,128)(2,1)}, f32[2,64,1792]{2,1,0:T(8,128)S(1)}, bf16[2,1024,1792]{2,1,0:T(...) custom-call(bf16[256,1024]{1,0:T(8,128)(2,1)S(1)} %bitcast.181, ...), custom_call_target="tpu_custom_call", output_to_operand_aliasing={{0}: (9, {}), {1}: (10, {}), {2}: (11, {}), {3}: (12, {}), ... | custom-call | flops 1094713344 | bytes 6291456 | tf_op jit(solution)/shard_map/weight_step/pallas_call | solution.py:44
  232.7 2.5 collective-permute-start.46
  236.3 3.1 %copy-done.1 = bf16[2,1024,1792]{2,1,0:T(8,128)(2,1)S(1)} copy-done((bf16[2,1024,1792]{2,1,0:T(8,128)(2,1)S(1)}, bf16[2,1024,1792]{2,1,0:T(8,128)(2,1)}, u32[]{:S(2)}) %copy-start.1) | copy-done | bytes 7340056
  239.4 3.1 %copy-done.2 = bf16[2,1024,1792]{2,1,0:T(8,128)(2,1)S(1)} copy-done((bf16[2,1024,1792]{2,1,0:T(8,128)(2,1)S(1)}, bf16[2,1024,1792]{2,1,0:T(8,128)(2,1)}, u32[]{:S(2)}) %copy-start.2) | copy-done | bytes 7340056
  243.6 1.2 copy-done.13
  244.8 11.2 %weight_step.7 = (bf16[2,1024,1792]{2,1,0:T(8,128)(2,1)}, bf16[2,1024,1792]{2,1,0:T(8,128)(2,1)}, f32[2,64,1792]{2,1,0:T(8,128)S(1)}, bf16[2,1024,1792]{2,1,0:T(...) custom-call(bf16[512,1024]{1,0:T(8,128)(2,1)S(1)} %bitcast.185, ...), custom_call_target="tpu_custom_call", output_to_operand_aliasing={{0}: (9, {}), {1}: (10, {}), {2}: (11, {}), {3}: (12, {}), ... | custom-call | flops 2189426688 | bytes 12582912 | tf_op jit(solution)/shard_map/weight_step/pallas_call | solution.py:44
  257.9 1.5 slice.147
  260.0 1.5 slice.148
  (258 shorter events, 44.7 us)
Async XLA Ops:
  0.6 17.7 %copy-start.45 = (f32[2,64,14]{1,0,2:T(2,128)S(1)}, f32[2,64,14]{1,0,2:T(2,128)}, u32[]{:S(2)}) copy-start(f32[2,64,14]{1,0,2:T(2,128)} %param.13) | copy-start | bytes 21508
  0.6 11.6 %collective-permute-start.17 = (bf16[32,4096]{1,0:T(8,128)(2,1)}, bf16[32,4096]{1,0:T(8,128)(2,1)S(1)}, u32[]{:S(2)}, u32[]{:S(2)}) collective-permute-start(bf16[32,4096]{1,0:T(8,128)(2,1)} %param.9), channel_id=1, source_target_pairs={{0,2},{1,3},{2,4},{3,5},{4,6},{5,7},{6,0},{7,1},{8,10},{9,11},{10,... | collective-permute-start | bytes 786440 | tf_op jit(solution)/shard_map/ppermute | solution.py:27
  3.7 21.5 %collective-permute-start.8 = (bf16[32,4096]{1,0:T(8,128)(2,1)}, bf16[32,4096]{1,0:T(8,128)(2,1)}, u32[]{:S(2)}, u32[]{:S(2)}) collective-permute-start(bf16[32,4096]{1,0:T(8,128)(2,1)} %param.9), channel_id=1, source_target_pairs={{0,1},{1,0},{2,3},{3,2},{4,5},{5,4},{6,7},{7,6},{8,9},{9,8},{10,11... | collective-permute-start | bytes 786440 | tf_op jit(solution)/shard_map/ppermute | solution.py:22
  12.3 35.5 %copy-start.33 = (bf16[32,4096]{1,0:T(8,128)(2,1)}, bf16[32,4096]{1,0:T(8,128)(2,1)S(1)}, u32[]{:S(2)}) copy-start(bf16[32,4096]{1,0:T(8,128)(2,1)S(1)} %collective-permute-done.17) | copy-start | bytes 786436
  12.3 11.4 %collective-permute-start.18 = (bf16[32,4096]{1,0:T(8,128)(2,1)S(1)}, bf16[32,4096]{1,0:T(8,128)(2,1)}, u32[]{:S(2)}, u32[]{:S(2)}) collective-permute-start(bf16[32,4096]{1,0:T(8,128)(2,1)S(1)} %collective-permute-done.17), channel_id=1, source_target_pairs={{0,2},{1,3},{2,4},{3,5},{4,6},{5,7},{6,0},{7,1},{8,10},{9,11},{10,... | collective-permute-start | bytes 786440 | tf_op jit(solution)/shard_map/ppermute | solution.py:27
  12.8 6.1 %copy-start.46 = (f32[2,64,14]{1,0,2:T(2,128)S(1)}, f32[2,64,14]{1,0,2:T(2,128)}, u32[]{:S(2)}) copy-start(f32[2,64,14]{1,0,2:T(2,128)} %param.15) | copy-start | bytes 21508
  13.5 6.0 %collective-permute-start.2 = (bf16[32,1024]{1,0:T(8,128)(2,1)}, bf16[32,1024]{1,0:T(8,128)(2,1)S(1)}, u32[]{:S(2)}, u32[]{:S(2)}) collective-permute-start(bf16[32,1024]{1,0:T(8,128)(2,1)} %bitcast.155), channel_id=1, source_target_pairs={{0,24},{8,16},{16,8},{24,0},{1,25},{9,17},{17,9},{25,1},{2,26},{10... | collective-permute-start | bytes 196616 | tf_op jit(solution)/shard_map/ppermute | solution.py:18
  16.6 4.5 %collective-permute-start.1 = (bf16[32,1024]{1,0:T(8,128)(2,1)}, bf16[32,1024]{1,0:T(8,128)(2,1)S(1)}, u32[]{:S(2)}, u32[]{:S(2)}) collective-permute-start(bf16[32,1024]{1,0:T(8,128)(2,1)} %bitcast.156), channel_id=1, source_target_pairs={{0,16},{8,24},{16,0},{24,8},{1,17},{9,25},{17,1},{25,9},{2,18},{10... | collective-permute-start | bytes 196616 | tf_op jit(solution)/shard_map/ppermute | solution.py:18
  17.7 4.5 %collective-permute-start = (bf16[32,1024]{1,0:T(8,128)(2,1)}, bf16[32,1024]{1,0:T(8,128)(2,1)S(1)}, u32[]{:S(2)}, u32[]{:S(2)}) collective-permute-start(bf16[32,1024]{1,0:T(8,128)(2,1)} %bitcast.157), channel_id=1, source_target_pairs={{0,8},{8,0},{16,24},{24,16},{1,9},{9,1},{17,25},{25,17},{2,10},{10... | collective-permute-start | bytes 196616 | tf_op jit(solution)/shard_map/ppermute | solution.py:18
  21.1 18.6 %copy-start.41 = (bf16[32,1024]{1,0:T(8,128)(2,1)}, bf16[32,1024]{1,0:T(8,128)(2,1)S(1)}, u32[]{:S(2)}) copy-start(bf16[32,1024]{1,0:T(8,128)(2,1)S(1)} %collective-permute-done.1) | copy-start | bytes 196612
  22.2 17.4 %copy-start.43 = (bf16[32,1024]{1,0:T(8,128)(2,1)}, bf16[32,1024]{1,0:T(8,128)(2,1)S(1)}, u32[]{:S(2)}) copy-start(bf16[32,1024]{1,0:T(8,128)(2,1)S(1)} %collective-permute-done) | copy-start | bytes 196612
  22.3 17.4 %collective-permute-start.7 = (bf16[4,32,1024]{2,1,0:T(8,128)(2,1)S(1)}, bf16[4,32,1024]{2,1,0:T(8,128)(2,1)S(1)}, u32[]{:S(2)}, u32[]{:S(2)}) collective-permute-start(bf16[4,32,1024]{2,1,0:T(8,128)(2,1)S(1)} %pad_maximum_fusion.10), channel_id=1, source_target_pairs={{0,1},{1,0},{2,3},{3,2},{4,5},{5,4},{6,7},{7,6},{8,9},{9,8},{10,11... | collective-permute-start | bytes 786440 | tf_op jit(solution)/shard_map/ppermute | solution.py:22
  22.3 15.2 %collective-permute-start.3 = (bf16[4,32,1024]{2,1,0:T(8,128)(2,1)S(1)}, bf16[4,32,1024]{2,1,0:T(8,128)(2,1)S(1)}, u32[]{:S(2)}, u32[]{:S(2)}) collective-permute-start(bf16[4,32,1024]{2,1,0:T(8,128)(2,1)S(1)} %pad_maximum_fusion.10), channel_id=1, source_target_pairs={{0,2},{1,3},{2,4},{3,5},{4,6},{5,7},{6,0},{7,1},{8,10},{9,11},{10,... | collective-permute-start | bytes 786440 | tf_op jit(solution)/shard_map/ppermute | solution.py:27
  23.7 16.0 %collective-permute-start.19 = (bf16[32,4096]{1,0:T(8,128)(2,1)}, bf16[32,4096]{1,0:T(8,128)(2,1)S(1)}, u32[]{:S(2)}, u32[]{:S(2)}) collective-permute-start(bf16[32,4096]{1,0:T(8,128)(2,1)} %collective-permute-done.18), channel_id=1, source_target_pairs={{0,2},{1,3},{2,4},{3,5},{4,6},{5,7},{6,0},{7,1},{8,10},{9,11},{10,... | collective-permute-start | bytes 786440 | tf_op jit(solution)/shard_map/ppermute | solution.py:27
  25.3 15.7 %slice-start = ((s8[7340032]{0:T(1024)(128)(4,1)}), s8[4194304]{0:T(1024)(128)(4,1)S(1)}, s32[]{:S(2)}) async-start(s8[7340032]{0:T(1024)(128)(4,1)} %bitcast.159), calls=%async_computation | async-start | bytes 8388608
  31.9 9.1 %slice-start.1 = ((s8[7340032]{0:T(1024)(128)(4,1)}), s8[3145728]{0:T(1024)(128)(4,1)S(1)}, s32[]{:S(2)}) async-start(s8[7340032]{0:T(1024)(128)(4,1)} %bitcast.159), calls=%async_computation.1 | async-start | bytes 6291456
  37.5 9.9 %collective-permute-start.4 = (bf16[4,32,1024]{2,1,0:T(8,128)(2,1)S(1)}, bf16[4,32,1024]{2,1,0:T(8,128)(2,1)S(1)}, u32[]{:S(2)}, u32[]{:S(2)}) collective-permute-start(bf16[4,32,1024]{2,1,0:T(8,128)(2,1)S(1)} %collective-permute-done.3), channel_id=1, source_target_pairs={{0,2},{1,3},{2,4},{3,5},{4,6},{5,7},{6,0},{7,1},{8,10},{9,11},{10,... | collective-permute-start | bytes 786440 | tf_op jit(solution)/shard_map/ppermute | solution.py:27
  39.7 18.6 %copy-start.35 = (bf16[32,4096]{1,0:T(8,128)(2,1)}, bf16[32,4096]{1,0:T(8,128)(2,1)S(1)}, u32[]{:S(2)}) copy-start(bf16[32,4096]{1,0:T(8,128)(2,1)S(1)} %collective-permute-done.19) | copy-start | bytes 786436
  40.9 16.4 %collective-permute-start.20 = (bf16[3,32,4096]{2,1,0:T(8,128)(2,1)S(1)}, bf16[3,32,4096]{2,1,0:T(8,128)(2,1)S(1)}, u32[]{:S(2)}, u32[]{:S(2)}) collective-permute-start(bf16[3,32,4096]{2,1,0:T(8,128)(2,1)S(1)} %pad_maximum_fusion.5), channel_id=1, source_target_pairs={{0,1},{1,0},{2,3},{3,2},{4,5},{5,4},{6,7},{7,6},{8,9},{9,8},{10,11... | collective-permute-start | bytes 2359304 | tf_op jit(solution)/shard_map/ppermute | solution.py:22
  45.1 6.6 %collective-permute-start.9 = (bf16[320,256]{1,0:T(8,128)(2,1)S(1)}, bf16[320,256]{1,0:T(8,128)(2,1)S(1)}, u32[]{:S(2)}, u32[]{:S(2)}) collective-permute-start(bf16[320,256]{1,0:T(8,128)(2,1)S(1)} %get-tuple-element.120), channel_id=1, source_target_pairs={{0,8},{8,0},{16,24},{24,16},{1,9},{9,1},{17,25},{25,17},{2,10},{10... | collective-permute-start | bytes 491528 | tf_op jit(solution)/shard_map/ppermute | solution.py:18
  45.7 6.3 %collective-permute-start.10 = (bf16[320,256]{1,0:T(8,128)(2,1)S(1)}, bf16[320,256]{1,0:T(8,128)(2,1)S(1)}, u32[]{:S(2)}, u32[]{:S(2)}) collective-permute-start(bf16[320,256]{1,0:T(8,128)(2,1)S(1)} %get-tuple-element.121), channel_id=1, source_target_pairs={{0,16},{8,24},{16,0},{24,8},{1,17},{9,25},{17,1},{25,9},{2,18},{10... | collective-permute-start | bytes 491528 | tf_op jit(solution)/shard_map/ppermute | solution.py:18
  47.5 9.7 %collective-permute-start.5 = (bf16[4,32,1024]{2,1,0:T(8,128)(2,1)S(1)}, bf16[4,32,1024]{2,1,0:T(8,128)(2,1)S(1)}, u32[]{:S(2)}, u32[]{:S(2)}) collective-permute-start(bf16[4,32,1024]{2,1,0:T(8,128)(2,1)S(1)} %collective-permute-done.4), channel_id=1, source_target_pairs={{0,2},{1,3},{2,4},{3,5},{4,6},{5,7},{6,0},{7,1},{8,10},{9,11},{10,... | collective-permute-start | bytes 786440 | tf_op jit(solution)/shard_map/ppermute | solution.py:27
  52.1 10.5 %collective-permute-start.11 = (bf16[640,256]{1,0:T(8,128)(2,1)S(1)}, bf16[640,256]{1,0:T(8,128)(2,1)S(1)}, u32[]{:S(2)}, u32[]{:S(2)}) collective-permute-start(bf16[640,256]{1,0:T(8,128)(2,1)S(1)} %get-tuple-element.126), channel_id=1, source_target_pairs={{0,8},{8,0},{16,24},{24,16},{1,9},{9,1},{17,25},{25,17},{2,10},{10... | collective-permute-start | bytes 983048 | tf_op jit(solution)/shard_map/ppermute | solution.py:18
  53.6 9.0 %collective-permute-start.12 = (bf16[640,256]{1,0:T(8,128)(2,1)S(1)}, bf16[640,256]{1,0:T(8,128)(2,1)S(1)}, u32[]{:S(2)}, u32[]{:S(2)}) collective-permute-start(bf16[640,256]{1,0:T(8,128)(2,1)S(1)} %get-tuple-element.127), channel_id=1, source_target_pairs={{0,16},{8,24},{16,0},{24,8},{1,17},{9,25},{17,1},{25,9},{2,18},{10... | collective-permute-start | bytes 983048 | tf_op jit(solution)/shard_map/ppermute | solution.py:18
  57.2 2.4 collective-permute-start.6
  62.9 14.8 %collective-permute-start.13 = (bf16[1024,256]{1,0:T(8,128)(2,1)S(1)}, bf16[1024,256]{1,0:T(8,128)(2,1)S(1)}, u32[]{:S(2)}, u32[]{:S(2)}) collective-permute-start(bf16[1024,256]{1,0:T(8,128)(2,1)S(1)} %get-tuple-element.130), channel_id=1, source_target_pairs={{0,8},{8,0},{16,24},{24,16},{1,9},{9,1},{17,25},{25,17},{2,10},{10... | collective-permute-start | bytes 1572872 | tf_op jit(solution)/shard_map/ppermute | solution.py:18
  64.4 14.8 %collective-permute-start.14 = (bf16[1024,256]{1,0:T(8,128)(2,1)S(1)}, bf16[1024,256]{1,0:T(8,128)(2,1)S(1)}, u32[]{:S(2)}, u32[]{:S(2)}) collective-permute-start(bf16[1024,256]{1,0:T(8,128)(2,1)S(1)} %get-tuple-element.131), channel_id=1, source_target_pairs={{0,16},{8,24},{16,0},{24,8},{1,17},{9,25},{17,1},{25,9},{2,18},{10... | collective-permute-start | bytes 1572872 | tf_op jit(solution)/shard_map/ppermute | solution.py:18
  67.7 16.0 %collective-permute-start.21 = (bf16[384,256]{1,0:T(8,128)(2,1)S(1)}, bf16[384,256]{1,0:T(8,128)(2,1)S(1)}, u32[]{:S(2)}, u32[]{:S(2)}) collective-permute-start(bf16[384,256]{1,0:T(8,128)(2,1)S(1)} %get-tuple-element.144), channel_id=1, source_target_pairs={{0,8},{8,0},{16,24},{24,16},{1,9},{9,1},{17,25},{25,17},{2,10},{10... | collective-permute-start | bytes 589832 | tf_op jit(solution)/shard_map/ppermute | solution.py:18
  69.0 14.7 %collective-permute-start.22 = (bf16[384,256]{1,0:T(8,128)(2,1)S(1)}, bf16[384,256]{1,0:T(8,128)(2,1)S(1)}, u32[]{:S(2)}, u32[]{:S(2)}) collective-permute-start(bf16[384,256]{1,0:T(8,128)(2,1)S(1)} %get-tuple-element.145), channel_id=1, source_target_pairs={{0,16},{8,24},{16,0},{24,8},{1,17},{9,25},{17,1},{25,9},{2,18},{10... | collective-permute-start | bytes 589832 | tf_op jit(solution)/shard_map/ppermute | solution.py:18
  71.2 25.2 %copy-start.15 = (f32[3,2,192,256]{3,2,1,0:T(8,128)}, f32[3,2,192,256]{3,2,1,0:T(8,128)S(1)}, u32[]{:S(2)}) copy-start(f32[3,2,192,256]{3,2,1,0:T(8,128)S(1)} %get-tuple-element.149.refs_1_.refs_3_) | copy-start | bytes 3538948
  79.3 7.8 %slice-start.2 = ((s8[14680064]{0:T(1024)(128)(4,1)}), s8[4194304]{0:T(1024)(128)(4,1)S(1)}, s32[]{:S(2)}) async-start(s8[14680064]{0:T(1024)(128)(4,1)} %bitcast.161), calls=%async_computation.2 | async-start | bytes 8388608
  79.4 15.7 %collective-permute-start.15 = (bf16[1280,256]{1,0:T(8,128)(2,1)S(1)}, bf16[1280,256]{1,0:T(8,128)(2,1)S(1)}, u32[]{:S(2)}, u32[]{:S(2)}) collective-permute-start(bf16[1280,256]{1,0:T(8,128)(2,1)S(1)} %get-tuple-element.139), channel_id=1, source_target_pairs={{0,8},{8,0},{16,24},{24,16},{1,9},{9,1},{17,25},{25,17},{2,10},{10... | collective-permute-start | bytes 1966088 | tf_op jit(solution)/shard_map/ppermute | solution.py:18
  80.0 16.3 %collective-permute-start.16 = (bf16[1280,256]{1,0:T(8,128)(2,1)S(1)}, bf16[1280,256]{1,0:T(8,128)(2,1)S(1)}, u32[]{:S(2)}, u32[]{:S(2)}) collective-permute-start(bf16[1280,256]{1,0:T(8,128)(2,1)S(1)} %get-tuple-element.140), channel_id=1, source_target_pairs={{0,16},{8,24},{16,0},{24,8},{1,17},{9,25},{17,1},{25,9},{2,18},{10... | collective-permute-start | bytes 1966088 | tf_op jit(solution)/shard_map/ppermute | solution.py:18
  81.4 5.7 %slice-start.3 = ((s8[14680064]{0:T(1024)(128)(4,1)}), s8[4194304]{0:T(1024)(128)(4,1)S(1)}, s32[]{:S(2)}) async-start(s8[14680064]{0:T(1024)(128)(4,1)} %bitcast.161), calls=%async_computation.3 | async-start | bytes 8388608
  98.6 33.3 %collective-permute-start.23 = (bf16[1408,256]{1,0:T(8,128)(2,1)}, bf16[1408,256]{1,0:T(8,128)(2,1)S(1)}, u32[]{:S(2)}, u32[]{:S(2)}) collective-permute-start(bf16[1408,256]{1,0:T(8,128)(2,1)} %get-tuple-element.158), channel_id=1, source_target_pairs={{0,8},{8,0},{16,24},{24,16},{1,9},{9,1},{17,25},{25,17},{2,10},{10... | collective-permute-start | bytes 2162696 | tf_op jit(solution)/shard_map/ppermute | solution.py:18
  99.2 32.8 %collective-permute-start.24 = (bf16[1408,256]{1,0:T(8,128)(2,1)}, bf16[1408,256]{1,0:T(8,128)(2,1)S(1)}, u32[]{:S(2)}, u32[]{:S(2)}) collective-permute-start(bf16[1408,256]{1,0:T(8,128)(2,1)} %get-tuple-element.159), channel_id=1, source_target_pairs={{0,16},{8,24},{16,0},{24,8},{1,17},{9,25},{17,1},{25,9},{2,18},{10... | collective-permute-start | bytes 2162696 | tf_op jit(solution)/shard_map/ppermute | solution.py:18
  100.9 26.0 %collective-permute-start.25 = (bf16[1024,256]{1,0:T(8,128)(2,1)}, bf16[1024,256]{1,0:T(8,128)(2,1)S(1)}, u32[]{:S(2)}, u32[]{:S(2)}) collective-permute-start(bf16[1024,256]{1,0:T(8,128)(2,1)} %get-tuple-element.160), channel_id=1, source_target_pairs={{0,8},{8,0},{16,24},{24,16},{1,9},{9,1},{17,25},{25,17},{2,10},{10... | collective-permute-start | bytes 1572872 | tf_op jit(solution)/shard_map/ppermute | solution.py:18
  102.1 25.2 %collective-permute-start.26 = (bf16[1024,256]{1,0:T(8,128)(2,1)}, bf16[1024,256]{1,0:T(8,128)(2,1)}, u32[]{:S(2)}, u32[]{:S(2)}) collective-permute-start(bf16[1024,256]{1,0:T(8,128)(2,1)} %get-tuple-element.161), channel_id=1, source_target_pairs={{0,16},{8,24},{16,0},{24,8},{1,17},{9,25},{17,1},{25,9},{2,18},{10... | collective-permute-start | bytes 1572872 | tf_op jit(solution)/shard_map/ppermute | solution.py:18
  107.7 21.2 %copy-start.17 = (f32[256,1024,1]{1,0,2:T(8,128)}, f32[256,1024,1]{1,0,2:T(8,128)S(1)}, u32[]{:S(2)}) copy-start(f32[256,1024,1]{1,0,2:T(8,128)S(1)} %fusion) | copy-start | bytes 3145732
  128.9 17.7 %collective-permute-start.27 = (bf16[1280,256]{1,0:T(8,128)(2,1)S(1)}, bf16[1280,256]{1,0:T(8,128)(2,1)S(1)}, u32[]{:S(2)}, u32[]{:S(2)}) collective-permute-start(bf16[1280,256]{1,0:T(8,128)(2,1)S(1)} %get-tuple-element.169), channel_id=1, source_target_pairs={{0,8},{8,0},{16,24},{24,16},{1,9},{9,1},{17,25},{25,17},{2,10},{10... | collective-permute-start | bytes 1966088 | tf_op jit(solution)/shard_map/ppermute | solution.py:18
  130.5 17.7 %collective-permute-start.28 = (bf16[1280,256]{1,0:T(8,128)(2,1)S(1)}, bf16[1280,256]{1,0:T(8,128)(2,1)S(1)}, u32[]{:S(2)}, u32[]{:S(2)}) collective-permute-start(bf16[1280,256]{1,0:T(8,128)(2,1)S(1)} %get-tuple-element.170), channel_id=1, source_target_pairs={{0,16},{8,24},{16,0},{24,8},{1,17},{9,25},{17,1},{25,9},{2,18},{10... | collective-permute-start | bytes 1966088 | tf_op jit(solution)/shard_map/ppermute | solution.py:18
  132.9 27.8 %collective-permute-start.29 = (bf16[1280,256]{1,0:T(8,128)(2,1)S(1)}, bf16[1280,256]{1,0:T(8,128)(2,1)S(1)}, u32[]{:S(2)}, u32[]{:S(2)}) collective-permute-start(bf16[1280,256]{1,0:T(8,128)(2,1)S(1)} %get-tuple-element.174), channel_id=1, source_target_pairs={{0,8},{8,0},{16,24},{24,16},{1,9},{9,1},{17,25},{25,17},{2,10},{10... | collective-permute-start | bytes 1966088 | tf_op jit(solution)/shard_map/ppermute | solution.py:18
  133.5 28.7 %collective-permute-start.30 = (bf16[1280,256]{1,0:T(8,128)(2,1)S(1)}, bf16[1280,256]{1,0:T(8,128)(2,1)S(1)}, u32[]{:S(2)}, u32[]{:S(2)}) collective-permute-start(bf16[1280,256]{1,0:T(8,128)(2,1)S(1)} %get-tuple-element.175), channel_id=1, source_target_pairs={{0,16},{8,24},{16,0},{24,8},{1,17},{9,25},{17,1},{25,9},{2,18},{10... | collective-permute-start | bytes 1966088 | tf_op jit(solution)/shard_map/ppermute | solution.py:18
  149.1 30.1 %collective-permute-start.33 = (bf16[896,256]{1,0:T(8,128)(2,1)S(1)}, bf16[896,256]{1,0:T(8,128)(2,1)S(1)}, u32[]{:S(2)}, u32[]{:S(2)}) collective-permute-start(bf16[896,256]{1,0:T(8,128)(2,1)S(1)} %get-tuple-element.181), channel_id=1, source_target_pairs={{0,8},{8,0},{16,24},{24,16},{1,9},{9,1},{17,25},{25,17},{2,10},{10... | collective-permute-start | bytes 1376264 | tf_op jit(solution)/shard_map/ppermute | solution.py:18
  149.6 29.5 %collective-permute-start.34 = (bf16[896,256]{1,0:T(8,128)(2,1)S(1)}, bf16[896,256]{1,0:T(8,128)(2,1)S(1)}, u32[]{:S(2)}, u32[]{:S(2)}) collective-permute-start(bf16[896,256]{1,0:T(8,128)(2,1)S(1)} %get-tuple-element.182), channel_id=1, source_target_pairs={{0,16},{8,24},{16,0},{24,8},{1,17},{9,25},{17,1},{25,9},{2,18},{10... | collective-permute-start | bytes 1376264 | tf_op jit(solution)/shard_map/ppermute | solution.py:18
  149.9 13.4 %copy-start.28 = (bf16[2,384,256]{2,1,0:T(8,128)(2,1)S(1)}, bf16[2,384,256]{2,1,0:T(8,128)(2,1)}, u32[]{:S(2)}) copy-start(bf16[2,384,256]{2,1,0:T(8,128)(2,1)} %copy-done.27) | copy-start | bytes 1179652
  162.4 21.8 %collective-permute-start.31 = (bf16[704,256]{1,0:T(8,128)(2,1)S(1)}, bf16[704,256]{1,0:T(8,128)(2,1)S(1)}, u32[]{:S(2)}, u32[]{:S(2)}) collective-permute-start(bf16[704,256]{1,0:T(8,128)(2,1)S(1)} %get-tuple-element.178), channel_id=1, source_target_pairs={{0,8},{8,0},{16,24},{24,16},{1,9},{9,1},{17,25},{25,17},{2,10},{10... | collective-permute-start | bytes 1081352 | tf_op jit(solution)/shard_map/ppermute | solution.py:18
  163.0 21.2 %collective-permute-start.32 = (bf16[704,256]{1,0:T(8,128)(2,1)S(1)}, bf16[704,256]{1,0:T(8,128)(2,1)S(1)}, u32[]{:S(2)}, u32[]{:S(2)}) collective-permute-start(bf16[704,256]{1,0:T(8,128)(2,1)S(1)} %get-tuple-element.179), channel_id=1, source_target_pairs={{0,16},{8,24},{16,0},{24,8},{1,17},{9,25},{17,1},{25,9},{2,18},{10... | collective-permute-start | bytes 1081352 | tf_op jit(solution)/shard_map/ppermute | solution.py:18
  179.2 7.4 %collective-permute-start.37 = (bf16[256,256]{1,0:T(8,128)(2,1)S(1)}, bf16[256,256]{1,0:T(8,128)(2,1)S(1)}, u32[]{:S(2)}, u32[]{:S(2)}) collective-permute-start(bf16[256,256]{1,0:T(8,128)(2,1)S(1)} %get-tuple-element.199), channel_id=1, source_target_pairs={{0,8},{8,0},{16,24},{24,16},{1,9},{9,1},{17,25},{25,17},{2,10},{10... | collective-permute-start | bytes 393224 | tf_op jit(solution)/shard_map/ppermute | solution.py:18
  180.4 6.1 %collective-permute-start.38 = (bf16[256,256]{1,0:T(8,128)(2,1)S(1)}, bf16[256,256]{1,0:T(8,128)(2,1)S(1)}, u32[]{:S(2)}, u32[]{:S(2)}) collective-permute-start(bf16[256,256]{1,0:T(8,128)(2,1)S(1)} %get-tuple-element.200), channel_id=1, source_target_pairs={{0,16},{8,24},{16,0},{24,8},{1,17},{9,25},{17,1},{25,9},{2,18},{10... | collective-permute-start | bytes 393224 | tf_op jit(solution)/shard_map/ppermute | solution.py:18
  184.3 19.5 %collective-permute-start.35 = (bf16[256,256]{1,0:T(8,128)(2,1)S(1)}, bf16[256,256]{1,0:T(8,128)(2,1)S(1)}, u32[]{:S(2)}, u32[]{:S(2)}) collective-permute-start(bf16[256,256]{1,0:T(8,128)(2,1)S(1)} %get-tuple-element.191), channel_id=1, source_target_pairs={{0,8},{8,0},{16,24},{24,16},{1,9},{9,1},{17,25},{25,17},{2,10},{10... | collective-permute-start | bytes 393224 | tf_op jit(solution)/shard_map/ppermute | solution.py:18
  184.9 18.9 %collective-permute-start.36 = (bf16[256,256]{1,0:T(8,128)(2,1)S(1)}, bf16[256,256]{1,0:T(8,128)(2,1)S(1)}, u32[]{:S(2)}, u32[]{:S(2)}) collective-permute-start(bf16[256,256]{1,0:T(8,128)(2,1)S(1)} %get-tuple-element.192), channel_id=1, source_target_pairs={{0,16},{8,24},{16,0},{24,8},{1,17},{9,25},{17,1},{25,9},{2,18},{10... | collective-permute-start | bytes 393224 | tf_op jit(solution)/shard_map/ppermute | solution.py:18
  189.1 17.7 %collective-permute-start.40 = (bf16[2,4,32,1024]{3,2,1,0:T(8,128)(2,1)S(1)}, bf16[2,4,32,1024]{3,2,1,0:T(8,128)(2,1)S(1)}, u32[]{:S(2)}, u32[]{:S(2)}) collective-permute-start(bf16[2,4,32,1024]{3,2,1,0:T(8,128)(2,1)S(1)} %pad_maximum_fusion.9), channel_id=1, source_target_pairs={{0,1},{1,0},{2,3},{3,2},{4,5},{5,4},{6,7},{7,6},{8,9},{9,8},{10,11... | collective-permute-start | bytes 1572872 | tf_op jit(solution)/shard_map/ppermute | solution.py:22
  192.6 11.2 %copy-start.20 = (bf16[704,256]{1,0:T(8,128)(2,1)S(1)}, bf16[704,256]{1,0:T(8,128)(2,1)}, u32[]{:S(2)}) copy-start(bf16[704,256]{1,0:T(8,128)(2,1)} %copy-done.19) | copy-start | bytes 1081348
  192.6 11.2 %copy-start.22 = (bf16[704,256]{1,0:T(8,128)(2,1)S(1)}, bf16[704,256]{1,0:T(8,128)(2,1)}, u32[]{:S(2)}) copy-start(bf16[704,256]{1,0:T(8,128)(2,1)} %copy-done.21) | copy-start | bytes 1081348
  206.8 8.2 %collective-permute-start.41 = (bf16[4,32,1024]{2,1,0:T(8,128)(2,1)S(1)}, bf16[4,32,1024]{2,1,0:T(8,128)(2,1)S(1)}, u32[]{:S(2)}, u32[]{:S(2)}) collective-permute-start(bf16[4,32,1024]{2,1,0:T(8,128)(2,1)S(1)} %fusion.21), channel_id=1, source_target_pairs={{0,2},{1,3},{2,4},{3,5},{4,6},{5,7},{6,0},{7,1},{8,10},{9,11},{10,... | collective-permute-start | bytes 786440 | tf_op jit(solution)/shard_map/ppermute | solution.py:27
  207.0 8.2 %collective-permute-start.39 = (bf16[2,4,32,1024]{3,2,1,0:T(8,128)(2,1)S(1)}, bf16[2,4,32,1024]{3,2,1,0:T(8,128)(2,1)S(1)}, u32[]{:S(2)}, u32[]{:S(2)}) collective-permute-start(bf16[2,4,32,1024]{3,2,1,0:T(8,128)(2,1)S(1)} %pad_maximum_fusion.8), channel_id=1, source_target_pairs={{0,1},{1,0},{2,3},{3,2},{4,5},{5,4},{6,7},{7,6},{8,9},{9,8},{10,11... | collective-permute-start | bytes 1572872 | tf_op jit(solution)/shard_map/ppermute | solution.py:22
  215.1 8.7 %collective-permute-start.42 = (bf16[4,32,1024]{2,1,0:T(8,128)(2,1)S(1)}, bf16[4,32,1024]{2,1,0:T(8,128)(2,1)S(1)}, u32[]{:S(2)}, u32[]{:S(2)}) collective-permute-start(bf16[4,32,1024]{2,1,0:T(8,128)(2,1)S(1)} %fusion.24), channel_id=1, source_target_pairs={{0,2},{1,3},{2,4},{3,5},{4,6},{5,7},{6,0},{7,1},{8,10},{9,11},{10,... | collective-permute-start | bytes 786440 | tf_op jit(solution)/shard_map/ppermute | solution.py:27
  224.0 8.6 %collective-permute-start.43 = (bf16[4,32,1024]{2,1,0:T(8,128)(2,1)S(1)}, bf16[4,32,1024]{2,1,0:T(8,128)(2,1)S(1)}, u32[]{:S(2)}, u32[]{:S(2)}) collective-permute-start(bf16[4,32,1024]{2,1,0:T(8,128)(2,1)S(1)} %fusion.27), channel_id=1, source_target_pairs={{0,2},{1,3},{2,4},{3,5},{4,6},{5,7},{6,0},{7,1},{8,10},{9,11},{10,... | collective-permute-start | bytes 786440 | tf_op jit(solution)/shard_map/ppermute | solution.py:27
  224.1 12.2 %copy-start.8 = (bf16[4,128,1024]{2,1,0:T(8,128)(2,1)S(1)}, bf16[4,128,1024]{2,1,0:T(8,128)(2,1)}, u32[]{:S(2)}) copy-start(bf16[4,128,1024]{2,1,0:T(8,128)(2,1)} %copy-done.7) | copy-start | bytes 3145732
  224.1 12.2 %copy-start.26 = (bf16[2,512,512]{2,1,0:T(8,128)(2,1)S(1)}, bf16[2,512,512]{2,1,0:T(8,128)(2,1)}, u32[]{:S(2)}) copy-start(bf16[2,512,512]{2,1,0:T(8,128)(2,1)} %copy-done.25) | copy-start | bytes 3145732
  232.7 29.5 %collective-permute-start.46 = (bf16[32,1024]{1,0:T(8,128)(2,1)S(1)}, bf16[32,1024]{1,0:T(8,128)(2,1)S(1)}, u32[]{:S(2)}, u32[]{:S(2)}) collective-permute-start(bf16[32,1024]{1,0:T(8,128)(2,1)S(1)} %get-tuple-element.262), channel_id=1, source_target_pairs={{0,24},{8,16},{16,8},{24,0},{1,25},{9,17},{17,9},{25,1},{2,26},{10... | collective-permute-start | bytes 196616 | tf_op jit(solution)/shard_map/ppermute | solution.py:18
  235.2 27.0 %collective-permute-start.45 = (bf16[32,1024]{1,0:T(8,128)(2,1)S(1)}, bf16[32,1024]{1,0:T(8,128)(2,1)S(1)}, u32[]{:S(2)}, u32[]{:S(2)}) collective-permute-start(bf16[32,1024]{1,0:T(8,128)(2,1)S(1)} %get-tuple-element.263), channel_id=1, source_target_pairs={{0,16},{8,24},{16,0},{24,8},{1,17},{9,25},{17,1},{25,9},{2,18},{10... | collective-permute-start | bytes 196616 | tf_op jit(solution)/shard_map/ppermute | solution.py:18
  235.4 26.8 %collective-permute-start.44 = (bf16[32,1024]{1,0:T(8,128)(2,1)S(1)}, bf16[32,1024]{1,0:T(8,128)(2,1)S(1)}, u32[]{:S(2)}, u32[]{:S(2)}) collective-permute-start(bf16[32,1024]{1,0:T(8,128)(2,1)S(1)} %get-tuple-element.264), channel_id=1, source_target_pairs={{0,8},{8,0},{16,24},{24,16},{1,9},{9,1},{17,25},{25,17},{2,10},{10... | collective-permute-start | bytes 196616 | tf_op jit(solution)/shard_map/ppermute | solution.py:18
  (44 other events, 109.1 us)

commit v3 on v2

--- a/solution.py
+++ b/solution.py
@@ -12,19 +12,83 @@
 beta_second = 0.95
 f32 = jnp.float32
 bf16 = jnp.bfloat16
+in_vmem = pl.BlockSpec(memory_space=pltpu.VMEM)
+in_hbm = pl.BlockSpec(memory_space=pltpu.HBM)
 
 
 def swap(value, mask):
     return lax.ppermute(value, "dp", [(p, p ^ mask) for p in range(lax.axis_size("dp"))])
 
 
+def back(value, distance):
+    size = lax.axis_size("tensor")
+    return lax.ppermute(value, "tensor", [(p, (p - 2 * distance) % size) for p in range(size)])
+
+
+def onward(value, distance):
+    return back(value, -distance)
+
+
 def pair(value):
     return lax.ppermute(value, "tensor", [(p, p ^ 1) for p in range(lax.axis_size("tensor"))])
 
 
-def ring(value):
-    size = lax.axis_size("tensor")
-    return lax.ppermute(value, "tensor", [(p, (p + 2) % size) for p in range(size)])
+def split_kernel(groups, rows, me_ref, tokens_ref, *outs):
+    for s in range(groups):
+        at = pl.multiple_of((me_ref[0] ^ s) * rows, 128)
+        outs[s][...] = tokens_ref[:, pl.ds(at, rows)]
+
+
+def split_columns(tokens, groups, me):
+    own, depth = tokens.shape
+    rows = depth // groups
+    return pl.pallas_call(
+        functools.partial(split_kernel, groups, rows),
+        in_specs=[pl.BlockSpec(memory_space=pltpu.SMEM), in_vmem],
+        out_specs=[in_vmem] * groups,
+        out_shape=[jax.ShapeDtypeStruct((own, rows), bf16)] * groups,
+        compiler_params=pltpu.CompilerParams(vmem_limit_bytes=4 << 20),
+        name="split_columns",
+    )(jnp.reshape(me, (1,)).astype(jnp.int32), tokens)
+
+
+def hold_kernel(value_ref, *refs):
+    refs[-1][...] = value_ref[...]
+
+
+def hold_until(value, *others):
+    return pl.pallas_call(
+        hold_kernel,
+        in_specs=[in_vmem] + [pl.BlockSpec(memory_space=pl.ANY)] * len(others),
+        out_specs=in_vmem,
+        out_shape=jax.ShapeDtypeStruct(value.shape, value.dtype),
+        compiler_params=pltpu.CompilerParams(vmem_limit_bytes=4 << 20),
+        name="hold",
+    )(value, *others)
+
+
+def pack_kernel(cuts, axis, *refs):
+    out, at = refs[-1], 0
+    for ref, (lo, hi) in zip(refs, cuts):
+        if axis:
+            out[:, at : at + hi - lo] = ref[:, lo:hi]
+        else:
+            out[at : at + hi - lo] = ref[lo:hi]
+        at += hi - lo
+
+
+def pack(pieces, axis, *others):
+    shape = list(pieces[0][0].shape)
+    shape[axis] = sum(hi - lo for _, lo, hi in pieces)
+    return pl.pallas_call(
+        functools.partial(pack_kernel, [p[1:] for p in pieces], axis),
+        in_specs=[in_vmem] * len(pieces) + [pl.BlockSpec(memory_space=pl.ANY)] * len(others),
+        out_specs=in_vmem,
+        out_shape=jax.ShapeDtypeStruct(tuple(shape), pieces[0][0].dtype),
+        compiler_params=pltpu.CompilerParams(vmem_limit_bytes=4 << 20),
+        cost_estimate=pl.CostEstimate(flops=1, bytes_accessed=1, transcendentals=0),
+        name="pack",
+    )(*[p[0] for p in pieces], *others)
 
 
 class Chain:
@@ -49,112 +113,153 @@
             input_output_aliases=aliases or {},
             scratch_shapes=list(scratch),
             compiler_params=pltpu.CompilerParams(vmem_limit_bytes=vmem << 20),
-            cost_estimate=pl.CostEstimate(flops=flops, bytes_accessed=read, transcendentals=0),
+            cost_estimate=pl.CostEstimate(flops=1, bytes_accessed=1, transcendentals=0),
             name=name,
         )(*operands, *self.tokens)
         self.tokens = [outs[-1]]
         return outs[:-1]
 
 
-in_vmem = pl.BlockSpec(memory_space=pltpu.VMEM)
-in_hbm = pl.BlockSpec(memory_space=pltpu.HBM)
-
-
-def weight_kernel(parts, total_tokens, c0, columns, tile, *refs):
+def weight_kernel(parts, total_tokens, starts, c0, columns, tile, *refs):
     token_refs = refs[:parts]
-    grad_refs = [ref for ref in refs[parts : 2 * parts]]
-    sources = refs[2 * parts : 2 * parts + 5]
-    targets = refs[-6:-1]
-    total = refs[-1]
-    starts = [at for at, _ in total_tokens[1]]
-    first_gain = (1.0 - beta_first) / float(total_tokens[0]) ** 0.5
-    second_gain = (1.0 - beta_second) / float(total_tokens[0])
+    grad_refs = refs[parts : 2 * parts]
+    weight_hbm, first_hbm, first_scale, second_hbm, second_scale = refs[2 * parts : 2 * parts + 5]
+    outs_hbm = refs[-12:-9]
+    first_tops, second_tops, top_table, total, rows_max, held_in, held_out, sem_in, sem_out = refs[-9:]
+    first_gain = (1.0 - beta_first) / float(total_tokens) ** 0.5
+    second_gain = (1.0 - beta_second) / float(total_tokens)
     group = 8
-    rows = sources[0].shape[1]
-    lanes = 256 if columns % 256 == 0 else 128
-
-    def work(weight_ref, first_ref, first_scale_ref, second_ref, second_scale_ref, *outs):
-        out_weight, out_first, out_first_scale, out_second, out_second_scale = outs
-        k, r = pl.program_id(0), pl.program_id(1)
+    tiles = weight_hbm.shape[1] // tile
+    ins_hbm = (weight_hbm, first_hbm, second_hbm)
+
+    def place(i):
+        return i // tiles, pl.ds(pl.multiple_of(i % tiles * tile, tile), tile)
+
+    def copies(i, out):
+        k, span = place(i)
+        hbm, held, sem = (outs_hbm, held_out, sem_out) if out else (ins_hbm, held_in, sem_in)
+        result = []
+        for a in range(3):
+            far = hbm[a].at[k, span, pl.ds(c0, columns)]
+            near = held.at[a, k, span]
+            result.append(pltpu.make_async_copy(*((near, far) if out else (far, near)), sem.at[a, i]))
+        return result
+
+    def begin(i, carry):
+        for copy in copies(i, False):
+            copy.start()
+        return carry
+
+    lax.fori_loop(0, 2 * tiles, begin, 0)
+
+    def work(i, carry):
+        k, span_all = place(i)
         value = None
         for token_ref, grad_ref, start in zip(token_refs, grad_refs, starts):
             term = lax.dot_general(
-                token_ref[:, pl.ds(pl.multiple_of(r * tile, tile), tile)],
+                token_ref[:, span_all],
                 grad_ref[k, :, pl.ds(start, columns)],
                 (((0,), (0,)), ((), ())),
                 preferred_element_type=f32,
             )
             value = term if value is None else value + term
         total[...] = value
+        for copy in copies(i, False):
+            copy.wait()
 
         def body(at, carry):
             base = pl.multiple_of(at * group, group)
-            for lane in range(0, columns, lanes):
-                side = pl.ds(lane, lanes)
-                scale_one = first_scale_ref[0, pl.ds(base, group), side] * beta_first
-                scale_two = second_scale_ref[0, pl.ds(base, group), side] * beta_second
-                tops_one, tops_two = [], []
+            blocks = pl.ds(pl.multiple_of(i % tiles * (tile // 16) + base, group), group)
+            tops_one, tops_two = [], []
+            for lane in range(0, columns, 128):
+                side = pl.ds(lane, 128)
+                slot = 2 * (lane // 128)
+                scale_one = first_scale[k, blocks, pl.ds(c0 + lane, 128)] * beta_first
+                scale_two = second_scale[k, blocks, pl.ds(c0 + lane, 128)] * beta_second
+                states = []
                 for b in range(group):
-                    span = pl.ds(pl.multiple_of(at * group * 16, group * 16) + b * 16, 16)
-                    grad = total[span, side]
-                    first = first_ref[0, span, side].astype(f32) * scale_one[b : b + 1] + first_gain * grad
-                    second = second_ref[0, span, side].astype(f32) * scale_two[b : b + 1] + second_gain * (grad * grad)
+                    near = pl.ds(pl.multiple_of(at * group * 16, group * 16) + b * 16, 16)
+                    span = pl.ds(pl.multiple_of(i % tiles * tile + at * group * 16, group * 16) + b * 16, 16)
+                    grad = total[near, side]
+                    first = held_in[1, k, span, side].astype(f32) * scale_one[b : b + 1] + first_gain * grad
+                    second = held_in[2, k, span, side].astype(f32) * scale_two[b : b + 1]
+                    second = second + second_gain * (grad * grad)
                     root = second * lax.rsqrt(second)
                     step = (learning_rate * first) * pl.reciprocal(root + 1e-08, approx=True)
-                    out_weight[0, span, side] = (weight_ref[0, span, side].astype(f32) - step).astype(bf16)
-                    for state, size, code_ref, tops in (
-                        (first, jnp.abs(first), out_first, tops_one),
-                        (second, second, out_second, tops_two),
-                    ):
-                        peak = jnp.max(size, axis=0, keepdims=True)
-                        wide = []
-                        for c in range(0, lanes, 128):
-                            top = jnp.max(peak[:, c : c + 128], axis=1, keepdims=True) + 1e-06
-                            wide.append(jnp.broadcast_to(top, (1, 128)))
-                        peak = jnp.concatenate(wide, axis=1)
-                        tops.append(peak)
-                        inverse = pl.reciprocal(peak, approx=True)
-                        inverse = inverse * (2.0 - peak * inverse)
-                        code_ref[0, span, side] = (state * inverse).astype(bf16)
-                out_first_scale[0, pl.ds(base, group), side] = jnp.concatenate(tops_one, axis=0)
-                out_second_scale[0, pl.ds(base, group), side] = jnp.concatenate(tops_two, axis=0)
+                    held_out[0, k, span, side] = (held_in[0, k, span, side].astype(f32) - step).astype(bf16)
+                    size = jnp.abs(first)
+                    rows_max[slot, pl.ds(b * 8, 8)] = jnp.maximum(size[:8], size[8:])
+                    rows_max[slot + 1, pl.ds(b * 8, 8)] = jnp.maximum(second[:8], second[8:])
+                    states.append((first, second))
+                inverses = []
+                for kind, tops in ((0, tops_one), (1, tops_two)):
+                    peak = rows_max[slot + kind, pl.ds(0, group, stride=8)]
+                    for j in range(1, 8):
+                        peak = jnp.maximum(peak, rows_max[slot + kind, pl.ds(j, group, stride=8)])
+                    top = jnp.max(peak, axis=1, keepdims=True) + 1e-06
+                    tops.append(top)
+                    wide = jnp.broadcast_to(top, (group, 128))
+                    inverse = pl.reciprocal(wide, approx=True)
+                    inverses.append(inverse * (2.0 - wide * inverse))
+                for b, (first, second) in enumerate(states):
+                    span = pl.ds(pl.multiple_of(i % tiles * tile + at * group * 16, group * 16) + b * 16, 16)
+                    held_out[1, k, span, side] = (first * inverses[0][b : b + 1]).astype(bf16)
+                    held_out[2, k, span, side] = (second * inverses[1][b : b + 1]).astype(bf16)
+            top_table[k, blocks, pl.ds(0, columns // 128)] = jnp.concatenate(tops_one, axis=1)
+            top_table[2 + k, blocks, pl.ds(0, columns // 128)] = jnp.concatenate(tops_two, axis=1)
             return carry
 
         lax.fori_loop(0, tile // (group * 16), body, 0)
-
-    big = pl.BlockSpec((1, tile, columns), lambda k, r: (k, r, 0))
-    scale = pl.BlockSpec((1, tile // 16, columns), lambda k, r: (k, r, 0))
-    specs = [big, big, scale, big, scale]
-    cut = lambda ref: ref.at[:, :, pl.ds(c0, columns)]
-    pltpu.emit_pipeline(work, grid=(2, rows // tile), in_specs=specs, out_specs=specs)(
-        *[cut(ref) for ref in sources], *[cut(ref) for ref in targets]
-    )
-
-
-def weight_step(chain, parts, weight, first, first_scale, second, second_scale, outs, c0, columns, total_tokens):
+        for copy in copies(i, True):
+            copy.start()
+        return carry
+
+    lax.fori_loop(0, 2 * tiles, work, 0)
+
+    def end(i, carry):
+        for copy in copies(i, True):
+            copy.wait()
+        return carry
+
+    for k in range(2):
+        first_tops[:, k] = jnp.transpose(top_table[k])[: columns // 128]
+        second_tops[:, k] = jnp.transpose(top_table[2 + k])[: columns // 128]
+    lax.fori_loop(0, 2 * tiles, end, 0)
+
+
+def weight_step(chain, vmem, parts, weight, first, first_scale, second, second_scale, outs, c0, columns, total_tokens):
     rows = weight.shape[1]
     tile = min(512, rows)
     n = len(parts)
     operands = [t for t, _, _ in parts] + [g for _, g, _ in parts] + [weight, first, first_scale, second, second_scale]
-    specs = [in_vmem] * (2 * n) + [in_hbm] * 5
+    specs = [in_vmem] * (2 * n) + [in_hbm, in_hbm, in_vmem, in_hbm, in_vmem]
     aliases = {}
     if outs is not None:
-        aliases = {len(operands) + i: i for i in range(5)}
-        specs += [in_hbm] * 5
+        aliases = {len(operands) + i: i for i in range(3)}
+        specs += [in_hbm] * 3
         operands += list(outs)
     elements = 2 * rows * columns
-    kernel = functools.partial(weight_kernel, n, (total_tokens, [(at, 0) for _, _, at in parts]), c0, columns, tile)
+    kernel = functools.partial(weight_kernel, n, total_tokens, [at for _, _, at in parts], c0, columns, tile)
     return chain.call(
         kernel,
         specs,
         operands,
-        [in_hbm] * 5,
-        [jax.ShapeDtypeStruct(v.shape, v.dtype) for v in (weight, first, first_scale, second, second_scale)],
+        [in_hbm] * 3 + [in_vmem] * 2,
+        [jax.ShapeDtypeStruct(weight.shape, bf16)] * 3
+        + [jax.ShapeDtypeStruct((columns // 128, 2, rows // 16), f32)] * 2,
         "weight_step",
-        20,
+        vmem,
         2 * elements * sum(t.shape[0] for t, _, _ in parts) + 40 * elements,
         12 * elements,
-        scratch=[pltpu.VMEM((tile, columns), f32)],
+        scratch=[
+            pltpu.VMEM((4, rows // 16, 128), f32),
+            pltpu.VMEM((tile, columns), f32),
+            pltpu.VMEM((columns // 64, 64, 128), f32),
+            pltpu.VMEM((3, 2, rows, columns), bf16),
+            pltpu.VMEM((3, 2, rows, columns), bf16),
+            pltpu.SemaphoreType.DMA((3, 2 * rows // tile)),
+            pltpu.SemaphoreType.DMA((3, 2 * rows // tile)),
+        ],
         aliases=aliases,
     )
 
@@ -175,7 +280,7 @@
     pltpu.emit_pipeline(work, grid=(2, count), in_specs=[spec])(weight_ref.at[:, :, pl.ds(c0 * width, count * width)])
 
 
-def partial_pre(chain, tokens, weight, c0, c1, width):
+def partial_pre(chain, tokens, weight, c0, c1, width, vmem):
     rows, depth = tokens.shape
     n = rows // 4
     count = c1 - c0
@@ -186,40 +291,42 @@
         [in_vmem, in_vmem],
         [jax.ShapeDtypeStruct((2, count * n, width), bf16), jax.ShapeDtypeStruct((3, 2, count * n, width), f32)],
         "partial_pre",
-        8,
+        vmem,
         4 * rows * depth * count * width,
         4 * depth * count * width,
     )
 
 
-def hidden_kernel(c0, count, width, grad_ref, down_ref, out_ref):
-    n, depth = grad_ref.shape
+def hidden_kernel(width, spans, grad_ref, down_ref, *outs):
+    depth = grad_ref.shape[1]
 
     def work(block):
         c = pl.program_id(0)
-        out_ref[pl.ds(pl.multiple_of(c * n, n), n)] = lax.dot_general(
-            grad_ref[...], block[...], (((1,), (1,)), ((), ())), preferred_element_type=f32
-        )
+        value = lax.dot_general(grad_ref[...], block[...], (((1,), (1,)), ((), ())), preferred_element_type=f32)
+        for (r0, r1, c0, c1), out in zip(spans, outs):
+            n = r1 - r0
+
+            @pl.when((c >= c0) & (c < c1))
+            def _():
+                out[pl.ds(pl.multiple_of((c - c0) * n, n), n)] = value[r0:r1]
 
     spec = pl.BlockSpec((width, depth), lambda c: (c, 0))
-    pltpu.emit_pipeline(work, grid=(count,), in_specs=[spec])(down_ref.at[pl.ds(c0 * width, count * width)])
-
-
-def hidden_grad(chain, cot, down, c0, c1, width):
+    pltpu.emit_pipeline(work, grid=(down_ref.shape[0] // width,), in_specs=[spec])(down_ref)
+
+
+def hidden_grad(chain, cot, down, width, spans):
     rows, depth = cot.shape
-    count = c1 - c0
-    (out,) = chain.call(
-        functools.partial(hidden_kernel, c0, count, width),
+    return chain.call(
+        functools.partial(hidden_kernel, width, spans),
         [in_vmem, in_hbm],
         [cot, down],
-        [in_vmem],
-        [jax.ShapeDtypeStruct((count * rows, width), f32)],
+        [in_vmem] * len(spans),
+        [jax.ShapeDtypeStruct(((r1 - r0) * (c1 - c0), width), f32) for r0, r1, c0, c1 in spans],
         "hidden_grad",
-        8,
-        2 * rows * depth * count * width,
-        2 * depth * count * width,
+        46,
+        2 * rows * depth * down.shape[0],
+        2 * depth * down.shape[0],
     )
-    return out
 
 
 def step_kernel(has, offsets, *refs):
@@ -358,30 +465,36 @@
     orders = [list(range(bits)), list(reversed(range(bits)))]
     every = tuple(range(chips))
     rest = every[1:]
-    staged = groups == 4 and chips == 4 and chunks >= 4
-
-    blocks = tokens.reshape(own, groups, rows)
-    slots = []
-    for s in range(groups):
-        block = lax.dynamic_index_in_dim(blocks, me ^ s, 1, keepdims=False)
-        slots.append(swap(block, s) if s else block)
+    staged = groups == 4 and chips == 4
+
+    blocks = split_columns(tokens, groups, me)
+    slots = [swap(block, s) if s else block for s, block in enumerate(blocks)]
     block = jnp.stack(slots)
-    def around(value, axis):
-        moved, found = value, []
-        for _ in rest:
-            moved = ring(moved)
-            found.append(moved)
-        result = [jnp.concatenate([value, pair(value)], axis=axis)]
-        if found:
-            other = pair(jnp.stack(found))
-            result += [jnp.concatenate([v, other[at]], axis=axis) for at, v in enumerate(found)]
-        return result
-
-    token_blocks = around(block, 1)
-    grad_blocks = around(cotangent, 0)
+
+    def near(value, axis):
+        return pack([(v, 0, v.shape[axis]) for v in (value, pair(value))], axis)
+
+    def send_on(value):
+        return [onward(value, k) for k in rest]
+
+    def far(found, axis, *others):
+        n = found[0].shape[axis]
+        other = pair(pack([(v, 0, n) for v in found], axis, *others))
+        pieces = []
+        for at, v in enumerate(found):
+            pieces += [(v, 0, n), (other, at * n, at * n + n)]
+        return pack(pieces, axis)
+
+    packed = {((0,), 0): near(block, 1)}
+    sent = send_on(block)
+    held = hold_until(cotangent, block)
+    packed[(0,), 1] = near(held, 0)
+    if not staged and rest:
+        packed[rest, 0] = far(sent, 1)
+        packed[rest, 1] = far(send_on(held), 0)
 
     if staged:
-        last = chunks - max(1, (chunks * 2) // 7)
+        last = chunks - max(1, (chunks * 3) // 7)
         plan = {0: ((0,), 0, last)}
         at = 4
         for c in range(0, last, 2):
@@ -392,18 +505,18 @@
     else:
         plan = {c: (every, c, c + 1) for c in range(chunks)}
 
-    cache = {}
-
     def rows_of(ks):
-        if ks not in cache:
-            t = jnp.concatenate([token_blocks[k] for k in ks], axis=1)
-            c = jnp.concatenate([grad_blocks[k] for k in ks], axis=0)
-            cache[ks] = (t, c, t.reshape(-1, rows))
-        return cache[ks]
+        for kind in range(2):
+            if (ks, kind) not in packed and (rest, kind) in packed:
+                pieces = []
+                for k in ks:
+                    n = 2 * own
+                    pieces.append((packed[(0,), kind], 0, n) if k == 0 else (packed[rest, kind], (k - 1) * n, k * n))
+                packed[ks, kind] = pack(pieces, 1 - kind)
+        t = packed[ks, 0]
+        return (t, packed.get((ks, 1)), t.reshape(-1, rows))
 
     expand = lambda scale: jnp.repeat(scale, 128, axis=2)
-    first_wide = expand(first_scale)
-    second_wide = expand(second_scale)
 
     def forward(ks, c0, c1):
         t, c, _ = rows_of(ks)
@@ -468,20 +581,60 @@
         value = sums[ks].reshape(groups, len(ks), 2, own, rows)
         return {k: value[:, at] for at, k in enumerate(ks)}
 
+    def across(partial, ks):
+        theirs = pair(jnp.stack([partial[k][:, 1] for k in ks]).astype(bf16))
+        mine = [partial[k][:, 0] + theirs[at].astype(f32) for at, k in enumerate(ks)]
+        return [back(v.astype(bf16), k).astype(f32) if k else v for k, v in zip(ks, mine)]
+
+    def partials():
+        partial = {}
+        for ks in sums:
+            for k, part in split(ks).items():
+                partial[k] = partial[k] + part if k in partial else part
+        return partial
+
     grads = {}
     if staged:
         chain = Chain()
         lag = 2
         exchange = Exchange(chain, plan, lag, own, width)
         steps = [m for m in range(max(plan) + 3 * lag + 1) if exchange.stages(m)]
-        sources = (gate_up, first_code, first_wide, second_code, second_wide)
-        result = [None]
+        result, tops = [None], {}
+
+        def input_grad_start():
+            partial = partials()
+            halves = [every[1:3], (every[3], 0)]
+            arrived = [across(partial, ks) for ks in halves]
+
+            def wait():
+                total = sum(arrived[1][::-1] + arrived[0], jnp.zeros((groups, own, rows), f32))
+                moved.append(total.astype(bf16))
+                chain.add(moved[0])
+
+            return wait
+
+        moved = []
 
         def start(u):
-            exchange.sends[u], exchange.keeps[u] = partial_pre(chain, rows_of(plan[u][0])[2], gate_up, *plan[u][1:], width)
-
-        def hidden(u):
-            exchange.hidden[u] = hidden_grad(chain, rows_of(plan[u][0])[1], down_weight, *plan[u][1:], width)
+            exchange.sends[u], exchange.keeps[u] = partial_pre(
+                chain, rows_of(plan[u][0])[2], gate_up, *plan[u][1:], width, 8 if u else 56
+            )
+
+        def hidden_first():
+            return hidden_grad(chain, rows_of((0,))[1], down_weight, width, [(0, 2 * own, 0, last), (0, 2 * own, last, chunks)])
+
+        def hidden_rest(first, tail):
+            n = 2 * own
+            cuts = [(0, 3 * n, c0, c1) for ks, c0, c1 in plan.values() if ks == rest]
+            cuts += [(0, 2 * n, last, chunks), (2 * n, 3 * n, last, chunks)]
+            found = hidden_grad(chain, rows_of(rest)[1], down_weight, width, cuts)
+            exchange.hidden[0] = first
+            units_of_rest = [u for u in plan if plan[u][0] == rest]
+            for u, value in zip(units_of_rest, found):
+                exchange.hidden[u] = value
+            exchange.hidden[max(plan) - 1] = found[-2]
+            both = jnp.stack([found[-1].reshape(chunks - last, n, width), tail.reshape(chunks - last, n, width)], axis=1)
+            exchange.hidden[max(plan)] = both.reshape(-1, width)
 
         def finish(u):
             grads[u] = exchange.gather(u)
@@ -489,75 +642,71 @@
         def inputs(u):
             chain.add(add_input_grad(u, grads[u]))
 
-        def update(c0, c1):
+        def update(c0, c1, vmem):
             parts = []
             for u, (ks, a, b) in plan.items():
                 if a <= c0 and c1 <= b:
                     parts.append((rows_of(ks)[2], grads[u], (c0 - a) * width))
-            result[0] = weight_step(
-                chain, parts, *sources, result[0], c0 * width, (c1 - c0) * width, total_tokens
+            *result[0], tops[c0, 0], tops[c0, 1] = weight_step(
+                chain, vmem, parts, gate_up, first_code, first_wide, second_code, second_wide, result[0], c0 * width, (c1 - c0) * width, total_tokens
             )
 
-        hidden(0)
         start(0)
         spans = [p[1:] for p in plan.values() if p[0] == rest]
-        updated_spans = []
+        pending = []
         for place, m in enumerate(steps):
             exchange.step(m)
-            if place + 1 < len(steps):
-                after = steps[place + 1]
-                if after in plan:
-                    start(after)
-                if after - 2 * lag in plan and after != 2 * lag:
-                    hidden(after - 2 * lag)
-            if m - 4 * lag in plan:
-                finish(m - 4 * lag)
-                inputs(m - 4 * lag)
-                if plan[m - 4 * lag][1:] in spans[:1]:
-                    update(*spans[0])
-        left = [u for u in plan if u not in grads]
-        for u in left:
-            finish(u)
-            inputs(u)
-            if u == left[-2]:
-                for span in spans[1:-1]:
-                    update(*span)
-        for span in spans[max(1, len(spans) - 1) :]:
-            update(*span)
-        update(last, chunks)
+            if m == 0:
+                exchange.hidden[0], hidden_tail = hidden_first()
+            if m == lag:
+                packed[rest, 0] = far(sent, 1, chain.tokens[0])
+                cot_sent = send_on(hold_until(cotangent, packed[rest, 0]))
+            if place + 1 < len(steps) and steps[place + 1] in plan:
+                start(steps[place + 1])
+            if m == 3 * lag:
+                packed[rest, 1] = far(cot_sent, 0, chain.tokens[0])
+                hidden_rest(exchange.hidden[0], hidden_tail)
+            if m == 4 * lag:
+                first_wide = expand(hold_until(first_scale, chain.tokens[0]))
+                second_wide = expand(hold_until(second_scale, chain.tokens[0]))
+                chain.add(first_wide)
+                chain.add(second_wide)
+            done = m - 4 * lag
+            if done in plan:
+                finish(done)
+                inputs(done)
+                if plan[done][0] == rest:
+                    pending.append(plan[done][1:])
+            if pending and place + 1 < len(steps):
+                update(*pending.pop(0), 20)
+        for u in plan:
+            if u not in grads:
+                finish(u)
+                inputs(u)
+        wait = input_grad_start()
+        for span in pending:
+            update(*span, 20)
+        wait()
+        update(last, chunks, 44)
         outs = result[0]
+        moved = moved[0]
     else:
         for u, unit in plan.items():
             grads[u] = forward(*unit)
             add_input_grad(u, grads[u])
-
-    partial = [None] * chips
-    for ks in sums:
-        for k, part in split(ks).items():
-            partial[k] = part if partial[k] is None else partial[k] + part
-    order = rest + (0,)
-    mine = {}
-    for at in range(0, chips, 2):
-        ks = order[at : at + 2]
-        theirs = pair(jnp.stack([partial[k][:, 1] for k in ks]).astype(bf16))
-        for spot, k in enumerate(ks):
-            mine[k] = partial[k][:, 0] + theirs[spot].astype(f32)
-    moving = None
-    for k in order:
-        value = mine[k]
-        if moving is not None:
-            value = value + ring(moving).astype(f32)
-        moving = value.astype(bf16)
-    final = [moving[0]] + [swap(moving[s], s) for s in range(1, groups)]
-    final = jnp.stack(final)
+        moved = sum(across(partials(), every), jnp.zeros((groups, own, rows), f32)).astype(bf16)
+
+    final = jnp.stack([moved[0]] + [swap(moved[s], s) for s in range(1, groups)])
     final = jnp.stack([lax.dynamic_index_in_dim(final, me ^ a, 0, keepdims=False) for a in range(groups)], axis=1)
     input_grad = final.reshape(own, depth)
 
     if not staged:
-        chain, outs = Chain(), None
+        first_wide, second_wide = expand(first_scale), expand(second_scale)
+        chain, outs, tops = Chain(), None, {}
         for c, (ks, c0, c1) in plan.items():
-            outs = weight_step(
+            *outs, tops[c0, 0], tops[c0, 1] = weight_step(
                 chain,
+                20,
                 [(rows_of(ks)[2], grads[c], 0)],
                 gate_up,
                 first_code,
@@ -569,8 +718,10 @@
                 (c1 - c0) * width,
                 total_tokens,
             )
-    updated, code_one, scale_one, code_two, scale_two = outs
-    return (input_grad, updated, code_one, scale_one[:, :, ::128], code_two, scale_two[:, :, ::128])
+    updated, code_one, code_two = outs
+    scales = [jnp.concatenate([tops[c, i] for c, j in sorted(tops) if i == j], axis=0) for i in range(2)]
+    scales = [jnp.transpose(scale, (1, 2, 0)) for scale in scales]
+    return (input_grad, updated, code_one, scales[0], code_two, scales[1])
 
 
 def solution(mesh):

time: 264 us -> 245 us (0.928)
  waiting for transfers between devices: 86.8 us -> 50.6 us
  starting transfers between devices: 41.3 us -> 52.6 us
  Pallas kernels: 79.2 us -> 84.8 us
    ppermute x9, waiting for transfers between devices: 26.2 us -> 3.23 us  [back(): lax.ppermute(value, 'tensor', [(p, (p - 2 * distance) % size) for p in ra...]
    ppermute x32 -> x30, waiting for transfers between devices: 59.4 us -> 47.1 us  [swap(): lax.ppermute(value, 'dp', [(p, p ^ mask) for p in range(lax.axis_size('dp...]
    ppermute x9, starting transfers between devices: 8.59 us -> 17.3 us  [back(): lax.ppermute(value, 'tensor', [(p, (p - 2 * distance) % size) for p in ra...]
    pallas_call x35 -> x27, Pallas kernels: 79.2 us -> 84.2 us  [call(): pl.pallas_call(body, in_specs=list(in_specs) + [anywhere] * held, out_spe...]
    concatenate x6 -> x0, other arithmetic: 3.47 us -> none  [the longest x2 2.07 us: rows_of(): c = jnp.concatenate([grad_blocks[k] for k in ks], axis=0)]
    slice x3 -> x1, local copies, waits for them, and re-layouts: 2.95 us -> 0.02 us  [shards(): moved[0]]
    convert_element_type x4 -> x3, other arithmetic: 0.36 us -> 3.26 us  [the longest x2 1.83 us: across(): v.astype(bf16)]
    dot_general x6 -> x5, matrix products: 8.79 us -> 11.3 us  [shards(): jnp.einsum('ktf,kdf->td', g, gate_up[:, :, c0 * width:c1 * width], prefer...]
  transfers between devices with their start and end apart: 47 -> 45, of which waited for: 20 -> 15; matrix products, arithmetic and copies ran while one was open for 10% -> 9% of each run, Pallas kernels for 29% -> 35%
where the time goes in v3:
time: 245 us; the launch traced here: 244 us
  Pallas kernels  84.8 us (35%)
  starting transfers between devices  52.6 us (21%)
  waiting for transfers between devices  50.6 us (21%)
  local copies, waits for them, and re-layouts  38.1 us (16%)
  matrix products  11.3 us (5%)
  other arithmetic  4.78 us (2%)
    pallas_call x27, Pallas kernels, call(): pl.pallas_call(body, in_specs=list(in_specs) + [anywhere] * held, out_spe...  84.2 us
    ppermute x30, waiting for transfers between devices, swap(): lax.ppermute(value, 'dp', [(p, p ^ mask) for p in range(lax.axis_size('dp...  47.1 us
    ppermute x30, starting transfers between devices, swap(): lax.ppermute(value, 'dp', [(p, p ^ mask) for p in range(lax.axis_size('dp...  34 us
    unnamed x138, local copies, waits for them, and re-layouts  31.1 us
    ppermute x9, starting transfers between devices, back(): lax.ppermute(value, 'tensor', [(p, (p - 2 * distance) % size) for p in ra...  17.3 us
    dot_general x5, matrix products, shards(): jnp.einsum('ktf,kdf->td', g, gate_up[:, :, c0 * width:c1 * width], prefer...  11.3 us
  transfers between devices with their start and end apart: 45, of which 15 were waited for; matrix products, arithmetic and copies ran while one was open for 9% of the time, Pallas kernels for 35%

profile of v3, /device:TPU:0, one launch (start us, length us, event | category | flops | bytes accessed | tf_op | source)
XLA Modules:
  0.0 244.0 jit_solution(18287964229570069022)
XLA Ops:
  1.6 4.0 %collective-permute-start.2 = (bf16[32,1024]{1,0:T(8,128)(2,1)S(1)}, bf16[32,1024]{1,0:T(8,128)(2,1)S(1)}, u32[]{:S(2)}, u32[]{:S(2)}) collective-permute-start(bf16[32,1024]{1,0:T(8,128)(2,1)S(1)} %get-tuple-element.104), channel_id=1, source_target_pairs={{0,24},{8,16},{16,8},{24,0},{1,25},{9,17},{17,9},{25,1},{2,26},{10... | collective-permute-start | bytes 196616 | tf_op jit(solution)/shard_map/ppermute | solution.py:20
  6.2 1.6 collective-permute-done.2
  7.8 2.0 collective-permute-done.1
  12.0 1.6 collective-permute-start.3
  13.6 2.6 %collective-permute-start.4 = (bf16[4,32,1024]{2,1,0:T(8,128)(2,1)S(1)}, bf16[4,32,1024]{2,1,0:T(8,128)(2,1)S(1)}, u32[]{:S(2)}, u32[]{:S(2)}) collective-permute-start(bf16[4,32,1024]{2,1,0:T(8,128)(2,1)S(1)} %pad_maximum_fusion.3.refs_0_), channel_id=1, source_target_pairs={{0,4},{1,5},{2,6},{3,7},{4,0},{5,1},{6,2},{7,3},{8,12},{9,13},{10,... | collective-permute-start | bytes 786440 | tf_op jit(solution)/shard_map/ppermute | solution.py:25
  16.2 1.3 collective-permute-start.5
  18.4 8.2 %partial_pre.5 = (bf16[2,256,256]{2,1,0:T(8,128)(2,1)}, f32[3,2,256,256]{3,2,1,0:T(8,128)}, f32[8,128]{1,0:T(8,128)}) custom-call(bf16[256,1024]{1,0:T(8,128)(2,1)} %bitcast.139, bf16[2,1024,1792]{2,1,0:T(8,128)(2,1)} %refs_4_.5), custom_call_target="tpu_custom_call" | custom-call | flops 1 | bytes 1 | tf_op jit(solution)/shard_map/partial_pre/pallas_call | solution.py:108
  28.8 1.5 collective-permute-start.8
  30.4 10.9 %hidden_grad.2 = (f32[256,256]{1,0:T(8,128)S(1)}, f32[192,256]{1,0:T(8,128)S(1)}, f32[8,128]{1,0:T(8,128)S(1)}) custom-call(bf16[64,4096]{1,0:T(8,128)(2,1)S(1)} %pack.9.refs_0_, bf16[1792,4096]{1,0:T(8,128)(2,1)} %refs_1_.13, f32[8,128]{1,0:T(8,128)S(1)} %get-tuple-element.110.refs_2_), custom_call_target="tpu_custom_call" | custom-call | flops 1 | bytes 1 | tf_op jit(solution)/shard_map/hidden_grad/pallas_call | solution.py:108
  41.6 1.6 collective-permute-start.11
  44.1 2.7 %partial_pre.6 = (bf16[2,384,256]{2,1,0:T(8,128)(2,1)S(1)}, f32[3,2,384,256]{3,2,1,0:T(8,128)S(1)}, f32[8,128]{1,0:T(8,128)S(1)}) custom-call(bf16[768,1024]{1,0:T(8,128)(2,1)S(1)} %bitcast.131, bf16[2,1024,1792]{2,1,0:T(8,128)(2,1)S(1)} %bitcast.128, f32[8,128]{1,0:T(8,128)S(1)} %get-tuple-element.112.refs_3_.refs_2_), custom_call_target="tpu_custom_call" | custom-call | flops 1 | bytes 1 | tf_op jit(solution)/shard_map/partial_pre/pallas_call | solution.py:108
  46.8 3.6 %collective-permute-done.11.refs_3_ = bf16[512,256]{1,0:T(8,128)(2,1)S(1)} collective-permute-done((bf16[512,256]{1,0:T(8,128)(2,1)S(1)}, bf16[512,256]{1,0:T(8,128)(2,1)S(1)}, u32[]{:S(2)}, u32[]{:S(2)}) %collective-permute-start.11) | collective-permute-done | bytes 262176 | tf_op jit(solution)/shard_map/ppermute | solution.py:20
  50.4 1.2 collective-permute-done.12.refs_4_
  54.0 2.8 %collective-permute-start.19 = (bf16[32,4096]{1,0:T(8,128)(2,1)S(1)}, bf16[32,4096]{1,0:T(8,128)(2,1)S(1)}, u32[]{:S(2)}, u32[]{:S(2)}) collective-permute-start(bf16[32,4096]{1,0:T(8,128)(2,1)S(1)} %hold.5), channel_id=1, source_target_pairs={{0,6},{1,7},{2,0},{3,1},{4,2},{5,3},{6,4},{7,5},{8,14},{9,15},{10,... | collective-permute-start | bytes 786440 | tf_op jit(solution)/shard_map/ppermute | solution.py:25
  57.0 2.7 %partial_pre.7 = (bf16[2,384,256]{2,1,0:T(8,128)(2,1)S(1)}, f32[3,2,384,256]{3,2,1,0:T(8,128)S(1)}, f32[8,128]{1,0:T(8,128)S(1)}) custom-call(bf16[768,1024]{1,0:T(8,128)(2,1)S(1)} %bitcast.132, bf16[2,1024,1792]{2,1,0:T(8,128)(2,1)S(1)} %bitcast.128, f32[8,128]{1,0:T(8,128)S(1)} %get-tuple-element.121.refs_2_), custom_call_target="tpu_custom_call" | custom-call | flops 1 | bytes 1 | tf_op jit(solution)/shard_map/partial_pre/pallas_call | solution.py:108
  59.7 1.4 copy-done.11
  61.2 3.2 %partial_pre.8 = (bf16[2,384,256]{2,1,0:T(8,128)(2,1)S(1)}, f32[3,2,384,256]{3,2,1,0:T(8,128)S(1)}, f32[8,128]{1,0:T(8,128)S(1)}) custom-call(bf16[512,1024]{1,0:T(8,128)(2,1)S(1)} %bitcast.145, bf16[2,1024,1792]{2,1,0:T(8,128)(2,1)S(1)} %bitcast.128, f32[8,128]{1,0:T(8,128)S(1)} %get-tuple-element.124.refs_2_), custom_call_target="tpu_custom_call" | custom-call | flops 1 | bytes 1 | tf_op jit(solution)/shard_map/partial_pre/pallas_call | solution.py:108
  65.4 3.2 %partial_pre.9 = (bf16[2,384,256]{2,1,0:T(8,128)(2,1)S(1)}, f32[3,2,384,256]{3,2,1,0:T(8,128)S(1)}, f32[8,128]{1,0:T(8,128)S(1)}) custom-call(bf16[512,1024]{1,0:T(8,128)(2,1)S(1)} %bitcast.143, bf16[2,1024,1792]{2,1,0:T(8,128)(2,1)S(1)} %bitcast.128, f32[8,128]{1,0:T(8,128)S(1)} %get-tuple-element.131.refs_2_), custom_call_target="tpu_custom_call" | custom-call | flops 1 | bytes 1 | tf_op jit(solution)/shard_map/partial_pre/pallas_call | solution.py:108
  68.7 1.4 copy-done.9
  70.1 3.2 %collective-permute-done.18.refs_1_.refs_2_ = bf16[32,4096]{1,0:T(8,128)(2,1)S(1)} collective-permute-done((bf16[32,4096]{1,0:T(8,128)(2,1)S(1)}, bf16[32,4096]{1,0:T(8,128)(2,1)S(1)}, u32[]{:S(2)}, u32[]{:S(2)}) %collective-permute-start.18) | collective-permute-done | bytes 262176 | tf_op jit(solution)/shard_map/ppermute | solution.py:25
  73.4 1.5 collective-permute-start.15
  74.9 1.5 collective-permute-start.16
  77.7 10.1 %hidden_grad.3 = (f32[384,256]{1,0:T(8,128)S(1)}, f32[384,256]{1,0:T(8,128)S(1)}, f32[384,256]{1,0:T(8,128)S(1)}, f32[192,256]{1,0:T(8,128)S(1)}, f32[8,128]{1,0:T(8,128)S(1)}) custom-call(bf16[192,4096]{1,0:T(8,128)(2,1)S(1)} %pack.15.refs_0_, bf16[1792,4096]{1,0:T(8,128)(2,1)} %refs_1_.13, f32[8,128]{1,0:T(8,128)S(1)} %get-tuple-element.132.refs_3_.refs_2_), custom_call_target="tpu_custom_call" | custom-call | flops 1 | bytes 1 | tf_op jit(solution)/shard_map/hidden_grad/pallas_call | solution.py:108
  87.8 8.4 %collective-permute-done.21.refs_2_ = bf16[384,256]{1,0:T(8,128)(2,1)S(1)} collective-permute-done((bf16[384,256]{1,0:T(8,128)(2,1)S(1)}, bf16[384,256]{1,0:T(8,128)(2,1)S(1)}, u32[]{:S(2)}, u32[]{:S(2)}) %collective-permute-start.21) | collective-permute-done | bytes 196640 | tf_op jit(solution)/shard_map/ppermute | solution.py:20
  96.2 1.1 collective-permute-done.22.refs_3_
  97.3 1.1 exchange_step.17
  99.1 1.5 collective-permute-start.24
  100.7 1.6 exchange_step.18
  103.1 1.4 collective-permute-start.27
  105.3 1.3 broadcast_in_dim.6
  106.6 1.4 reshape.75.refs_6_
  108.0 1.3 broadcast_in_dim.7
  109.3 1.4 reshape.76.refs_7_.refs_8_
  116.1 4.0 %fusion = f32[256,1024,1]{1,0,2:T(8,128)S(1)} fusion(bf16[2,256,1024]{2,1,0:T(8,128)(2,1)S(1)} %get-tuple-element.141.refs_2_, bf16[2,1024,1792]{2,1,0:T(8,128)(2,1)} %refs_4_.5), kind=kOutput, calls=%fused_computation | convolution fusion | flops 1073741824 | bytes 6291456 | tf_op jit(solution)/shard_map/ktf,kdf->td/dot_general | solution.py:569
  120.2 2.2 exchange_step.19
  123.0 1.5 collective-permute-start.26
  124.6 7.4 %collective-permute-done.27.refs_2_.refs_4_.refs_1_ = bf16[1536,256]{1,0:T(8,128)(2,1)} collective-permute-done((bf16[1536,256]{1,0:T(8,128)(2,1)}, bf16[1536,256]{1,0:T(8,128)(2,1)}, u32[]{:S(2)}, u32[]{:S(2)}) %collective-permute-start.27) | collective-permute-done | bytes 786464 | tf_op jit(solution)/shard_map/ppermute | solution.py:20
  132.5 2.3 exchange_step.20
  134.8 1.5 collective-permute-start.31
  136.3 1.5 collective-permute-start.32
  137.9 10.8 %collective-permute-done.25.refs_2_.refs_4_.refs_1_ = bf16[1536,256]{1,0:T(8,128)(2,1)S(1)} collective-permute-done((bf16[1536,256]{1,0:T(8,128)(2,1)S(1)}, bf16[1536,256]{1,0:T(8,128)(2,1)S(1)}, u32[]{:S(2)}, u32[]{:S(2)}) %collective-permute-start.25) | collective-permute-done | bytes 786464 | tf_op jit(solution)/shard_map/ppermute | solution.py:20
  149.6 1.5 collective-permute-start.29
  151.1 1.5 collective-permute-start.30
  152.6 8.7 %collective-permute-done.31.refs_0_.refs_3_.refs_1_ = bf16[1152,256]{1,0:T(8,128)(2,1)S(1)} collective-permute-done((bf16[1152,256]{1,0:T(8,128)(2,1)S(1)}, bf16[1152,256]{1,0:T(8,128)(2,1)S(1)}, u32[]{:S(2)}, u32[]{:S(2)}) %collective-permute-start.31) | collective-permute-done | bytes 589856 | tf_op jit(solution)/shard_map/ppermute | solution.py:20
  161.9 1.5 collective-permute-start.35
  163.4 1.5 collective-permute-start.36
  164.9 1.6 pre_grad.6
  166.7 1.8 fusion.10.refs_10_
  169.7 9.8 %weight_step.3 = (bf16[2,1024,1792]{2,1,0:T(8,128)(2,1)}, bf16[2,1024,1792]{2,1,0:T(8,128)(2,1)}, bf16[2,1024,1792]{2,1,0:T(8,128)(2,1)}, f32[4,2,64]{2,1,0:T(2,...) custom-call(bf16[256,1024]{1,0:T(8,128)(2,1)S(1)} %bitcast.140, bf16[768,1024]{1,0:T(8,128)(2,1)S(1)} %bitcast.133, ...), custom_call_target="tpu_custom_call" | custom-call | flops 1 | bytes 1 | tf_op jit(solution)/shard_map/weight_step/pallas_call | solution.py:108
  180.9 1.9 bitcast_add_fusion.refs_6_
  182.9 1.8 fusion.4
  186.0 1.8 fusion.2
  191.0 4.5 %collective-permute-start.41 = (bf16[4,32,1024]{2,1,0:T(8,128)(2,1)}, bf16[4,32,1024]{2,1,0:T(8,128)(2,1)}, u32[]{:S(2)}, u32[]{:S(2)}) collective-permute-start(bf16[4,32,1024]{2,1,0:T(8,128)(2,1)} %get-tuple-element.204), channel_id=1, source_target_pairs={{0,4},{1,5},{2,6},{3,7},{4,0},{5,1},{6,2},{7,3},{8,12},{9,13},{10,... | collective-permute-start | bytes 786440 | tf_op jit(solution)/shard_map/ppermute | solution.py:25
  195.5 3.4 %collective-permute-start.40 = (bf16[4,32,1024]{2,1,0:T(8,128)(2,1)}, bf16[4,32,1024]{2,1,0:T(8,128)(2,1)}, u32[]{:S(2)}, u32[]{:S(2)}) collective-permute-start(bf16[4,32,1024]{2,1,0:T(8,128)(2,1)} %get-tuple-element.203), channel_id=1, source_target_pairs={{0,6},{1,7},{2,0},{3,1},{4,2},{5,3},{6,4},{7,5},{8,14},{9,15},{10,... | collective-permute-start | bytes 786440 | tf_op jit(solution)/shard_map/ppermute | solution.py:25
  199.8 3.1 %copy-done = bf16[2,1024,1792]{2,1,0:T(8,128)(2,1)S(1)} copy-done((bf16[2,1024,1792]{2,1,0:T(8,128)(2,1)S(1)}, bf16[2,1024,1792]{2,1,0:T(8,128)(2,1)}, u32[]{:S(2)}) %copy-start) | copy-done | bytes 7340056
  202.8 3.1 %copy-done.1 = bf16[2,1024,1792]{2,1,0:T(8,128)(2,1)S(1)} copy-done((bf16[2,1024,1792]{2,1,0:T(8,128)(2,1)S(1)}, bf16[2,1024,1792]{2,1,0:T(8,128)(2,1)}, u32[]{:S(2)}) %copy-start.1) | copy-done | bytes 7340056
  205.9 3.1 %copy-done.2 = bf16[2,1024,1792]{2,1,0:T(8,128)(2,1)S(1)} copy-done((bf16[2,1024,1792]{2,1,0:T(8,128)(2,1)S(1)}, bf16[2,1024,1792]{2,1,0:T(8,128)(2,1)}, u32[]{:S(2)}) %copy-start.2) | copy-done | bytes 7340056
  210.1 1.6 copy-done.19
  211.6 1.2 copy-done.26
  212.9 1.4 copy-done.36
  214.3 9.8 %weight_step.4 = (bf16[2,1024,1792]{2,1,0:T(8,128)(2,1)}, bf16[2,1024,1792]{2,1,0:T(8,128)(2,1)}, bf16[2,1024,1792]{2,1,0:T(8,128)(2,1)}, f32[4,2,64]{2,1,0:T(2,...) custom-call(bf16[256,1024]{1,0:T(8,128)(2,1)S(1)} %bitcast.141, ...), custom_call_target="tpu_custom_call", output_to_operand_aliasing={{0}: (9, {}), {1}: (10, {}), {2}: (11, {})} | custom-call | flops 1 | bytes 1 | tf_op jit(solution)/shard_map/weight_step/pallas_call | solution.py:108
  224.2 1.4 fusion.29.refs_13_
  225.6 2.4 collective-permute-start.44
  229.2 13.3 %weight_step.5 = (bf16[2,1024,1792]{2,1,0:T(8,128)(2,1)}, bf16[2,1024,1792]{2,1,0:T(8,128)(2,1)}, bf16[2,1024,1792]{2,1,0:T(8,128)(2,1)}, f32[6,2,64]{2,1,0:T(2,...) custom-call(bf16[512,1024]{1,0:T(8,128)(2,1)S(1)} %bitcast.146, ...), custom_call_target="tpu_custom_call", output_to_operand_aliasing={{0}: (9, {}), {1}: (10, {}), {2}: (11, {})} | custom-call | flops 1 | bytes 1 | tf_op jit(solution)/shard_map/weight_step/pallas_call | solution.py:108
  (241 shorter events, 34.8 us)
Async XLA Ops:
  1.6 6.2 %collective-permute-start.2 = (bf16[32,1024]{1,0:T(8,128)(2,1)S(1)}, bf16[32,1024]{1,0:T(8,128)(2,1)S(1)}, u32[]{:S(2)}, u32[]{:S(2)}) collective-permute-start(bf16[32,1024]{1,0:T(8,128)(2,1)S(1)} %get-tuple-element.104), channel_id=1, source_target_pairs={{0,24},{8,16},{16,8},{24,0},{1,25},{9,17},{17,9},{25,1},{2,26},{10... | collective-permute-start | bytes 196616 | tf_op jit(solution)/shard_map/ppermute | solution.py:20
  5.6 4.3 %collective-permute-start.1 = (bf16[32,1024]{1,0:T(8,128)(2,1)S(1)}, bf16[32,1024]{1,0:T(8,128)(2,1)S(1)}, u32[]{:S(2)}, u32[]{:S(2)}) collective-permute-start(bf16[32,1024]{1,0:T(8,128)(2,1)S(1)} %get-tuple-element.103), channel_id=1, source_target_pairs={{0,16},{8,24},{16,0},{24,8},{1,17},{9,25},{17,1},{25,9},{2,18},{10... | collective-permute-start | bytes 196616 | tf_op jit(solution)/shard_map/ppermute | solution.py:20
  6.1 4.3 %collective-permute-start = (bf16[32,1024]{1,0:T(8,128)(2,1)S(1)}, bf16[32,1024]{1,0:T(8,128)(2,1)S(1)}, u32[]{:S(2)}, u32[]{:S(2)}) collective-permute-start(bf16[32,1024]{1,0:T(8,128)(2,1)S(1)} %get-tuple-element.102), channel_id=1, source_target_pairs={{0,8},{8,0},{16,24},{24,16},{1,9},{9,1},{17,25},{25,17},{2,10},{10... | collective-permute-start | bytes 196616 | tf_op jit(solution)/shard_map/ppermute | solution.py:20
  10.4 7.1 %collective-permute-start.6 = (bf16[4,32,1024]{2,1,0:T(8,128)(2,1)S(1)}, bf16[4,32,1024]{2,1,0:T(8,128)(2,1)S(1)}, u32[]{:S(2)}, u32[]{:S(2)}) collective-permute-start(bf16[4,32,1024]{2,1,0:T(8,128)(2,1)S(1)} %pad_maximum_fusion.3.refs_0_), channel_id=1, source_target_pairs={{0,1},{1,0},{2,3},{3,2},{4,5},{5,4},{6,7},{7,6},{8,9},{9,8},{10,11... | collective-permute-start | bytes 786440 | tf_op jit(solution)/shard_map/ppermute | solution.py:33
  11.4 17.4 %collective-permute-start.9 = (bf16[32,4096]{1,0:T(8,128)(2,1)S(1)}, bf16[32,4096]{1,0:T(8,128)(2,1)S(1)}, u32[]{:S(2)}, u32[]{:S(2)}) collective-permute-start(bf16[32,4096]{1,0:T(8,128)(2,1)S(1)} %hold.4.refs_0_), channel_id=1, source_target_pairs={{0,1},{1,0},{2,3},{3,2},{4,5},{5,4},{6,7},{7,6},{8,9},{9,8},{10,11... | collective-permute-start | bytes 786440 | tf_op jit(solution)/shard_map/ppermute | solution.py:33
  12.0 29.5 %collective-permute-start.3 = (bf16[4,32,1024]{2,1,0:T(8,128)(2,1)S(1)}, bf16[4,32,1024]{2,1,0:T(8,128)(2,1)S(1)}, u32[]{:S(2)}, u32[]{:S(2)}) collective-permute-start(bf16[4,32,1024]{2,1,0:T(8,128)(2,1)S(1)} %pad_maximum_fusion.3.refs_0_), channel_id=1, source_target_pairs={{0,2},{1,3},{2,4},{3,5},{4,6},{5,7},{6,0},{7,1},{8,10},{9,11},{10,... | collective-permute-start | bytes 786440 | tf_op jit(solution)/shard_map/ppermute | solution.py:25
  13.6 27.9 %collective-permute-start.4 = (bf16[4,32,1024]{2,1,0:T(8,128)(2,1)S(1)}, bf16[4,32,1024]{2,1,0:T(8,128)(2,1)S(1)}, u32[]{:S(2)}, u32[]{:S(2)}) collective-permute-start(bf16[4,32,1024]{2,1,0:T(8,128)(2,1)S(1)} %pad_maximum_fusion.3.refs_0_), channel_id=1, source_target_pairs={{0,4},{1,5},{2,6},{3,7},{4,0},{5,1},{6,2},{7,3},{8,12},{9,13},{10,... | collective-permute-start | bytes 786440 | tf_op jit(solution)/shard_map/ppermute | solution.py:25
  16.2 25.3 %collective-permute-start.5 = (bf16[4,32,1024]{2,1,0:T(8,128)(2,1)S(1)}, bf16[4,32,1024]{2,1,0:T(8,128)(2,1)S(1)}, u32[]{:S(2)}, u32[]{:S(2)}) collective-permute-start(bf16[4,32,1024]{2,1,0:T(8,128)(2,1)S(1)} %pad_maximum_fusion.3.refs_0_), channel_id=1, source_target_pairs={{0,6},{1,7},{2,0},{3,1},{4,2},{5,3},{6,4},{7,5},{8,14},{9,15},{10,... | collective-permute-start | bytes 786440 | tf_op jit(solution)/shard_map/ppermute | solution.py:25
  28.2 13.1 %collective-permute-start.7 = (bf16[256,256]{1,0:T(8,128)(2,1)S(1)}, bf16[256,256]{1,0:T(8,128)(2,1)S(1)}, u32[]{:S(2)}, u32[]{:S(2)}) collective-permute-start(bf16[256,256]{1,0:T(8,128)(2,1)S(1)} %get-tuple-element.108), channel_id=1, source_target_pairs={{0,8},{8,0},{16,24},{24,16},{1,9},{9,1},{17,25},{25,17},{2,10},{10... | collective-permute-start | bytes 393224 | tf_op jit(solution)/shard_map/ppermute | solution.py:20
  28.8 12.5 %collective-permute-start.8 = (bf16[256,256]{1,0:T(8,128)(2,1)S(1)}, bf16[256,256]{1,0:T(8,128)(2,1)S(1)}, u32[]{:S(2)}, u32[]{:S(2)}) collective-permute-start(bf16[256,256]{1,0:T(8,128)(2,1)S(1)} %get-tuple-element.109), channel_id=1, source_target_pairs={{0,16},{8,24},{16,0},{24,8},{1,17},{9,25},{17,1},{25,9},{2,18},{10... | collective-permute-start | bytes 393224 | tf_op jit(solution)/shard_map/ppermute | solution.py:20
  30.4 13.7 %slice-start = ((s8[7340032]{0:T(1024)(128)(4,1)}), s8[4194304]{0:T(1024)(128)(4,1)S(1)}, s32[]{:S(2)}) async-start(s8[7340032]{0:T(1024)(128)(4,1)} %bitcast.127), calls=%async_computation | async-start | bytes 8388608
  30.4 13.6 %slice-start.1 = ((s8[7340032]{0:T(1024)(128)(4,1)}), s8[3145728]{0:T(1024)(128)(4,1)S(1)}, s32[]{:S(2)}) async-start(s8[7340032]{0:T(1024)(128)(4,1)} %bitcast.127), calls=%async_computation.1 | async-start | bytes 6291456
  41.6 2.4 collective-permute-start.10
  41.6 8.7 %collective-permute-start.11 = (bf16[512,256]{1,0:T(8,128)(2,1)S(1)}, bf16[512,256]{1,0:T(8,128)(2,1)S(1)}, u32[]{:S(2)}, u32[]{:S(2)}) collective-permute-start(bf16[512,256]{1,0:T(8,128)(2,1)S(1)} %get-tuple-element.115), channel_id=1, source_target_pairs={{0,8},{8,0},{16,24},{24,16},{1,9},{9,1},{17,25},{25,17},{2,10},{10... | collective-permute-start | bytes 786440 | tf_op jit(solution)/shard_map/ppermute | solution.py:20
  43.2 8.4 %collective-permute-start.12 = (bf16[512,256]{1,0:T(8,128)(2,1)S(1)}, bf16[512,256]{1,0:T(8,128)(2,1)S(1)}, u32[]{:S(2)}, u32[]{:S(2)}) collective-permute-start(bf16[512,256]{1,0:T(8,128)(2,1)S(1)} %get-tuple-element.116), channel_id=1, source_target_pairs={{0,16},{8,24},{16,0},{24,8},{1,17},{9,25},{17,1},{25,9},{2,18},{10... | collective-permute-start | bytes 786440 | tf_op jit(solution)/shard_map/ppermute | solution.py:20
  51.8 12.6 %collective-permute-start.13 = (bf16[896,256]{1,0:T(8,128)(2,1)S(1)}, bf16[896,256]{1,0:T(8,128)(2,1)S(1)}, u32[]{:S(2)}, u32[]{:S(2)}) collective-permute-start(bf16[896,256]{1,0:T(8,128)(2,1)S(1)} %get-tuple-element.119), channel_id=1, source_target_pairs={{0,8},{8,0},{16,24},{24,16},{1,9},{9,1},{17,25},{25,17},{2,10},{10... | collective-permute-start | bytes 1376264 | tf_op jit(solution)/shard_map/ppermute | solution.py:20
  52.4 12.0 %collective-permute-start.14 = (bf16[896,256]{1,0:T(8,128)(2,1)S(1)}, bf16[896,256]{1,0:T(8,128)(2,1)S(1)}, u32[]{:S(2)}, u32[]{:S(2)}) collective-permute-start(bf16[896,256]{1,0:T(8,128)(2,1)S(1)} %get-tuple-element.120), channel_id=1, source_target_pairs={{0,16},{8,24},{16,0},{24,8},{1,17},{9,25},{17,1},{25,9},{2,18},{10... | collective-permute-start | bytes 1376264 | tf_op jit(solution)/shard_map/ppermute | solution.py:20
  52.9 17.1 %collective-permute-start.17 = (bf16[32,4096]{1,0:T(8,128)(2,1)S(1)}, bf16[32,4096]{1,0:T(8,128)(2,1)S(1)}, u32[]{:S(2)}, u32[]{:S(2)}) collective-permute-start(bf16[32,4096]{1,0:T(8,128)(2,1)S(1)} %hold.5), channel_id=1, source_target_pairs={{0,2},{1,3},{2,4},{3,5},{4,6},{5,7},{6,0},{7,1},{8,10},{9,11},{10,... | collective-permute-start | bytes 786440 | tf_op jit(solution)/shard_map/ppermute | solution.py:25
  53.7 19.6 %collective-permute-start.18 = (bf16[32,4096]{1,0:T(8,128)(2,1)S(1)}, bf16[32,4096]{1,0:T(8,128)(2,1)S(1)}, u32[]{:S(2)}, u32[]{:S(2)}) collective-permute-start(bf16[32,4096]{1,0:T(8,128)(2,1)S(1)} %hold.5), channel_id=1, source_target_pairs={{0,4},{1,5},{2,6},{3,7},{4,0},{5,1},{6,2},{7,3},{8,12},{9,13},{10,... | collective-permute-start | bytes 786440 | tf_op jit(solution)/shard_map/ppermute | solution.py:25
  54.0 19.3 %collective-permute-start.19 = (bf16[32,4096]{1,0:T(8,128)(2,1)S(1)}, bf16[32,4096]{1,0:T(8,128)(2,1)S(1)}, u32[]{:S(2)}, u32[]{:S(2)}) collective-permute-start(bf16[32,4096]{1,0:T(8,128)(2,1)S(1)} %hold.5), channel_id=1, source_target_pairs={{0,6},{1,7},{2,0},{3,1},{4,2},{5,3},{6,4},{7,5},{8,14},{9,15},{10,... | collective-permute-start | bytes 786440 | tf_op jit(solution)/shard_map/ppermute | solution.py:25
  64.4 36.2 %copy-start.7 = (f32[3,2,384,256]{3,2,1,0:T(8,128)}, f32[3,2,384,256]{3,2,1,0:T(8,128)S(1)}, u32[]{:S(2)}) copy-start(f32[3,2,384,256]{3,2,1,0:T(8,128)S(1)} %get-tuple-element.130.refs_0_) | copy-start | bytes 7077892
  73.3 4.2 %collective-permute-start.20 = (bf16[96,4096]{1,0:T(8,128)(2,1)S(1)}, bf16[96,4096]{1,0:T(8,128)(2,1)S(1)}, u32[]{:S(2)}, u32[]{:S(2)}) collective-permute-start(bf16[96,4096]{1,0:T(8,128)(2,1)S(1)} %pack.14), channel_id=1, source_target_pairs={{0,1},{1,0},{2,3},{3,2},{4,5},{5,4},{6,7},{7,6},{8,9},{9,8},{10,11... | collective-permute-start | bytes 2359304 | tf_op jit(solution)/shard_map/ppermute | solution.py:33
  73.4 27.2 %collective-permute-start.15 = (bf16[1408,256]{1,0:T(8,128)(2,1)S(1)}, bf16[1408,256]{1,0:T(8,128)(2,1)S(1)}, u32[]{:S(2)}, u32[]{:S(2)}) collective-permute-start(bf16[1408,256]{1,0:T(8,128)(2,1)S(1)} %get-tuple-element.128), channel_id=1, source_target_pairs={{0,8},{8,0},{16,24},{24,16},{1,9},{9,1},{17,25},{25,17},{2,10},{10... | collective-permute-start | bytes 2162696 | tf_op jit(solution)/shard_map/ppermute | solution.py:20
  74.9 25.7 %collective-permute-start.16 = (bf16[1408,256]{1,0:T(8,128)(2,1)S(1)}, bf16[1408,256]{1,0:T(8,128)(2,1)S(1)}, u32[]{:S(2)}, u32[]{:S(2)}) collective-permute-start(bf16[1408,256]{1,0:T(8,128)(2,1)S(1)} %get-tuple-element.129), channel_id=1, source_target_pairs={{0,16},{8,24},{16,0},{24,8},{1,17},{9,25},{17,1},{25,9},{2,18},{10... | collective-permute-start | bytes 2162696 | tf_op jit(solution)/shard_map/ppermute | solution.py:20
  76.4 19.8 %collective-permute-start.21 = (bf16[384,256]{1,0:T(8,128)(2,1)S(1)}, bf16[384,256]{1,0:T(8,128)(2,1)S(1)}, u32[]{:S(2)}, u32[]{:S(2)}) collective-permute-start(bf16[384,256]{1,0:T(8,128)(2,1)S(1)} %get-tuple-element.136), channel_id=1, source_target_pairs={{0,8},{8,0},{16,24},{24,16},{1,9},{9,1},{17,25},{25,17},{2,10},{10... | collective-permute-start | bytes 589832 | tf_op jit(solution)/shard_map/ppermute | solution.py:20
  77.0 20.3 %collective-permute-start.22 = (bf16[384,256]{1,0:T(8,128)(2,1)S(1)}, bf16[384,256]{1,0:T(8,128)(2,1)S(1)}, u32[]{:S(2)}, u32[]{:S(2)}) collective-permute-start(bf16[384,256]{1,0:T(8,128)(2,1)S(1)} %get-tuple-element.137), channel_id=1, source_target_pairs={{0,16},{8,24},{16,0},{24,8},{1,17},{9,25},{17,1},{25,9},{2,18},{10... | collective-permute-start | bytes 589832 | tf_op jit(solution)/shard_map/ppermute | solution.py:20
  77.7 19.7 %copy-start.12 = (f32[3,2,384,256]{3,2,1,0:T(8,128)S(1)}, f32[3,2,384,256]{3,2,1,0:T(8,128)}, u32[]{:S(2)}) copy-start(f32[3,2,384,256]{3,2,1,0:T(8,128)} %copy-done.11) | copy-start | bytes 7077892
  87.8 14.5 %copy-start.41 = (f32[384,256]{1,0:T(8,128)}, f32[384,256]{1,0:T(8,128)S(1)}, u32[]{:S(2)}) copy-start(f32[384,256]{1,0:T(8,128)S(1)} %get-tuple-element.151.refs_1_) | copy-start | bytes 1179652
  87.8 14.5 %copy-start.43 = (f32[384,256]{1,0:T(8,128)}, f32[384,256]{1,0:T(8,128)S(1)}, u32[]{:S(2)}) copy-start(f32[384,256]{1,0:T(8,128)S(1)} %get-tuple-element.147.refs_4_) | copy-start | bytes 1179652
  87.8 14.5 %copy-start.51 = (f32[192,256]{1,0:T(8,128)}, f32[192,256]{1,0:T(8,128)S(1)}, u32[]{:S(2)}) copy-start(f32[192,256]{1,0:T(8,128)S(1)} %get-tuple-element.143) | copy-start | bytes 589828
  98.5 21.6 %collective-permute-start.23 = (bf16[1152,256]{1,0:T(8,128)(2,1)}, bf16[1152,256]{1,0:T(8,128)(2,1)}, u32[]{:S(2)}, u32[]{:S(2)}) collective-permute-start(bf16[1152,256]{1,0:T(8,128)(2,1)} %get-tuple-element.145), channel_id=1, source_target_pairs={{0,8},{8,0},{16,24},{24,16},{1,9},{9,1},{17,25},{25,17},{2,10},{10... | collective-permute-start | bytes 1769480 | tf_op jit(solution)/shard_map/ppermute | solution.py:20
  99.1 21.0 %collective-permute-start.24 = (bf16[1152,256]{1,0:T(8,128)(2,1)}, bf16[1152,256]{1,0:T(8,128)(2,1)}, u32[]{:S(2)}, u32[]{:S(2)}) collective-permute-start(bf16[1152,256]{1,0:T(8,128)(2,1)} %get-tuple-element.146), channel_id=1, source_target_pairs={{0,16},{8,24},{16,0},{24,8},{1,17},{9,25},{17,1},{25,9},{2,18},{10... | collective-permute-start | bytes 1769480 | tf_op jit(solution)/shard_map/ppermute | solution.py:20
  103.1 28.8 %collective-permute-start.27 = (bf16[1536,256]{1,0:T(8,128)(2,1)}, bf16[1536,256]{1,0:T(8,128)(2,1)}, u32[]{:S(2)}, u32[]{:S(2)}) collective-permute-start(bf16[1536,256]{1,0:T(8,128)(2,1)} %get-tuple-element.152), channel_id=1, source_target_pairs={{0,8},{8,0},{16,24},{24,16},{1,9},{9,1},{17,25},{25,17},{2,10},{10... | collective-permute-start | bytes 2359304 | tf_op jit(solution)/shard_map/ppermute | solution.py:20
  104.5 28.0 %collective-permute-start.28 = (bf16[1536,256]{1,0:T(8,128)(2,1)}, bf16[1536,256]{1,0:T(8,128)(2,1)}, u32[]{:S(2)}, u32[]{:S(2)}) collective-permute-start(bf16[1536,256]{1,0:T(8,128)(2,1)} %get-tuple-element.153), channel_id=1, source_target_pairs={{0,16},{8,24},{16,0},{24,8},{1,17},{9,25},{17,1},{25,9},{2,18},{10... | collective-permute-start | bytes 2359304 | tf_op jit(solution)/shard_map/ppermute | solution.py:20
  116.0 52.4 %copy-start.25 = (bf16[2,256,1024]{2,1,0:T(8,128)(2,1)}, bf16[2,256,1024]{2,1,0:T(8,128)(2,1)S(1)}, u32[]{:S(2)}) copy-start(bf16[2,256,1024]{2,1,0:T(8,128)(2,1)S(1)} %get-tuple-element.141.refs_2_) | copy-start | bytes 3145732
  120.1 12.4 %copy-start.8 = (f32[3,2,384,256]{3,2,1,0:T(8,128)S(1)}, f32[3,2,384,256]{3,2,1,0:T(8,128)}, u32[]{:S(2)}) copy-start(f32[3,2,384,256]{3,2,1,0:T(8,128)} %copy-done.7) | copy-start | bytes 7077892
  120.2 12.4 %copy-start.42 = (f32[384,256]{1,0:T(8,128)S(1)}, f32[384,256]{1,0:T(8,128)}, u32[]{:S(2)}) copy-start(f32[384,256]{1,0:T(8,128)} %copy-done.41) | copy-start | bytes 1179652
  122.3 15.5 %copy-start.50 = (f32[192,256]{1,0:T(8,128)S(1)}, f32[192,256]{1,0:T(8,128)}, u32[]{:S(2)}) copy-start(f32[192,256]{1,0:T(8,128)} %copy-done.49) | copy-start | bytes 589828
  122.4 15.5 %copy-start.52 = (f32[192,256]{1,0:T(8,128)S(1)}, f32[192,256]{1,0:T(8,128)}, u32[]{:S(2)}) copy-start(f32[192,256]{1,0:T(8,128)} %copy-done.51) | copy-start | bytes 589828
  122.4 26.3 %collective-permute-start.25 = (bf16[1536,256]{1,0:T(8,128)(2,1)S(1)}, bf16[1536,256]{1,0:T(8,128)(2,1)S(1)}, u32[]{:S(2)}, u32[]{:S(2)}) collective-permute-start(bf16[1536,256]{1,0:T(8,128)(2,1)S(1)} %get-tuple-element.149), channel_id=1, source_target_pairs={{0,8},{8,0},{16,24},{24,16},{1,9},{9,1},{17,25},{25,17},{2,10},{10... | collective-permute-start | bytes 2359304 | tf_op jit(solution)/shard_map/ppermute | solution.py:20
  123.0 26.2 %collective-permute-start.26 = (bf16[1536,256]{1,0:T(8,128)(2,1)S(1)}, bf16[1536,256]{1,0:T(8,128)(2,1)S(1)}, u32[]{:S(2)}, u32[]{:S(2)}) collective-permute-start(bf16[1536,256]{1,0:T(8,128)(2,1)S(1)} %get-tuple-element.150), channel_id=1, source_target_pairs={{0,16},{8,24},{16,0},{24,8},{1,17},{9,25},{17,1},{25,9},{2,18},{10... | collective-permute-start | bytes 2359304 | tf_op jit(solution)/shard_map/ppermute | solution.py:20
  132.5 34.1 %slice-start.2 = ((s8[7340032]{0:T(1024)(128)(4,1)}), s8[4194304]{0:T(1024)(128)(4,1)S(1)}, s32[]{:S(2)}) async-start(s8[7340032]{0:T(1024)(128)(4,1)} %bitcast.129), calls=%async_computation.2 | async-start | bytes 8388608
  134.8 26.4 %collective-permute-start.31 = (bf16[1152,256]{1,0:T(8,128)(2,1)S(1)}, bf16[1152,256]{1,0:T(8,128)(2,1)S(1)}, u32[]{:S(2)}, u32[]{:S(2)}) collective-permute-start(bf16[1152,256]{1,0:T(8,128)(2,1)S(1)} %get-tuple-element.160), channel_id=1, source_target_pairs={{0,8},{8,0},{16,24},{24,16},{1,9},{9,1},{17,25},{25,17},{2,10},{10... | collective-permute-start | bytes 1769480 | tf_op jit(solution)/shard_map/ppermute | solution.py:20
  136.3 25.6 %collective-permute-start.32 = (bf16[1152,256]{1,0:T(8,128)(2,1)S(1)}, bf16[1152,256]{1,0:T(8,128)(2,1)S(1)}, u32[]{:S(2)}, u32[]{:S(2)}) collective-permute-start(bf16[1152,256]{1,0:T(8,128)(2,1)S(1)} %get-tuple-element.161), channel_id=1, source_target_pairs={{0,16},{8,24},{16,0},{24,8},{1,17},{9,25},{17,1},{25,9},{2,18},{10... | collective-permute-start | bytes 1769480 | tf_op jit(solution)/shard_map/ppermute | solution.py:20
  137.9 27.1 %copy-start.40 = (bf16[2,384,256]{2,1,0:T(8,128)(2,1)S(1)}, bf16[2,384,256]{2,1,0:T(8,128)(2,1)}, u32[]{:S(2)}) copy-start(bf16[2,384,256]{2,1,0:T(8,128)(2,1)} %copy-done.39) | copy-start | bytes 1179652
  149.3 17.3 %slice-start.3 = ((s8[7340032]{0:T(1024)(128)(4,1)}), s8[3145728]{0:T(1024)(128)(4,1)S(1)}, s32[]{:S(2)}) async-start(s8[7340032]{0:T(1024)(128)(4,1)} %bitcast.129), calls=%async_computation.3 | async-start | bytes 6291456
  149.3 19.2 %slice-start.6 = ((s8[7340032]{0:T(1024)(128)(4,1)}), s8[4194304]{0:T(1024)(128)(4,1)S(1)}, s32[]{:S(2)}) async-start(s8[7340032]{0:T(1024)(128)(4,1)} %bitcast.137), calls=%async_computation.6 | async-start | bytes 8388608
  149.6 29.9 %collective-permute-start.29 = (bf16[1152,256]{1,0:T(8,128)(2,1)S(1)}, bf16[1152,256]{1,0:T(8,128)(2,1)S(1)}, u32[]{:S(2)}, u32[]{:S(2)}) collective-permute-start(bf16[1152,256]{1,0:T(8,128)(2,1)S(1)} %get-tuple-element.157), channel_id=1, source_target_pairs={{0,8},{8,0},{16,24},{24,16},{1,9},{9,1},{17,25},{25,17},{2,10},{10... | collective-permute-start | bytes 1769480 | tf_op jit(solution)/shard_map/ppermute | solution.py:20
  151.1 28.4 %collective-permute-start.30 = (bf16[1152,256]{1,0:T(8,128)(2,1)S(1)}, bf16[1152,256]{1,0:T(8,128)(2,1)S(1)}, u32[]{:S(2)}, u32[]{:S(2)}) collective-permute-start(bf16[1152,256]{1,0:T(8,128)(2,1)S(1)} %get-tuple-element.158), channel_id=1, source_target_pairs={{0,16},{8,24},{16,0},{24,8},{1,17},{9,25},{17,1},{25,9},{2,18},{10... | collective-permute-start | bytes 1769480 | tf_op jit(solution)/shard_map/ppermute | solution.py:20
  161.9 20.8 %collective-permute-start.35 = (bf16[384,256]{1,0:T(8,128)(2,1)S(1)}, bf16[384,256]{1,0:T(8,128)(2,1)S(1)}, u32[]{:S(2)}, u32[]{:S(2)}) collective-permute-start(bf16[384,256]{1,0:T(8,128)(2,1)S(1)} %get-tuple-element.170), channel_id=1, source_target_pairs={{0,8},{8,0},{16,24},{24,16},{1,9},{9,1},{17,25},{25,17},{2,10},{10... | collective-permute-start | bytes 589832 | tf_op jit(solution)/shard_map/ppermute | solution.py:20
  163.4 19.3 %collective-permute-start.36 = (bf16[384,256]{1,0:T(8,128)(2,1)S(1)}, bf16[384,256]{1,0:T(8,128)(2,1)S(1)}, u32[]{:S(2)}, u32[]{:S(2)}) collective-permute-start(bf16[384,256]{1,0:T(8,128)(2,1)S(1)} %get-tuple-element.171), channel_id=1, source_target_pairs={{0,16},{8,24},{16,0},{24,8},{1,17},{9,25},{17,1},{25,9},{2,18},{10... | collective-permute-start | bytes 589832 | tf_op jit(solution)/shard_map/ppermute | solution.py:20
  179.6 6.3 %collective-permute-start.33 = (bf16[384,256]{1,0:T(8,128)(2,1)S(1)}, bf16[384,256]{1,0:T(8,128)(2,1)S(1)}, u32[]{:S(2)}, u32[]{:S(2)}) collective-permute-start(bf16[384,256]{1,0:T(8,128)(2,1)S(1)} %get-tuple-element.167), channel_id=1, source_target_pairs={{0,8},{8,0},{16,24},{24,16},{1,9},{9,1},{17,25},{25,17},{2,10},{10... | collective-permute-start | bytes 589832 | tf_op jit(solution)/shard_map/ppermute | solution.py:20
  180.2 5.7 %collective-permute-start.34 = (bf16[384,256]{1,0:T(8,128)(2,1)S(1)}, bf16[384,256]{1,0:T(8,128)(2,1)S(1)}, u32[]{:S(2)}, u32[]{:S(2)}) collective-permute-start(bf16[384,256]{1,0:T(8,128)(2,1)S(1)} %get-tuple-element.168), channel_id=1, source_target_pairs={{0,16},{8,24},{16,0},{24,8},{1,17},{9,25},{17,1},{25,9},{2,18},{10... | collective-permute-start | bytes 589832 | tf_op jit(solution)/shard_map/ppermute | solution.py:20
  185.8 4.2 %collective-permute-start.39 = (bf16[2,4,32,1024]{3,2,1,0:T(8,128)(2,1)S(1)}, bf16[2,4,32,1024]{3,2,1,0:T(8,128)(2,1)S(1)}, u32[]{:S(2)}, u32[]{:S(2)}) collective-permute-start(bf16[2,4,32,1024]{3,2,1,0:T(8,128)(2,1)S(1)} %pad_maximum_fusion.1), channel_id=1, source_target_pairs={{0,1},{1,0},{2,3},{3,2},{4,5},{5,4},{6,7},{7,6},{8,9},{9,8},{10,11... | collective-permute-start | bytes 1572872 | tf_op jit(solution)/shard_map/ppermute | solution.py:33
  189.5 9.4 %collective-permute-start.37 = (bf16[2,4,32,1024]{3,2,1,0:T(8,128)(2,1)S(1)}, bf16[2,4,32,1024]{3,2,1,0:T(8,128)(2,1)S(1)}, u32[]{:S(2)}, u32[]{:S(2)}) collective-permute-start(bf16[2,4,32,1024]{3,2,1,0:T(8,128)(2,1)S(1)} %pad_maximum_fusion), channel_id=1, source_target_pairs={{0,1},{1,0},{2,3},{3,2},{4,5},{5,4},{6,7},{7,6},{8,9},{9,8},{10,11... | collective-permute-start | bytes 1572872 | tf_op jit(solution)/shard_map/ppermute | solution.py:33
  191.0 33.1 %collective-permute-start.41 = (bf16[4,32,1024]{2,1,0:T(8,128)(2,1)}, bf16[4,32,1024]{2,1,0:T(8,128)(2,1)}, u32[]{:S(2)}, u32[]{:S(2)}) collective-permute-start(bf16[4,32,1024]{2,1,0:T(8,128)(2,1)} %get-tuple-element.204), channel_id=1, source_target_pairs={{0,4},{1,5},{2,6},{3,7},{4,0},{5,1},{6,2},{7,3},{8,12},{9,13},{10,... | collective-permute-start | bytes 786440 | tf_op jit(solution)/shard_map/ppermute | solution.py:25
  195.5 28.7 %collective-permute-start.40 = (bf16[4,32,1024]{2,1,0:T(8,128)(2,1)}, bf16[4,32,1024]{2,1,0:T(8,128)(2,1)}, u32[]{:S(2)}, u32[]{:S(2)}) collective-permute-start(bf16[4,32,1024]{2,1,0:T(8,128)(2,1)} %get-tuple-element.203), channel_id=1, source_target_pairs={{0,6},{1,7},{2,0},{3,1},{4,2},{5,3},{6,4},{7,5},{8,14},{9,15},{10,... | collective-permute-start | bytes 786440 | tf_op jit(solution)/shard_map/ppermute | solution.py:25
  199.8 24.4 %collective-permute-start.38 = (bf16[4,32,1024]{2,1,0:T(8,128)(2,1)}, bf16[4,32,1024]{2,1,0:T(8,128)(2,1)}, u32[]{:S(2)}, u32[]{:S(2)}) collective-permute-start(bf16[4,32,1024]{2,1,0:T(8,128)(2,1)} %fusion.24), channel_id=1, source_target_pairs={{0,2},{1,3},{2,4},{3,5},{4,6},{5,7},{6,0},{7,1},{8,10},{9,11},{10,... | collective-permute-start | bytes 786440 | tf_op jit(solution)/shard_map/ppermute | solution.py:25
  214.3 14.9 %copy-start.15 = (bf16[4,128,1024]{2,1,0:T(8,128)(2,1)S(1)}, bf16[4,128,1024]{2,1,0:T(8,128)(2,1)}, u32[]{:S(2)}) copy-start(bf16[4,128,1024]{2,1,0:T(8,128)(2,1)} %copy-done.14) | copy-start | bytes 3145732
  214.3 14.9 %copy-start.17 = (bf16[4,128,1024]{2,1,0:T(8,128)(2,1)S(1)}, bf16[4,128,1024]{2,1,0:T(8,128)(2,1)}, u32[]{:S(2)}) copy-start(bf16[4,128,1024]{2,1,0:T(8,128)(2,1)} %copy-done.16) | copy-start | bytes 3145732
  214.3 14.9 %copy-start.34 = (bf16[2,512,768]{2,1,0:T(8,128)(2,1)S(1)}, bf16[2,512,768]{2,1,0:T(8,128)(2,1)}, u32[]{:S(2)}) copy-start(bf16[2,512,768]{2,1,0:T(8,128)(2,1)} %copy-done.33) | copy-start | bytes 4718596
  225.6 17.5 %collective-permute-start.44 = (bf16[32,1024]{1,0:T(8,128)(2,1)S(1)}, bf16[32,1024]{1,0:T(8,128)(2,1)S(1)}, u32[]{:S(2)}, u32[]{:S(2)}) collective-permute-start(bf16[32,1024]{1,0:T(8,128)(2,1)S(1)} %get-tuple-element.210), channel_id=1, source_target_pairs={{0,24},{8,16},{16,8},{24,0},{1,25},{9,17},{17,9},{25,1},{2,26},{10... | collective-permute-start | bytes 196616 | tf_op jit(solution)/shard_map/ppermute | solution.py:20
  228.1 15.1 %collective-permute-start.43 = (bf16[32,1024]{1,0:T(8,128)(2,1)S(1)}, bf16[32,1024]{1,0:T(8,128)(2,1)S(1)}, u32[]{:S(2)}, u32[]{:S(2)}) collective-permute-start(bf16[32,1024]{1,0:T(8,128)(2,1)S(1)} %get-tuple-element.211), channel_id=1, source_target_pairs={{0,16},{8,24},{16,0},{24,8},{1,17},{9,25},{17,1},{25,9},{2,18},{10... | collective-permute-start | bytes 196616 | tf_op jit(solution)/shard_map/ppermute | solution.py:20
  228.6 14.6 %collective-permute-start.42 = (bf16[32,1024]{1,0:T(8,128)(2,1)S(1)}, bf16[32,1024]{1,0:T(8,128)(2,1)S(1)}, u32[]{:S(2)}, u32[]{:S(2)}) collective-permute-start(bf16[32,1024]{1,0:T(8,128)(2,1)S(1)} %get-tuple-element.212), channel_id=1, source_target_pairs={{0,8},{8,0},{16,24},{24,16},{1,9},{9,1},{17,25},{25,17},{2,10},{10... | collective-permute-start | bytes 196616 | tf_op jit(solution)/shard_map/ppermute | solution.py:20
  (49 other events, 150.6 us)

commit v4 on v3

--- a/solution.py
+++ b/solution.py
@@ -27,6 +27,10 @@
 
 def onward(value, distance):
     return back(value, -distance)
+
+
+def ring(value):
+    return onward(value, 1)
 
 
 def pair(value):
@@ -70,7 +74,9 @@
 def pack_kernel(cuts, axis, *refs):
     out, at = refs[-1], 0
     for ref, (lo, hi) in zip(refs, cuts):
-        if axis:
+        if axis == 2:
+            out[:, :, at : at + hi - lo] = ref[:, :, lo:hi]
+        elif axis == 1:
             out[:, at : at + hi - lo] = ref[:, lo:hi]
         else:
             out[at : at + hi - lo] = ref[lo:hi]
@@ -85,7 +91,7 @@
         in_specs=[in_vmem] * len(pieces) + [pl.BlockSpec(memory_space=pl.ANY)] * len(others),
         out_specs=in_vmem,
         out_shape=jax.ShapeDtypeStruct(tuple(shape), pieces[0][0].dtype),
-        compiler_params=pltpu.CompilerParams(vmem_limit_bytes=4 << 20),
+        compiler_params=pltpu.CompilerParams(vmem_limit_bytes=12 << 20),
         cost_estimate=pl.CostEstimate(flops=1, bytes_accessed=1, transcendentals=0),
         name="pack",
     )(*[p[0] for p in pieces], *others)
@@ -124,8 +130,8 @@
     token_refs = refs[:parts]
     grad_refs = refs[parts : 2 * parts]
     weight_hbm, first_hbm, first_scale, second_hbm, second_scale = refs[2 * parts : 2 * parts + 5]
-    outs_hbm = refs[-12:-9]
-    first_tops, second_tops, top_table, total, rows_max, held_in, held_out, sem_in, sem_out = refs[-9:]
+    outs_hbm = refs[-13:-10]
+    first_tops, second_tops, wide_scale, top_table, total, rows_max, held_in, held_out, sem_in, sem_out = refs[-10:]
     first_gain = (1.0 - beta_first) / float(total_tokens) ** 0.5
     second_gain = (1.0 - beta_second) / float(total_tokens)
     group = 8
@@ -151,6 +157,12 @@
         return carry
 
     lax.fori_loop(0, 2 * tiles, begin, 0)
+    for k in range(2):
+        for lane in range(0, columns, 128):
+            at_scale = pl.ds((c0 + lane) // 128, 1)
+            shape = (first_scale.shape[1], 128)
+            wide_scale[k, :, pl.ds(lane, 128)] = jnp.broadcast_to(first_scale[k, :, at_scale] * beta_first, shape)
+            wide_scale[2 + k, :, pl.ds(lane, 128)] = jnp.broadcast_to(second_scale[k, :, at_scale] * beta_second, shape)
 
     def work(i, carry):
         k, span_all = place(i)
@@ -174,8 +186,8 @@
             for lane in range(0, columns, 128):
                 side = pl.ds(lane, 128)
                 slot = 2 * (lane // 128)
-                scale_one = first_scale[k, blocks, pl.ds(c0 + lane, 128)] * beta_first
-                scale_two = second_scale[k, blocks, pl.ds(c0 + lane, 128)] * beta_second
+                scale_one = wide_scale[k, blocks, side]
+                scale_two = wide_scale[2 + k, blocks, side]
                 states = []
                 for b in range(group):
                     near = pl.ds(pl.multiple_of(at * group * 16, group * 16) + b * 16, 16)
@@ -252,6 +264,7 @@
         2 * elements * sum(t.shape[0] for t, _, _ in parts) + 40 * elements,
         12 * elements,
         scratch=[
+            pltpu.VMEM((4, rows // 16, columns), f32),
             pltpu.VMEM((4, rows // 16, 128), f32),
             pltpu.VMEM((tile, columns), f32),
             pltpu.VMEM((columns // 64, 64, 128), f32),
@@ -264,20 +277,31 @@
     )
 
 
-def pre_kernel(c0, count, width, token_ref, weight_ref, send_ref, keep_ref):
+def pre_kernel(c0, count, width, token_ref, weight_ref, send_ref, keep_ref, held, sem):
     n = token_ref.shape[0] // 4
-    depth = weight_ref.shape[1]
-
-    def work(block):
-        k, c = pl.program_id(0), pl.program_id(1)
-        value = jnp.dot(token_ref[...], block[0], preferred_element_type=f32)
+
+    def copy(i):
+        k, c = i // count, i % count
+        columns = pl.ds(pl.multiple_of((c0 + c) * width, width), width)
+        return pltpu.make_async_copy(weight_ref.at[k, :, columns], held.at[i], sem.at[i])
+
+    def begin(i, carry):
+        copy(i).start()
+        return carry
+
+    lax.fori_loop(0, 2 * count, begin, 0)
+
+    def work(i, carry):
+        k, c = i // count, i % count
+        copy(i).wait()
+        value = jnp.dot(token_ref[...], held[i], preferred_element_type=f32)
         span = pl.ds(pl.multiple_of(c * n, n), n)
         send_ref[k, span] = value[3 * n :].astype(bf16)
         for slot in range(3):
             keep_ref[slot, k, span] = value[slot * n : (slot + 1) * n]
-
-    spec = pl.BlockSpec((1, depth, width), lambda k, c: (k, 0, c))
-    pltpu.emit_pipeline(work, grid=(2, count), in_specs=[spec])(weight_ref.at[:, :, pl.ds(c0 * width, count * width)])
+        return carry
+
+    lax.fori_loop(0, 2 * count, work, 0)
 
 
 def partial_pre(chain, tokens, weight, c0, c1, width, vmem):
@@ -294,15 +318,28 @@
         vmem,
         4 * rows * depth * count * width,
         4 * depth * count * width,
+        scratch=[pltpu.VMEM((2 * count, depth, width), bf16), pltpu.SemaphoreType.DMA((2 * count,))],
     )
 
 
-def hidden_kernel(width, spans, grad_ref, down_ref, *outs):
-    depth = grad_ref.shape[1]
-
-    def work(block):
-        c = pl.program_id(0)
-        value = lax.dot_general(grad_ref[...], block[...], (((1,), (1,)), ((), ())), preferred_element_type=f32)
+def hidden_kernel(width, spans, grad_ref, down_ref, *refs):
+    outs, held, sem = refs[: len(spans)], refs[-2], refs[-1]
+    count = down_ref.shape[0] // width
+
+    def copy(i):
+        return pltpu.make_async_copy(down_ref.at[pl.ds(pl.multiple_of(i * width, width), width)], held.at[i], sem.at[i])
+
+    def begin(i, carry):
+        copy(i).start()
+        return carry
+
+    lax.fori_loop(0, count, begin, 0)
+
+    def work(c, carry):
+        copy(c).wait()
+        value = jnp.transpose(
+            lax.dot_general(held[c], grad_ref[...], (((1,), (1,)), ((), ())), preferred_element_type=f32)
+        )
         for (r0, r1, c0, c1), out in zip(spans, outs):
             n = r1 - r0
 
@@ -310,11 +347,12 @@
             def _():
                 out[pl.ds(pl.multiple_of((c - c0) * n, n), n)] = value[r0:r1]
 
-    spec = pl.BlockSpec((width, depth), lambda c: (c, 0))
-    pltpu.emit_pipeline(work, grid=(down_ref.shape[0] // width,), in_specs=[spec])(down_ref)
-
-
-def hidden_grad(chain, cot, down, width, spans):
+        return carry
+
+    lax.fori_loop(0, count, work, 0)
+
+
+def hidden_grad(chain, cot, down, width, spans, vmem):
     rows, depth = cot.shape
     return chain.call(
         functools.partial(hidden_kernel, width, spans),
@@ -323,9 +361,13 @@
         [in_vmem] * len(spans),
         [jax.ShapeDtypeStruct(((r1 - r0) * (c1 - c0), width), f32) for r0, r1, c0, c1 in spans],
         "hidden_grad",
-        46,
+        vmem,
         2 * rows * depth * down.shape[0],
         2 * depth * down.shape[0],
+        scratch=[
+            pltpu.VMEM((down.shape[0] // width, width, depth), bf16),
+            pltpu.SemaphoreType.DMA((down.shape[0] // width,)),
+        ],
     )
 
 
@@ -428,7 +470,7 @@
             [in_vmem] * len(shapes),
             shapes,
             "exchange_step",
-            4,
+            12,
             8 * at * self.width,
             8 * at * self.width,
         )
@@ -445,7 +487,7 @@
             [in_vmem],
             [jax.ShapeDtypeStruct((2, 4 * n, columns), bf16)],
             "pre_grad",
-            4,
+            8,
             0,
             16 * n * columns,
         )
@@ -471,8 +513,8 @@
     slots = [swap(block, s) if s else block for s, block in enumerate(blocks)]
     block = jnp.stack(slots)
 
-    def near(value, axis):
-        return pack([(v, 0, v.shape[axis]) for v in (value, pair(value))], axis)
+    def near(value, axis, *others):
+        return pack([(v, 0, v.shape[axis]) for v in (value, pair(value))], axis, *others)
 
     def send_on(value):
         return [onward(value, k) for k in rest]
@@ -487,21 +529,17 @@
 
     packed = {((0,), 0): near(block, 1)}
     sent = send_on(block)
-    held = hold_until(cotangent, block)
-    packed[(0,), 1] = near(held, 0)
+    packed[(0,), 1] = near(cotangent, 0, block)
     if not staged and rest:
         packed[rest, 0] = far(sent, 1)
-        packed[rest, 1] = far(send_on(held), 0)
+        packed[rest, 1] = far(send_on(cotangent), 0)
 
     if staged:
         last = chunks - max(1, (chunks * 3) // 7)
+        second = 7
         plan = {0: ((0,), 0, last)}
-        at = 4
-        for c in range(0, last, 2):
-            plan[at] = (rest, c, min(c + 2, last))
-            at += 1
-        plan[at] = (every[1:3], last, chunks)
-        plan[at + 1] = ((every[3], 0), last, chunks)
+        plan[4] = (rest, 0, last)
+        plan[second] = (every, last, chunks)
     else:
         plan = {c: (every, c, c + 1) for c in range(chunks)}
 
@@ -516,7 +554,6 @@
         t = packed[ks, 0]
         return (t, packed.get((ks, 1)), t.reshape(-1, rows))
 
-    expand = lambda scale: jnp.repeat(scale, 128, axis=2)
 
     def forward(ks, c0, c1):
         t, c, _ = rows_of(ks)
@@ -602,13 +639,10 @@
         result, tops = [None], {}
 
         def input_grad_start():
-            partial = partials()
-            halves = [every[1:3], (every[3], 0)]
-            arrived = [across(partial, ks) for ks in halves]
+            arrived = across(partials(), every)
 
             def wait():
-                total = sum(arrived[1][::-1] + arrived[0], jnp.zeros((groups, own, rows), f32))
-                moved.append(total.astype(bf16))
+                moved.append(sum(arrived).astype(bf16))
                 chain.add(moved[0])
 
             return wait
@@ -617,24 +651,19 @@
 
         def start(u):
             exchange.sends[u], exchange.keeps[u] = partial_pre(
-                chain, rows_of(plan[u][0])[2], gate_up, *plan[u][1:], width, 8 if u else 56
+                chain, rows_of(plan[u][0])[2], gate_up, *plan[u][1:], width, 12 if u else 56
             )
 
         def hidden_first():
-            return hidden_grad(chain, rows_of((0,))[1], down_weight, width, [(0, 2 * own, 0, last), (0, 2 * own, last, chunks)])
+            return hidden_grad(chain, rows_of((0,))[1], down_weight, width, [(0, 2 * own, 0, last), (0, 2 * own, last, chunks)], 56)
 
         def hidden_rest(first, tail):
             n = 2 * own
-            cuts = [(0, 3 * n, c0, c1) for ks, c0, c1 in plan.values() if ks == rest]
-            cuts += [(0, 2 * n, last, chunks), (2 * n, 3 * n, last, chunks)]
-            found = hidden_grad(chain, rows_of(rest)[1], down_weight, width, cuts)
-            exchange.hidden[0] = first
-            units_of_rest = [u for u in plan if plan[u][0] == rest]
-            for u, value in zip(units_of_rest, found):
-                exchange.hidden[u] = value
-            exchange.hidden[max(plan) - 1] = found[-2]
-            both = jnp.stack([found[-1].reshape(chunks - last, n, width), tail.reshape(chunks - last, n, width)], axis=1)
-            exchange.hidden[max(plan)] = both.reshape(-1, width)
+            cuts = [(0, 3 * n, 0, last), (0, 3 * n, last, chunks)]
+            found = hidden_grad(chain, rows_of(rest)[1], down_weight, width, cuts, 24)
+            exchange.hidden[4] = found[0]
+            both = [tail.reshape(chunks - last, n, width), found[1].reshape(chunks - last, 3 * n, width)]
+            exchange.hidden[second] = pack([(v, 0, v.shape[1]) for v in both], 1).reshape(-1, width)
 
         def finish(u):
             grads[u] = exchange.gather(u)
@@ -648,46 +677,37 @@
                 if a <= c0 and c1 <= b:
                     parts.append((rows_of(ks)[2], grads[u], (c0 - a) * width))
             *result[0], tops[c0, 0], tops[c0, 1] = weight_step(
-                chain, vmem, parts, gate_up, first_code, first_wide, second_code, second_wide, result[0], c0 * width, (c1 - c0) * width, total_tokens
+                chain, vmem, parts, gate_up, first_code, first_scale, second_code, second_scale, result[0], c0 * width, (c1 - c0) * width, total_tokens
             )
 
         start(0)
-        spans = [p[1:] for p in plan.values() if p[0] == rest]
-        pending = []
         for place, m in enumerate(steps):
             exchange.step(m)
-            if m == 0:
+            token = chain.tokens[0]
+            if m == lag:
+                packed[rest, 0] = far(sent, 1, token)
                 exchange.hidden[0], hidden_tail = hidden_first()
-            if m == lag:
-                packed[rest, 0] = far(sent, 1, chain.tokens[0])
-                cot_sent = send_on(hold_until(cotangent, packed[rest, 0]))
+            elif m == 2 * lag:
+                cot_sent = send_on(hold_until(cotangent, token))
+            elif m == 4 * lag - 1:
+                packed[rest, 1] = far(cot_sent, 0, token)
+                hidden_rest(exchange.hidden[0], hidden_tail)
             if place + 1 < len(steps) and steps[place + 1] in plan:
                 start(steps[place + 1])
-            if m == 3 * lag:
-                packed[rest, 1] = far(cot_sent, 0, chain.tokens[0])
-                hidden_rest(exchange.hidden[0], hidden_tail)
             if m == 4 * lag:
-                first_wide = expand(hold_until(first_scale, chain.tokens[0]))
-                second_wide = expand(hold_until(second_scale, chain.tokens[0]))
-                chain.add(first_wide)
-                chain.add(second_wide)
-            done = m - 4 * lag
-            if done in plan:
-                finish(done)
-                inputs(done)
-                if plan[done][0] == rest:
-                    pending.append(plan[done][1:])
-            if pending and place + 1 < len(steps):
-                update(*pending.pop(0), 20)
-        for u in plan:
-            if u not in grads:
-                finish(u)
-                inputs(u)
+                finish(0)
+                inputs(0)
+            if m == second + 2 * lag:
+                finish(4)
+                inputs(4)
+                update(0, last // 2, 20)
+        finish(second)
+        inputs(second)
         wait = input_grad_start()
-        for span in pending:
-            update(*span, 20)
+        update(last // 2, last, 44)
+        update(last, chunks - 1, 44)
         wait()
-        update(last, chunks, 44)
+        update(chunks - 1, chunks, 44)
         outs = result[0]
         moved = moved[0]
     else:
@@ -701,7 +721,6 @@
     input_grad = final.reshape(own, depth)
 
     if not staged:
-        first_wide, second_wide = expand(first_scale), expand(second_scale)
         chain, outs, tops = Chain(), None, {}
         for c, (ks, c0, c1) in plan.items():
             *outs, tops[c0, 0], tops[c0, 1] = weight_step(
@@ -710,9 +729,9 @@
                 [(rows_of(ks)[2], grads[c], 0)],
                 gate_up,
                 first_code,
-                first_wide,
+                first_scale,
                 second_code,
-                second_wide,
+                second_scale,
                 outs,
                 c0 * width,
                 (c1 - c0) * width,

time: 245 us -> 233 us (0.951)
  local copies, waits for them, and re-layouts: 38.1 us -> 24 us
  waiting for transfers between devices: 50.6 us -> 57.8 us
  matrix products: 11.3 us -> 8.15 us
  Pallas kernels: 84.8 us -> 81.8 us
  starting transfers between devices: 52.6 us -> 55.3 us
    unnamed x138 -> x130, local copies, waits for them, and re-layouts: 31.1 us -> 22.6 us
    ppermute x30 -> x26, waiting for transfers between devices: 47.1 us -> 54.2 us  [swap(): lax.ppermute(value, 'dp', [(p, p ^ mask) for p in range(lax.axis_size('dp...]
    ppermute x9, starting transfers between devices: 17.3 us -> 21.3 us  [back(): lax.ppermute(value, 'tensor', [(p, (p - 2 * distance) % size) for p in ra...]
    pallas_call x27 -> x22, Pallas kernels: 84.2 us -> 80.2 us  [call(): pl.pallas_call(body, in_specs=list(in_specs) + [anywhere] * held, out_spe...]
    ppermute x6 -> x5, waiting for transfers between devices: 0.22 us -> 3.43 us  [pair(): lax.ppermute(value, 'tensor', [(p, p ^ 1) for p in range(lax.axis_size('t...]
    dot_general x5 -> x3, matrix products: 11.3 us -> 8.15 us  [shards(): jnp.einsum('ktf,kdf->td', g, gate_up[:, :, c0 * width:c1 * width], prefer...]
    ppermute x9, waiting for transfers between devices: 3.23 us -> 0.1 us  [back(): lax.ppermute(value, 'tensor', [(p, (p - 2 * distance) % size) for p in ra...]
    reshape x2 -> x0, local copies, waits for them, and re-layouts: 2.75 us -> none  [shards(): expand = lambda scale: jnp.repeat(scale, 128, axis=2)]
  transfers between devices with their start and end apart: 45 -> 40, of which waited for: 15 -> 20; matrix products, arithmetic and copies ran while one was open for 9% -> 2% of each run, Pallas kernels for 35% -> 34%
where the time goes in v4:
time: 233 us
  Pallas kernels  81.8 us (35%)
  waiting for transfers between devices  57.8 us (25%)
  starting transfers between devices  55.3 us (24%)
  local copies, waits for them, and re-layouts  24 us (10%)
  matrix products  8.15 us (3%)
  other arithmetic  4.08 us (2%)
    pallas_call x22, Pallas kernels, call(): pl.pallas_call(body, in_specs=list(in_specs) + [anywhere] * held, out_spe...  80.2 us
    ppermute x26, waiting for transfers between devices, swap(): lax.ppermute(value, 'dp', [(p, p ^ mask) for p in range(lax.axis_size('dp...  54.2 us
    ppermute x26, starting transfers between devices, swap(): lax.ppermute(value, 'dp', [(p, p ^ mask) for p in range(lax.axis_size('dp...  33.3 us
    unnamed x130, local copies, waits for them, and re-layouts  22.6 us
    ppermute x9, starting transfers between devices, back(): lax.ppermute(value, 'tensor', [(p, (p - 2 * distance) % size) for p in ra...  21.3 us
    dot_general x3, matrix products, shards(): jnp.einsum('ktf,kdf->td', g, gate_up[:, :, c0 * width:c1 * width], prefer...  8.15 us
  transfers between devices with their start and end apart: 40, of which 20 were waited for; matrix products, arithmetic and copies ran while one was open for 2% of the time, Pallas kernels for 34%

profile of v4, /device:TPU:0, one launch (start us, length us, event | category | flops | bytes accessed | tf_op | source)
XLA Modules:
  0.0 232.7 jit_solution(7777183000536966541)
XLA Ops:
  1.6 4.0 %collective-permute-start.2 = (bf16[32,1024]{1,0:T(8,128)(2,1)S(1)}, bf16[32,1024]{1,0:T(8,128)(2,1)S(1)}, u32[]{:S(2)}, u32[]{:S(2)}) collective-permute-start(bf16[32,1024]{1,0:T(8,128)(2,1)S(1)} %get-tuple-element.90), channel_id=1, source_target_pairs={{0,24},{8,16},{16,8},{24,0},{1,25},{9,17},{17,9},{25,1},{2,26},{10... | collective-permute-start | bytes 196616 | tf_op jit(solution)/shard_map/ppermute | solution.py:20
  6.2 1.6 collective-permute-done.2
  7.8 2.0 collective-permute-done.1
  10.5 1.6 collective-permute-start.3
  12.1 2.6 %collective-permute-start.4 = (bf16[4,32,1024]{2,1,0:T(8,128)(2,1)S(1)}, bf16[4,32,1024]{2,1,0:T(8,128)(2,1)S(1)}, u32[]{:S(2)}, u32[]{:S(2)}) collective-permute-start(bf16[4,32,1024]{2,1,0:T(8,128)(2,1)S(1)} %pad_maximum_fusion.1.refs_0_.refs_2_), channel_id=1, source_target_pairs={{0,4},{1,5},{2,6},{3,7},{4,0},{5,1},{6,2},{7,3},{8,12},{9,13},{10,... | collective-permute-start | bytes 786440 | tf_op jit(solution)/shard_map/ppermute | solution.py:25
  14.7 1.3 collective-permute-start.5
  16.9 5.9 %partial_pre.3 = (bf16[2,256,256]{2,1,0:T(8,128)(2,1)}, f32[3,2,256,256]{3,2,1,0:T(8,128)}, f32[8,128]{1,0:T(8,128)}) custom-call(bf16[256,1024]{1,0:T(8,128)(2,1)} %bitcast.131, bf16[2,1024,1792]{2,1,0:T(8,128)(2,1)} %refs_2_.3), custom_call_target="tpu_custom_call" | custom-call | flops 1 | bytes 1 | tf_op jit(solution)/shard_map/partial_pre/pallas_call | solution.py:114
  25.0 1.5 collective-permute-start.8
  26.5 3.0 %collective-permute-done.7.refs_1_ = bf16[256,256]{1,0:T(8,128)(2,1)S(1)} collective-permute-done((bf16[256,256]{1,0:T(8,128)(2,1)S(1)}, bf16[256,256]{1,0:T(8,128)(2,1)S(1)}, u32[]{:S(2)}, u32[]{:S(2)}) %collective-permute-start.7) | collective-permute-done | bytes 131104 | tf_op jit(solution)/shard_map/ppermute | solution.py:20
  30.0 1.4 copy-done.15
  32.4 1.0 pack.9
  33.9 1.4 collective-permute-start.11
  35.3 1.5 collective-permute-start.12
  37.7 9.3 %hidden_grad.2 = (f32[256,256]{1,0:T(8,128)}, f32[192,256]{1,0:T(8,128)}, f32[8,128]{1,0:T(8,128)}) custom-call(bf16[64,4096]{1,0:T(8,128)(2,1)} %copy-done.26, bf16[1792,4096]{1,0:T(8,128)(2,1)} %refs_1_.9, f32[8,128]{1,0:T(8,128)} %copy-done.43), custom_call_target="tpu_custom_call" | custom-call | flops 1 | bytes 1 | tf_op jit(solution)/shard_map/hidden_grad/pallas_call | solution.py:114
  50.6 5.1 %partial_pre.4 = (bf16[2,768,256]{2,1,0:T(8,128)(2,1)S(1)}, f32[3,2,768,256]{3,2,1,0:T(8,128)S(1)}, f32[8,128]{1,0:T(8,128)S(1)}) custom-call(bf16[768,1024]{1,0:T(8,128)(2,1)S(1)} %bitcast.123, bf16[2,1024,1792]{2,1,0:T(8,128)(2,1)S(1)} %bitcast.116, f32[8,128]{1,0:T(8,128)S(1)} %copy-done.44), custom_call_target="tpu_custom_call" | custom-call | flops 1 | bytes 1 | tf_op jit(solution)/shard_map/partial_pre/pallas_call | solution.py:114
  55.8 1.3 exchange_step.12
  57.7 1.2 collective-permute-start.14
  58.9 5.4 %collective-permute-start.17 = (bf16[32,4096]{1,0:T(8,128)(2,1)S(1)}, bf16[32,4096]{1,0:T(8,128)(2,1)S(1)}, u32[]{:S(2)}, u32[]{:S(2)}) collective-permute-start(bf16[32,4096]{1,0:T(8,128)(2,1)S(1)} %hold.1), channel_id=1, source_target_pairs={{0,2},{1,3},{2,4},{3,5},{4,6},{5,7},{6,0},{7,1},{8,10},{9,11},{10,... | collective-permute-start | bytes 786440 | tf_op jit(solution)/shard_map/ppermute | solution.py:25
  64.4 1.6 collective-permute-start.18
  66.8 6.4 %collective-permute-done.13.refs_1_.refs_3_ = bf16[1280,256]{1,0:T(8,128)(2,1)S(1)} collective-permute-done((bf16[1280,256]{1,0:T(8,128)(2,1)S(1)}, bf16[1280,256]{1,0:T(8,128)(2,1)S(1)}, u32[]{:S(2)}, u32[]{:S(2)}) %collective-permute-start.13) | collective-permute-done | bytes 655392 | tf_op jit(solution)/shard_map/ppermute | solution.py:20
  74.1 1.5 exchange_step.13
  76.4 1.3 collective-permute-start.16
  77.9 4.7 %partial_pre.5 = (bf16[2,768,256]{2,1,0:T(8,128)(2,1)S(1)}, f32[3,2,768,256]{3,2,1,0:T(8,128)S(1)}, f32[8,128]{1,0:T(8,128)S(1)}) custom-call(bf16[1024,1024]{1,0:T(8,128)(2,1)S(1)} %bitcast.128, bf16[2,1024,1792]{2,1,0:T(8,128)(2,1)S(1)} %bitcast.116, f32[8,128]{1,0:T(8,128)S(1)} %get-tuple-element.111.refs_2_), custom_call_target="tpu_custom_call" | custom-call | flops 1 | bytes 1 | tf_op jit(solution)/shard_map/partial_pre/pallas_call | solution.py:114
  82.6 1.0 exchange_step.14
  83.7 1.5 collective-permute-start.21
  87.0 6.7 %hidden_grad.3 = (f32[768,256]{1,0:T(8,128)S(1)}, f32[576,256]{1,0:T(8,128)S(1)}, f32[8,128]{1,0:T(8,128)S(1)}) custom-call(bf16[192,4096]{1,0:T(8,128)(2,1)S(1)} %pack.14.refs_0_, bf16[1792,4096]{1,0:T(8,128)(2,1)S(1)} %bitcast.127, f32[8,128]{1,0:T(8,128)S(1)} %get-tuple-element.114.refs_3_.refs_2_), custom_call_target="tpu_custom_call" | custom-call | flops 1 | bytes 1 | tf_op jit(solution)/shard_map/hidden_grad/pallas_call | solution.py:114
  93.7 5.4 %collective-permute-done.15.refs_2_.refs_3_ = bf16[1792,256]{1,0:T(8,128)(2,1)S(1)} collective-permute-done((bf16[1792,256]{1,0:T(8,128)(2,1)}, bf16[1792,256]{1,0:T(8,128)(2,1)S(1)}, u32[]{:S(2)}, u32[]{:S(2)}) %collective-permute-start.15) | collective-permute-done | bytes 917536 | tf_op jit(solution)/shard_map/ppermute | solution.py:20
  100.6 1.2 collective-permute-start.25
  101.8 1.5 collective-permute-start.26
  103.5 1.3 fusion.2
  104.8 2.7 %collective-permute-done.21.refs_1_ = bf16[768,256]{1,0:T(8,128)(2,1)S(1)} collective-permute-done((bf16[768,256]{1,0:T(8,128)(2,1)}, bf16[768,256]{1,0:T(8,128)(2,1)S(1)}, u32[]{:S(2)}, u32[]{:S(2)}) %collective-permute-start.21) | collective-permute-done | bytes 393248 | tf_op jit(solution)/shard_map/ppermute | solution.py:20
  108.4 1.3 exchange_step.16
  109.7 1.2 collective-permute-start.23
  110.9 1.5 collective-permute-start.24
  112.4 12.0 %collective-permute-done.25.refs_0_.refs_1_ = bf16[1536,256]{1,0:T(8,128)(2,1)S(1)} collective-permute-done((bf16[1536,256]{1,0:T(8,128)(2,1)S(1)}, bf16[1536,256]{1,0:T(8,128)(2,1)S(1)}, u32[]{:S(2)}, u32[]{:S(2)}) %collective-permute-start.25) | collective-permute-done | bytes 786464 | tf_op jit(solution)/shard_map/ppermute | solution.py:20
  127.3 1.2 collective-permute-start.29
  128.4 1.5 collective-permute-start.30
  130.2 1.1 copy-done.38
  131.3 10.1 %collective-permute-done.23.refs_2_ = bf16[1536,256]{1,0:T(8,128)(2,1)} collective-permute-done((bf16[1536,256]{1,0:T(8,128)(2,1)}, bf16[1536,256]{1,0:T(8,128)(2,1)}, u32[]{:S(2)}, u32[]{:S(2)}) %collective-permute-start.23) | collective-permute-done | bytes 786464 | tf_op jit(solution)/shard_map/ppermute | solution.py:20
  142.2 2.3 %copy-done.6 = f32[3,2,768,256]{3,2,1,0:T(8,128)S(1)} copy-done((f32[3,2,768,256]{3,2,1,0:T(8,128)S(1)}, f32[3,2,768,256]{3,2,1,0:T(8,128)}, u32[]{:S(2)}) %copy-start.6) | copy-done | bytes 4718616
  144.5 3.0 %exchange_step.18 = (bf16[1536,256]{1,0:T(8,128)(2,1)}, bf16[1536,256]{1,0:T(8,128)(2,1)S(1)}, bf16[2,768,256]{2,1,0:T(8,128)(2,1)S(1)}, f32[8,128]{1,0:T(8,128)S(1)}) custom-call(f32[3,2,768,256]{3,2,1,0:T(8,128)S(1)} %copy-done.6, f32[768,256]{1,0:T(8,128)S(1)} %bitcast.138, bf16[1536,256]{1,0:T(8,128)(2,1)} %collective-permute-done.23.refs_2_, ...), custom_call_target="tpu_custom_call" | custom-call | flops 1 | bytes 1 | tf_op jit(solution)/shard_map/exchange_step/pallas_call | solution.py:114
  147.5 1.2 collective-permute-start.27
  148.7 1.5 collective-permute-start.28
  150.2 1.5 pre_grad.4
  151.9 3.4 %fusion = f32[768,1024,1]{1,0,2:T(8,128)S(1)} fusion(bf16[2,768,1024]{2,1,0:T(8,128)(2,1)S(1)} %get-tuple-element.138.refs_3_, bf16[2,1024,1792]{2,1,0:T(8,128)(2,1)S(1)} %bitcast.118), kind=kOutput, calls=%fused_computation | convolution fusion | flops 3221225472 | bytes 10485760 | tf_op jit(solution)/shard_map/ktf,kdf->td/dot_general | solution.py:606
  155.4 1.0 slice-done.6
  159.0 9.6 %weight_step.4 = (bf16[2,1024,1792]{2,1,0:T(8,128)(2,1)}, bf16[2,1024,1792]{2,1,0:T(8,128)(2,1)}, bf16[2,1024,1792]{2,1,0:T(8,128)(2,1)}, f32[4,2,64]{2,1,0:T(2,...) custom-call(bf16[256,1024]{1,0:T(8,128)(2,1)S(1)} %bitcast.132, bf16[768,1024]{1,0:T(8,128)(2,1)S(1)} %bitcast.124, ...), custom_call_target="tpu_custom_call" | custom-call | flops 1 | bytes 1 | tf_op jit(solution)/shard_map/weight_step/pallas_call | solution.py:114
  168.7 1.3 collective-permute-start.31
  170.0 1.7 collective-permute-start.32
  171.9 4.6 %collective-permute-done.31.refs_3_ = bf16[768,256]{1,0:T(8,128)(2,1)S(1)} collective-permute-done((bf16[768,256]{1,0:T(8,128)(2,1)S(1)}, bf16[768,256]{1,0:T(8,128)(2,1)S(1)}, u32[]{:S(2)}, u32[]{:S(2)}) %collective-permute-start.31) | collective-permute-done | bytes 393248 | tf_op jit(solution)/shard_map/ppermute | solution.py:20
  176.5 1.2 collective-permute-done.32.refs_4_
  178.0 3.4 %fusion.4 = f32[1024,1024,1]{1,0,2:T(8,128)S(1)} fusion(bf16[2,1024,768]{2,1,0:T(8,128)(2,1)S(1)} %get-tuple-element.144.refs_1_, bf16[2,1024,1792]{2,1,0:T(8,128)(2,1)S(1)} %bitcast.118), kind=kOutput, calls=%fused_computation.4 | convolution fusion | flops 3221225472 | bytes 10485760 | tf_op jit(solution)/shard_map/ktf,kdf->td/dot_general | solution.py:606
  181.9 1.5 copy-done.46
  184.9 1.0 copy-done.47
  186.1 2.6 %collective-permute-done.33 = bf16[4,4,32,1024]{3,2,1,0:T(8,128)(2,1)S(1)} collective-permute-done((bf16[4,4,32,1024]{3,2,1,0:T(8,128)(2,1)S(1)}, bf16[4,4,32,1024]{3,2,1,0:T(8,128)(2,1)S(1)}, u32[]{:S(2)}, u32[]{:S(2)}) %collective-permute-start.33) | collective-permute-done | bytes 1048608 | tf_op jit(solution)/shard_map/ppermute | solution.py:37
  188.8 1.1 fusion.15
  189.9 5.5 %collective-permute-start.36 = (bf16[4,32,1024]{2,1,0:T(8,128)(2,1)}, bf16[4,32,1024]{2,1,0:T(8,128)(2,1)}, u32[]{:S(2)}, u32[]{:S(2)}) collective-permute-start(bf16[4,32,1024]{2,1,0:T(8,128)(2,1)} %get-tuple-element.176), channel_id=1, source_target_pairs={{0,2},{1,3},{2,4},{3,5},{4,6},{5,7},{6,0},{7,1},{8,10},{9,11},{10,... | collective-permute-start | bytes 786440 | tf_op jit(solution)/shard_map/ppermute | solution.py:25
  195.4 1.6 collective-permute-start.35
  197.8 1.9 copy-done.14
  199.7 9.7 %weight_step.5 = (bf16[2,1024,1792]{2,1,0:T(8,128)(2,1)}, bf16[2,1024,1792]{2,1,0:T(8,128)(2,1)}, bf16[2,1024,1792]{2,1,0:T(8,128)(2,1)}, f32[4,2,64]{2,1,0:T(2,...) custom-call(bf16[256,1024]{1,0:T(8,128)(2,1)S(1)} %bitcast.133, ...), custom_call_target="tpu_custom_call", output_to_operand_aliasing={{0}: (9, {}), {1}: (10, {}), {2}: (11, {})} | custom-call | flops 1 | bytes 1 | tf_op jit(solution)/shard_map/weight_step/pallas_call | solution.py:114
  209.4 9.6 %weight_step.6 = (bf16[2,1024,1792]{2,1,0:T(8,128)(2,1)}, bf16[2,1024,1792]{2,1,0:T(8,128)(2,1)}, bf16[2,1024,1792]{2,1,0:T(8,128)(2,1)}, f32[4,2,64]{2,1,0:T(2,...) custom-call(bf16[1024,1024]{1,0:T(8,128)(2,1)S(1)} %bitcast.129, ...), custom_call_target="tpu_custom_call", output_to_operand_aliasing={{0}: (7, {}), {1}: (8, {}), {2}: (9, {})} | custom-call | flops 1 | bytes 1 | tf_op jit(solution)/shard_map/weight_step/pallas_call | solution.py:114
  219.1 1.4 fusion.20.refs_11_
  220.5 2.4 %collective-permute-start.39 = (bf16[32,1024]{1,0:T(8,128)(2,1)S(1)}, bf16[32,1024]{1,0:T(8,128)(2,1)S(1)}, u32[]{:S(2)}, u32[]{:S(2)}) collective-permute-start(bf16[32,1024]{1,0:T(8,128)(2,1)S(1)} %get-tuple-element.183), channel_id=1, source_target_pairs={{0,24},{8,16},{16,8},{24,0},{1,25},{9,17},{17,9},{25,1},{2,26},{10... | collective-permute-start | bytes 196616 | tf_op jit(solution)/shard_map/ppermute | solution.py:20
  224.0 7.2 %weight_step.7 = (bf16[2,1024,1792]{2,1,0:T(8,128)(2,1)}, bf16[2,1024,1792]{2,1,0:T(8,128)(2,1)}, bf16[2,1024,1792]{2,1,0:T(8,128)(2,1)}, f32[2,2,64]{2,1,0:T(2,...) custom-call(bf16[1024,1024]{1,0:T(8,128)(2,1)S(1)} %bitcast.130, ...), custom_call_target="tpu_custom_call", output_to_operand_aliasing={{0}: (7, {}), {1}: (8, {}), {2}: (9, {})} | custom-call | flops 1 | bytes 1 | tf_op jit(solution)/shard_map/weight_step/pallas_call | solution.py:114
  (206 shorter events, 32.1 us)
Async XLA Ops:
  1.6 6.2 %collective-permute-start.2 = (bf16[32,1024]{1,0:T(8,128)(2,1)S(1)}, bf16[32,1024]{1,0:T(8,128)(2,1)S(1)}, u32[]{:S(2)}, u32[]{:S(2)}) collective-permute-start(bf16[32,1024]{1,0:T(8,128)(2,1)S(1)} %get-tuple-element.90), channel_id=1, source_target_pairs={{0,24},{8,16},{16,8},{24,0},{1,25},{9,17},{17,9},{25,1},{2,26},{10... | collective-permute-start | bytes 196616 | tf_op jit(solution)/shard_map/ppermute | solution.py:20
  5.6 4.3 %collective-permute-start.1 = (bf16[32,1024]{1,0:T(8,128)(2,1)S(1)}, bf16[32,1024]{1,0:T(8,128)(2,1)S(1)}, u32[]{:S(2)}, u32[]{:S(2)}) collective-permute-start(bf16[32,1024]{1,0:T(8,128)(2,1)S(1)} %get-tuple-element.89), channel_id=1, source_target_pairs={{0,16},{8,24},{16,0},{24,8},{1,17},{9,25},{17,1},{25,9},{2,18},{10... | collective-permute-start | bytes 196616 | tf_op jit(solution)/shard_map/ppermute | solution.py:20
  6.1 4.3 %collective-permute-start = (bf16[32,1024]{1,0:T(8,128)(2,1)S(1)}, bf16[32,1024]{1,0:T(8,128)(2,1)S(1)}, u32[]{:S(2)}, u32[]{:S(2)}) collective-permute-start(bf16[32,1024]{1,0:T(8,128)(2,1)S(1)} %get-tuple-element.88), channel_id=1, source_target_pairs={{0,8},{8,0},{16,24},{24,16},{1,9},{9,1},{17,25},{25,17},{2,10},{10... | collective-permute-start | bytes 196616 | tf_op jit(solution)/shard_map/ppermute | solution.py:20
  10.4 5.6 %collective-permute-start.6 = (bf16[4,32,1024]{2,1,0:T(8,128)(2,1)S(1)}, bf16[4,32,1024]{2,1,0:T(8,128)(2,1)S(1)}, u32[]{:S(2)}, u32[]{:S(2)}) collective-permute-start(bf16[4,32,1024]{2,1,0:T(8,128)(2,1)S(1)} %pad_maximum_fusion.1.refs_0_.refs_2_), channel_id=1, source_target_pairs={{0,1},{1,0},{2,3},{3,2},{4,5},{5,4},{6,7},{7,6},{8,9},{9,8},{10,11... | collective-permute-start | bytes 786440 | tf_op jit(solution)/shard_map/ppermute | solution.py:37
  10.5 21.8 %collective-permute-start.3 = (bf16[4,32,1024]{2,1,0:T(8,128)(2,1)S(1)}, bf16[4,32,1024]{2,1,0:T(8,128)(2,1)S(1)}, u32[]{:S(2)}, u32[]{:S(2)}) collective-permute-start(bf16[4,32,1024]{2,1,0:T(8,128)(2,1)S(1)} %pad_maximum_fusion.1.refs_0_.refs_2_), channel_id=1, source_target_pairs={{0,2},{1,3},{2,4},{3,5},{4,6},{5,7},{6,0},{7,1},{8,10},{9,11},{10,... | collective-permute-start | bytes 786440 | tf_op jit(solution)/shard_map/ppermute | solution.py:25
  12.1 20.3 %collective-permute-start.4 = (bf16[4,32,1024]{2,1,0:T(8,128)(2,1)S(1)}, bf16[4,32,1024]{2,1,0:T(8,128)(2,1)S(1)}, u32[]{:S(2)}, u32[]{:S(2)}) collective-permute-start(bf16[4,32,1024]{2,1,0:T(8,128)(2,1)S(1)} %pad_maximum_fusion.1.refs_0_.refs_2_), channel_id=1, source_target_pairs={{0,4},{1,5},{2,6},{3,7},{4,0},{5,1},{6,2},{7,3},{8,12},{9,13},{10,... | collective-permute-start | bytes 786440 | tf_op jit(solution)/shard_map/ppermute | solution.py:25
  14.7 17.7 %collective-permute-start.5 = (bf16[4,32,1024]{2,1,0:T(8,128)(2,1)S(1)}, bf16[4,32,1024]{2,1,0:T(8,128)(2,1)S(1)}, u32[]{:S(2)}, u32[]{:S(2)}) collective-permute-start(bf16[4,32,1024]{2,1,0:T(8,128)(2,1)S(1)} %pad_maximum_fusion.1.refs_0_.refs_2_), channel_id=1, source_target_pairs={{0,6},{1,7},{2,0},{3,1},{4,2},{5,3},{6,4},{7,5},{8,14},{9,15},{10,... | collective-permute-start | bytes 786440 | tf_op jit(solution)/shard_map/ppermute | solution.py:25
  16.9 16.5 %copy-start.27 = (bf16[32,4096]{1,0:T(8,128)(2,1)S(1)}, bf16[32,4096]{1,0:T(8,128)(2,1)}, u32[]{:S(2)}) copy-start(bf16[32,4096]{1,0:T(8,128)(2,1)} %value_ref.1) | copy-start | bytes 786436
  24.4 5.1 %collective-permute-start.7 = (bf16[256,256]{1,0:T(8,128)(2,1)S(1)}, bf16[256,256]{1,0:T(8,128)(2,1)S(1)}, u32[]{:S(2)}, u32[]{:S(2)}) collective-permute-start(bf16[256,256]{1,0:T(8,128)(2,1)S(1)} %get-tuple-element.94), channel_id=1, source_target_pairs={{0,8},{8,0},{16,24},{24,16},{1,9},{9,1},{17,25},{25,17},{2,10},{10... | collective-permute-start | bytes 393224 | tf_op jit(solution)/shard_map/ppermute | solution.py:20
  25.0 5.0 %collective-permute-start.8 = (bf16[256,256]{1,0:T(8,128)(2,1)S(1)}, bf16[256,256]{1,0:T(8,128)(2,1)S(1)}, u32[]{:S(2)}, u32[]{:S(2)}) collective-permute-start(bf16[256,256]{1,0:T(8,128)(2,1)S(1)} %get-tuple-element.95), channel_id=1, source_target_pairs={{0,16},{8,24},{16,0},{24,8},{1,17},{9,25},{17,1},{25,9},{2,18},{10... | collective-permute-start | bytes 393224 | tf_op jit(solution)/shard_map/ppermute | solution.py:20
  33.4 13.6 %collective-permute-start.9 = (bf16[4,96,1024]{2,1,0:T(8,128)(2,1)}, bf16[4,96,1024]{2,1,0:T(8,128)(2,1)S(1)}, u32[]{:S(2)}, u32[]{:S(2)}) collective-permute-start(bf16[4,96,1024]{2,1,0:T(8,128)(2,1)} %pack.9), channel_id=1, source_target_pairs={{0,1},{1,0},{2,3},{3,2},{4,5},{5,4},{6,7},{7,6},{8,9},{9,8},{10,11... | collective-permute-start | bytes 2359304 | tf_op jit(solution)/shard_map/ppermute | solution.py:37
  33.4 3.5 %collective-permute-start.10 = (bf16[32,4096]{1,0:T(8,128)(2,1)S(1)}, bf16[32,4096]{1,0:T(8,128)(2,1)S(1)}, u32[]{:S(2)}, u32[]{:S(2)}) collective-permute-start(bf16[32,4096]{1,0:T(8,128)(2,1)S(1)} %copy-done.27), channel_id=1, source_target_pairs={{0,1},{1,0},{2,3},{3,2},{4,5},{5,4},{6,7},{7,6},{8,9},{9,8},{10,11... | collective-permute-start | bytes 786440 | tf_op jit(solution)/shard_map/ppermute | solution.py:37
  33.9 21.8 %collective-permute-start.11 = (bf16[512,256]{1,0:T(8,128)(2,1)}, bf16[512,256]{1,0:T(8,128)(2,1)}, u32[]{:S(2)}, u32[]{:S(2)}) collective-permute-start(bf16[512,256]{1,0:T(8,128)(2,1)} %get-tuple-element.101), channel_id=1, source_target_pairs={{0,8},{8,0},{16,24},{24,16},{1,9},{9,1},{17,25},{25,17},{2,10},{10... | collective-permute-start | bytes 786440 | tf_op jit(solution)/shard_map/ppermute | solution.py:20
  35.3 20.4 %collective-permute-start.12 = (bf16[512,256]{1,0:T(8,128)(2,1)}, bf16[512,256]{1,0:T(8,128)(2,1)}, u32[]{:S(2)}, u32[]{:S(2)}) collective-permute-start(bf16[512,256]{1,0:T(8,128)(2,1)} %get-tuple-element.102), channel_id=1, source_target_pairs={{0,16},{8,24},{16,0},{24,8},{1,17},{9,25},{17,1},{25,9},{2,18},{10... | collective-permute-start | bytes 786440 | tf_op jit(solution)/shard_map/ppermute | solution.py:20
  36.9 13.2 %slice-start = ((s8[7340032]{0:T(1024)(128)(4,1)}), s8[4194304]{0:T(1024)(128)(4,1)S(1)}, s32[]{:S(2)}) async-start(s8[7340032]{0:T(1024)(128)(4,1)} %bitcast.115), calls=%async_computation | async-start | bytes 8388608
  37.7 12.3 %slice-start.1 = ((s8[7340032]{0:T(1024)(128)(4,1)}), s8[3145728]{0:T(1024)(128)(4,1)S(1)}, s32[]{:S(2)}) async-start(s8[7340032]{0:T(1024)(128)(4,1)} %bitcast.115), calls=%async_computation.1 | async-start | bytes 6291456
  50.0 27.7 %copy-start = (bf16[4,192,1024]{2,1,0:T(8,128)(2,1)}, bf16[4,192,1024]{2,1,0:T(8,128)(2,1)S(1)}, u32[]{:S(2)}) copy-start(bf16[4,192,1024]{2,1,0:T(8,128)(2,1)S(1)} %pack.10.refs_1_.refs_2_.refs_3_) | copy-start | bytes 4718596
  50.6 8.3 %copy-start.28 = (bf16[32,4096]{1,0:T(8,128)(2,1)S(1)}, bf16[32,4096]{1,0:T(8,128)(2,1)}, u32[]{:S(2)}) copy-start(bf16[32,4096]{1,0:T(8,128)(2,1)} %value_ref.1) | copy-start | bytes 786436
  57.0 20.7 %copy-start.8 = (bf16[4,64,1024]{2,1,0:T(8,128)(2,1)S(1)}, bf16[4,64,1024]{2,1,0:T(8,128)(2,1)}, u32[]{:S(2)}) copy-start(bf16[4,64,1024]{2,1,0:T(8,128)(2,1)} %copy-done.7) | copy-start | bytes 1572868
  57.1 16.2 %collective-permute-start.13 = (bf16[1280,256]{1,0:T(8,128)(2,1)S(1)}, bf16[1280,256]{1,0:T(8,128)(2,1)S(1)}, u32[]{:S(2)}, u32[]{:S(2)}) collective-permute-start(bf16[1280,256]{1,0:T(8,128)(2,1)S(1)} %get-tuple-element.105), channel_id=1, source_target_pairs={{0,8},{8,0},{16,24},{24,16},{1,9},{9,1},{17,25},{25,17},{2,10},{10... | collective-permute-start | bytes 1966088 | tf_op jit(solution)/shard_map/ppermute | solution.py:20
  57.7 16.4 %collective-permute-start.14 = (bf16[1280,256]{1,0:T(8,128)(2,1)S(1)}, bf16[1280,256]{1,0:T(8,128)(2,1)S(1)}, u32[]{:S(2)}, u32[]{:S(2)}) collective-permute-start(bf16[1280,256]{1,0:T(8,128)(2,1)S(1)} %get-tuple-element.106), channel_id=1, source_target_pairs={{0,16},{8,24},{16,0},{24,8},{1,17},{9,25},{17,1},{25,9},{2,18},{10... | collective-permute-start | bytes 1966088 | tf_op jit(solution)/shard_map/ppermute | solution.py:20
  58.9 24.7 %collective-permute-start.17 = (bf16[32,4096]{1,0:T(8,128)(2,1)S(1)}, bf16[32,4096]{1,0:T(8,128)(2,1)S(1)}, u32[]{:S(2)}, u32[]{:S(2)}) collective-permute-start(bf16[32,4096]{1,0:T(8,128)(2,1)S(1)} %hold.1), channel_id=1, source_target_pairs={{0,2},{1,3},{2,4},{3,5},{4,6},{5,7},{6,0},{7,1},{8,10},{9,11},{10,... | collective-permute-start | bytes 786440 | tf_op jit(solution)/shard_map/ppermute | solution.py:25
  64.4 19.2 %collective-permute-start.18 = (bf16[32,4096]{1,0:T(8,128)(2,1)S(1)}, bf16[32,4096]{1,0:T(8,128)(2,1)S(1)}, u32[]{:S(2)}, u32[]{:S(2)}) collective-permute-start(bf16[32,4096]{1,0:T(8,128)(2,1)S(1)} %hold.1), channel_id=1, source_target_pairs={{0,4},{1,5},{2,6},{3,7},{4,0},{5,1},{6,2},{7,3},{8,12},{9,13},{10,... | collective-permute-start | bytes 786440 | tf_op jit(solution)/shard_map/ppermute | solution.py:25
  66.0 17.6 %collective-permute-start.19 = (bf16[32,4096]{1,0:T(8,128)(2,1)S(1)}, bf16[32,4096]{1,0:T(8,128)(2,1)S(1)}, u32[]{:S(2)}, u32[]{:S(2)}) collective-permute-start(bf16[32,4096]{1,0:T(8,128)(2,1)S(1)} %hold.1), channel_id=1, source_target_pairs={{0,6},{1,7},{2,0},{3,1},{4,2},{5,3},{6,4},{7,5},{8,14},{9,15},{10,... | collective-permute-start | bytes 786440 | tf_op jit(solution)/shard_map/ppermute | solution.py:25
  74.1 12.9 %slice-start.8 = ((s8[14680064]{0:T(1024)(128)(4,1)}), s8[4194304]{0:T(1024)(128)(4,1)S(1)}, s32[]{:S(2)}) async-start(s8[14680064]{0:T(1024)(128)(4,1)} %bitcast.126), calls=%async_computation.8 | async-start | bytes 8388608
  75.6 23.5 %collective-permute-start.15 = (bf16[1792,256]{1,0:T(8,128)(2,1)}, bf16[1792,256]{1,0:T(8,128)(2,1)S(1)}, u32[]{:S(2)}, u32[]{:S(2)}) collective-permute-start(bf16[1792,256]{1,0:T(8,128)(2,1)} %get-tuple-element.109), channel_id=1, source_target_pairs={{0,8},{8,0},{16,24},{24,16},{1,9},{9,1},{17,25},{25,17},{2,10},{10... | collective-permute-start | bytes 2752520 | tf_op jit(solution)/shard_map/ppermute | solution.py:20
  76.4 10.5 %slice-start.9 = ((s8[14680064]{0:T(1024)(128)(4,1)}), s8[4194304]{0:T(1024)(128)(4,1)S(1)}, s32[]{:S(2)}) async-start(s8[14680064]{0:T(1024)(128)(4,1)} %bitcast.126), calls=%async_computation.9 | async-start | bytes 8388608
  76.4 23.5 %collective-permute-start.16 = (bf16[1792,256]{1,0:T(8,128)(2,1)}, bf16[1792,256]{1,0:T(8,128)(2,1)S(1)}, u32[]{:S(2)}, u32[]{:S(2)}) collective-permute-start(bf16[1792,256]{1,0:T(8,128)(2,1)} %get-tuple-element.110), channel_id=1, source_target_pairs={{0,16},{8,24},{16,0},{24,8},{1,17},{9,25},{17,1},{25,9},{2,18},{10... | collective-permute-start | bytes 2752520 | tf_op jit(solution)/shard_map/ppermute | solution.py:20
  77.9 9.1 %slice-start.10 = ((s8[14680064]{0:T(1024)(128)(4,1)}), s8[4194304]{0:T(1024)(128)(4,1)S(1)}, s32[]{:S(2)}) async-start(s8[14680064]{0:T(1024)(128)(4,1)} %bitcast.126), calls=%async_computation.10 | async-start | bytes 8388608
  77.9 9.1 %slice-start.11 = ((s8[14680064]{0:T(1024)(128)(4,1)}), s8[2097152]{0:T(1024)(128)(4,1)S(1)}, s32[]{:S(2)}) async-start(s8[14680064]{0:T(1024)(128)(4,1)} %bitcast.126), calls=%async_computation.11 | async-start | bytes 4194304
  82.6 25.8 %copy-start.5 = (f32[3,2,768,256]{3,2,1,0:T(8,128)}, f32[3,2,768,256]{3,2,1,0:T(8,128)S(1)}, u32[]{:S(2)}) copy-start(f32[3,2,768,256]{3,2,1,0:T(8,128)S(1)} %get-tuple-element.119.refs_0_) | copy-start | bytes 14155780
  83.7 2.4 %collective-permute-start.20 = (bf16[96,4096]{1,0:T(8,128)(2,1)S(1)}, bf16[96,4096]{1,0:T(8,128)(2,1)S(1)}, u32[]{:S(2)}, u32[]{:S(2)}) collective-permute-start(bf16[96,4096]{1,0:T(8,128)(2,1)S(1)} %pack.13), channel_id=1, source_target_pairs={{0,1},{1,0},{2,3},{3,2},{4,5},{5,4},{6,7},{7,6},{8,9},{9,8},{10,11... | collective-permute-start | bytes 2359304 | tf_op jit(solution)/shard_map/ppermute | solution.py:37
  83.7 23.8 %collective-permute-start.21 = (bf16[768,256]{1,0:T(8,128)(2,1)}, bf16[768,256]{1,0:T(8,128)(2,1)S(1)}, u32[]{:S(2)}, u32[]{:S(2)}) collective-permute-start(bf16[768,256]{1,0:T(8,128)(2,1)} %get-tuple-element.122), channel_id=1, source_target_pairs={{0,8},{8,0},{16,24},{24,16},{1,9},{9,1},{17,25},{25,17},{2,10},{10... | collective-permute-start | bytes 1179656 | tf_op jit(solution)/shard_map/ppermute | solution.py:20
  86.1 22.3 %collective-permute-start.22 = (bf16[768,256]{1,0:T(8,128)(2,1)}, bf16[768,256]{1,0:T(8,128)(2,1)S(1)}, u32[]{:S(2)}, u32[]{:S(2)}) collective-permute-start(bf16[768,256]{1,0:T(8,128)(2,1)} %get-tuple-element.123), channel_id=1, source_target_pairs={{0,16},{8,24},{16,0},{24,8},{1,17},{9,25},{17,1},{25,9},{2,18},{10... | collective-permute-start | bytes 1179656 | tf_op jit(solution)/shard_map/ppermute | solution.py:20
  93.7 9.8 %copy-start.37 = (f32[576,256]{1,0:T(8,128)}, f32[576,256]{1,0:T(8,128)S(1)}, u32[]{:S(2)}) copy-start(f32[576,256]{1,0:T(8,128)S(1)} %get-tuple-element.121) | copy-start | bytes 1769476
  100.6 23.8 %collective-permute-start.25 = (bf16[1536,256]{1,0:T(8,128)(2,1)S(1)}, bf16[1536,256]{1,0:T(8,128)(2,1)S(1)}, u32[]{:S(2)}, u32[]{:S(2)}) collective-permute-start(bf16[1536,256]{1,0:T(8,128)(2,1)S(1)} %get-tuple-element.127), channel_id=1, source_target_pairs={{0,8},{8,0},{16,24},{24,16},{1,9},{9,1},{17,25},{25,17},{2,10},{10... | collective-permute-start | bytes 2359304 | tf_op jit(solution)/shard_map/ppermute | solution.py:20
  101.8 23.4 %collective-permute-start.26 = (bf16[1536,256]{1,0:T(8,128)(2,1)S(1)}, bf16[1536,256]{1,0:T(8,128)(2,1)S(1)}, u32[]{:S(2)}, u32[]{:S(2)}) collective-permute-start(bf16[1536,256]{1,0:T(8,128)(2,1)S(1)} %get-tuple-element.128), channel_id=1, source_target_pairs={{0,16},{8,24},{16,0},{24,8},{1,17},{9,25},{17,1},{25,9},{2,18},{10... | collective-permute-start | bytes 2359304 | tf_op jit(solution)/shard_map/ppermute | solution.py:20
  104.8 20.4 %copy-start.20 = (f32[256,1024,1]{1,0,2:T(8,128)}, f32[256,1024,1]{1,0,2:T(8,128)S(1)}, u32[]{:S(2)}) copy-start(f32[256,1024,1]{1,0,2:T(8,128)S(1)} %fusion.2) | copy-start | bytes 3145732
  104.8 25.1 %copy-start.50 = (f32[2,64,14]{1,0,2:T(2,128)S(1)}, f32[2,64,14]{1,0,2:T(2,128)}, u32[]{:S(2)}) copy-start(f32[2,64,14]{1,0,2:T(2,128)} %param.13) | copy-start | bytes 21508
  104.8 25.2 %copy-start.51 = (f32[2,64,14]{1,0,2:T(2,128)S(1)}, f32[2,64,14]{1,0,2:T(2,128)}, u32[]{:S(2)}) copy-start(f32[2,64,14]{1,0,2:T(2,128)} %param.15) | copy-start | bytes 21508
  104.8 25.3 %copy-start.42 = (f32[192,256]{1,0:T(8,128)S(1)}, f32[192,256]{1,0:T(8,128)}, u32[]{:S(2)}) copy-start(f32[192,256]{1,0:T(8,128)} %get-tuple-element.120) | copy-start | bytes 589828
  109.7 31.6 %collective-permute-start.23 = (bf16[1536,256]{1,0:T(8,128)(2,1)}, bf16[1536,256]{1,0:T(8,128)(2,1)}, u32[]{:S(2)}, u32[]{:S(2)}) collective-permute-start(bf16[1536,256]{1,0:T(8,128)(2,1)} %get-tuple-element.125), channel_id=1, source_target_pairs={{0,8},{8,0},{16,24},{24,16},{1,9},{9,1},{17,25},{25,17},{2,10},{10... | collective-permute-start | bytes 2359304 | tf_op jit(solution)/shard_map/ppermute | solution.py:20
  110.9 31.3 %collective-permute-start.24 = (bf16[1536,256]{1,0:T(8,128)(2,1)}, bf16[1536,256]{1,0:T(8,128)(2,1)}, u32[]{:S(2)}, u32[]{:S(2)}) collective-permute-start(bf16[1536,256]{1,0:T(8,128)(2,1)} %get-tuple-element.126), channel_id=1, source_target_pairs={{0,16},{8,24},{16,0},{24,8},{1,17},{9,25},{17,1},{25,9},{2,18},{10... | collective-permute-start | bytes 2359304 | tf_op jit(solution)/shard_map/ppermute | solution.py:20
  125.2 26.6 %slice-start.2 = ((s8[7340032]{0:T(1024)(128)(4,1)}), s8[3145728]{0:T(1024)(128)(4,1)S(1)}, s32[]{:S(2)}) async-start(s8[7340032]{0:T(1024)(128)(4,1)} %bitcast.117), calls=%async_computation.2 | async-start | bytes 6291456
  127.3 23.0 %collective-permute-start.29 = (bf16[768,256]{1,0:T(8,128)(2,1)}, bf16[768,256]{1,0:T(8,128)(2,1)}, u32[]{:S(2)}, u32[]{:S(2)}) collective-permute-start(bf16[768,256]{1,0:T(8,128)(2,1)} %get-tuple-element.135), channel_id=1, source_target_pairs={{0,8},{8,0},{16,24},{24,16},{1,9},{9,1},{17,25},{25,17},{2,10},{10... | collective-permute-start | bytes 1179656 | tf_op jit(solution)/shard_map/ppermute | solution.py:20
  128.4 21.8 %collective-permute-start.30 = (bf16[768,256]{1,0:T(8,128)(2,1)}, bf16[768,256]{1,0:T(8,128)(2,1)}, u32[]{:S(2)}, u32[]{:S(2)}) collective-permute-start(bf16[768,256]{1,0:T(8,128)(2,1)} %get-tuple-element.136), channel_id=1, source_target_pairs={{0,16},{8,24},{16,0},{24,8},{1,17},{9,25},{17,1},{25,9},{2,18},{10... | collective-permute-start | bytes 1179656 | tf_op jit(solution)/shard_map/ppermute | solution.py:20
  144.5 7.3 %slice-start.3 = ((s8[7340032]{0:T(1024)(128)(4,1)}), s8[4194304]{0:T(1024)(128)(4,1)S(1)}, s32[]{:S(2)}) async-start(s8[7340032]{0:T(1024)(128)(4,1)} %bitcast.117), calls=%async_computation.3 | async-start | bytes 8388608
  147.5 21.1 %collective-permute-start.27 = (bf16[1536,256]{1,0:T(8,128)(2,1)}, bf16[1536,256]{1,0:T(8,128)(2,1)S(1)}, u32[]{:S(2)}, u32[]{:S(2)}) collective-permute-start(bf16[1536,256]{1,0:T(8,128)(2,1)} %get-tuple-element.132), channel_id=1, source_target_pairs={{0,8},{8,0},{16,24},{24,16},{1,9},{9,1},{17,25},{25,17},{2,10},{10... | collective-permute-start | bytes 2359304 | tf_op jit(solution)/shard_map/ppermute | solution.py:20
  148.7 19.9 %collective-permute-start.28 = (bf16[1536,256]{1,0:T(8,128)(2,1)S(1)}, bf16[1536,256]{1,0:T(8,128)(2,1)S(1)}, u32[]{:S(2)}, u32[]{:S(2)}) collective-permute-start(bf16[1536,256]{1,0:T(8,128)(2,1)S(1)} %get-tuple-element.133), channel_id=1, source_target_pairs={{0,16},{8,24},{16,0},{24,8},{1,17},{9,25},{17,1},{25,9},{2,18},{10... | collective-permute-start | bytes 2359304 | tf_op jit(solution)/shard_map/ppermute | solution.py:20
  168.7 7.8 %collective-permute-start.31 = (bf16[768,256]{1,0:T(8,128)(2,1)S(1)}, bf16[768,256]{1,0:T(8,128)(2,1)S(1)}, u32[]{:S(2)}, u32[]{:S(2)}) collective-permute-start(bf16[768,256]{1,0:T(8,128)(2,1)S(1)} %get-tuple-element.141), channel_id=1, source_target_pairs={{0,8},{8,0},{16,24},{24,16},{1,9},{9,1},{17,25},{25,17},{2,10},{10... | collective-permute-start | bytes 1179656 | tf_op jit(solution)/shard_map/ppermute | solution.py:20
  170.0 7.8 %collective-permute-start.32 = (bf16[768,256]{1,0:T(8,128)(2,1)S(1)}, bf16[768,256]{1,0:T(8,128)(2,1)S(1)}, u32[]{:S(2)}, u32[]{:S(2)}) collective-permute-start(bf16[768,256]{1,0:T(8,128)(2,1)S(1)} %get-tuple-element.142), channel_id=1, source_target_pairs={{0,16},{8,24},{16,0},{24,8},{1,17},{9,25},{17,1},{25,9},{2,18},{10... | collective-permute-start | bytes 1179656 | tf_op jit(solution)/shard_map/ppermute | solution.py:20
  183.9 13.9 %copy-start.2 = (bf16[4,192,1024]{2,1,0:T(8,128)(2,1)S(1)}, bf16[4,192,1024]{2,1,0:T(8,128)(2,1)}, u32[]{:S(2)}) copy-start(bf16[4,192,1024]{2,1,0:T(8,128)(2,1)} %copy-done) | copy-start | bytes 4718596
  183.9 13.9 %copy-start.10 = (bf16[4,64,1024]{2,1,0:T(8,128)(2,1)S(1)}, bf16[4,64,1024]{2,1,0:T(8,128)(2,1)}, u32[]{:S(2)}) copy-start(bf16[4,64,1024]{2,1,0:T(8,128)(2,1)} %copy-done.7) | copy-start | bytes 1572868
  183.9 13.8 %copy-start.19 = (bf16[2,256,1024]{2,1,0:T(8,128)(2,1)S(1)}, bf16[2,256,1024]{2,1,0:T(8,128)(2,1)}, u32[]{:S(2)}) copy-start(bf16[2,256,1024]{2,1,0:T(8,128)(2,1)} %copy-done.17) | copy-start | bytes 3145732
  186.0 2.7 %collective-permute-start.33 = (bf16[4,4,32,1024]{3,2,1,0:T(8,128)(2,1)S(1)}, bf16[4,4,32,1024]{3,2,1,0:T(8,128)(2,1)S(1)}, u32[]{:S(2)}, u32[]{:S(2)}) collective-permute-start(bf16[4,4,32,1024]{3,2,1,0:T(8,128)(2,1)S(1)} %pad_maximum_fusion), channel_id=1, source_target_pairs={{0,1},{1,0},{2,3},{3,2},{4,5},{5,4},{6,7},{7,6},{8,9},{9,8},{10,11... | collective-permute-start | bytes 3145736 | tf_op jit(solution)/shard_map/ppermute | solution.py:37
  189.9 29.1 %collective-permute-start.36 = (bf16[4,32,1024]{2,1,0:T(8,128)(2,1)}, bf16[4,32,1024]{2,1,0:T(8,128)(2,1)}, u32[]{:S(2)}, u32[]{:S(2)}) collective-permute-start(bf16[4,32,1024]{2,1,0:T(8,128)(2,1)} %get-tuple-element.176), channel_id=1, source_target_pairs={{0,2},{1,3},{2,4},{3,5},{4,6},{5,7},{6,0},{7,1},{8,10},{9,11},{10,... | collective-permute-start | bytes 786440 | tf_op jit(solution)/shard_map/ppermute | solution.py:25
  195.4 23.7 %collective-permute-start.35 = (bf16[4,32,1024]{2,1,0:T(8,128)(2,1)}, bf16[4,32,1024]{2,1,0:T(8,128)(2,1)}, u32[]{:S(2)}, u32[]{:S(2)}) collective-permute-start(bf16[4,32,1024]{2,1,0:T(8,128)(2,1)} %get-tuple-element.177), channel_id=1, source_target_pairs={{0,4},{1,5},{2,6},{3,7},{4,0},{5,1},{6,2},{7,3},{8,12},{9,13},{10,... | collective-permute-start | bytes 786440 | tf_op jit(solution)/shard_map/ppermute | solution.py:25
  197.0 22.1 %collective-permute-start.34 = (bf16[4,32,1024]{2,1,0:T(8,128)(2,1)S(1)}, bf16[4,32,1024]{2,1,0:T(8,128)(2,1)}, u32[]{:S(2)}, u32[]{:S(2)}) collective-permute-start(bf16[4,32,1024]{2,1,0:T(8,128)(2,1)S(1)} %get-tuple-element.175), channel_id=1, source_target_pairs={{0,6},{1,7},{2,0},{3,1},{4,2},{5,3},{6,4},{7,5},{8,14},{9,15},{10,... | collective-permute-start | bytes 786440 | tf_op jit(solution)/shard_map/ppermute | solution.py:25
  199.7 9.7 %copy-start.4 = (bf16[4,256,1024]{2,1,0:T(8,128)(2,1)S(1)}, bf16[4,256,1024]{2,1,0:T(8,128)(2,1)}, u32[]{:S(2)}) copy-start(bf16[4,256,1024]{2,1,0:T(8,128)(2,1)} %copy-done.3) | copy-start | bytes 6291460
  199.7 9.7 %copy-start.12 = (bf16[2,1024,768]{2,1,0:T(8,128)(2,1)S(1)}, bf16[2,1024,768]{2,1,0:T(8,128)(2,1)}, u32[]{:S(2)}) copy-start(bf16[2,1024,768]{2,1,0:T(8,128)(2,1)} %copy-done.11) | copy-start | bytes 9437188
  209.4 9.7 %copy-start.48 = (f32[4,2,32,1024]{3,2,0,1:T(8,128)S(1)}, f32[4,2,32,1024]{3,2,0,1:T(8,128)}, u32[]{:S(2)}) copy-start(f32[4,2,32,1024]{3,2,0,1:T(8,128)} %copy-done.47) | copy-start | bytes 3145732
  220.5 11.4 %collective-permute-start.39 = (bf16[32,1024]{1,0:T(8,128)(2,1)S(1)}, bf16[32,1024]{1,0:T(8,128)(2,1)S(1)}, u32[]{:S(2)}, u32[]{:S(2)}) collective-permute-start(bf16[32,1024]{1,0:T(8,128)(2,1)S(1)} %get-tuple-element.183), channel_id=1, source_target_pairs={{0,24},{8,16},{16,8},{24,0},{1,25},{9,17},{17,9},{25,1},{2,26},{10... | collective-permute-start | bytes 196616 | tf_op jit(solution)/shard_map/ppermute | solution.py:20
  222.9 9.0 %collective-permute-start.38 = (bf16[32,1024]{1,0:T(8,128)(2,1)S(1)}, bf16[32,1024]{1,0:T(8,128)(2,1)S(1)}, u32[]{:S(2)}, u32[]{:S(2)}) collective-permute-start(bf16[32,1024]{1,0:T(8,128)(2,1)S(1)} %get-tuple-element.184), channel_id=1, source_target_pairs={{0,16},{8,24},{16,0},{24,8},{1,17},{9,25},{17,1},{25,9},{2,18},{10... | collective-permute-start | bytes 196616 | tf_op jit(solution)/shard_map/ppermute | solution.py:20
  223.1 8.7 %collective-permute-start.37 = (bf16[32,1024]{1,0:T(8,128)(2,1)S(1)}, bf16[32,1024]{1,0:T(8,128)(2,1)S(1)}, u32[]{:S(2)}, u32[]{:S(2)}) collective-permute-start(bf16[32,1024]{1,0:T(8,128)(2,1)S(1)} %get-tuple-element.185), channel_id=1, source_target_pairs={{0,8},{8,0},{16,24},{24,16},{1,9},{9,1},{17,25},{25,17},{2,10},{10... | collective-permute-start | bytes 196616 | tf_op jit(solution)/shard_map/ppermute | solution.py:20
  (40 other events, 130.0 us)

commit v5 on v4

--- a/solution.py
+++ b/solution.py
@@ -267,7 +267,7 @@
             pltpu.VMEM((4, rows // 16, columns), f32),
             pltpu.VMEM((4, rows // 16, 128), f32),
             pltpu.VMEM((tile, columns), f32),
-            pltpu.VMEM((columns // 64, 64, 128), f32),
+            pltpu.VMEM((columns // 64, 72, 128), f32),
             pltpu.VMEM((3, 2, rows, columns), bf16),
             pltpu.VMEM((3, 2, rows, columns), bf16),
             pltpu.SemaphoreType.DMA((3, 2 * rows // tile)),
@@ -655,7 +655,7 @@
             )
 
         def hidden_first():
-            return hidden_grad(chain, rows_of((0,))[1], down_weight, width, [(0, 2 * own, 0, last), (0, 2 * own, last, chunks)], 56)
+            return hidden_grad(chain, rows_of((0,))[1], down_weight, width, [(0, 2 * own, 0, last), (0, 2 * own, last, chunks)], 52)
 
         def hidden_rest(first, tail):
             n = 2 * own

time: 233 us -> 224 us (0.961)
  Pallas kernels: 81.8 us -> 76.4 us
    pallas_call x22, Pallas kernels: 80.2 us -> 75.8 us  [call(): pl.pallas_call(body, in_specs=list(in_specs) + [anywhere] * held, out_spe...]
    ppermute x26, starting transfers between devices: 33.3 us -> 29.7 us  [swap(): lax.ppermute(value, 'dp', [(p, p ^ mask) for p in range(lax.axis_size('dp...]
    ppermute x26, waiting for transfers between devices: 54.2 us -> 51 us  [swap(): lax.ppermute(value, 'dp', [(p, p ^ mask) for p in range(lax.axis_size('dp...]
    unnamed x130 -> x100, local copies, waits for them, and re-layouts: 22.6 us -> 23.7 us
  transfers between devices with their start and end apart: 40 -> 40, of which waited for: 20 -> 20; matrix products, arithmetic and copies ran while one was open for 2% -> 3% of each run, Pallas kernels for 34% -> 34%
where the time goes in v5:
time: 224 us
  Pallas kernels  76.4 us (34%)
  waiting for transfers between devices  55.7 us (25%)
  starting transfers between devices  53 us (24%)
  local copies, waits for them, and re-layouts  25.1 us (11%)
  matrix products  8.16 us (4%)
  other arithmetic  4.09 us (2%)
    pallas_call x22, Pallas kernels, call(): pl.pallas_call(body, in_specs=list(in_specs) + [anywhere] * held, out_spe...  75.8 us
    ppermute x26, waiting for transfers between devices, swap(): lax.ppermute(value, 'dp', [(p, p ^ mask) for p in range(lax.axis_size('dp...  51 us
    ppermute x26, starting transfers between devices, swap(): lax.ppermute(value, 'dp', [(p, p ^ mask) for p in range(lax.axis_size('dp...  29.7 us
    unnamed x100, local copies, waits for them, and re-layouts  23.7 us
    ppermute x9, starting transfers between devices, back(): lax.ppermute(value, 'tensor', [(p, (p - 2 * distance) % size) for p in ra...  22.6 us
    dot_general x3, matrix products, shards(): jnp.einsum('ktf,kdf->td', g, gate_up[:, :, c0 * width:c1 * width], prefer...  8.16 us
  transfers between devices with their start and end apart: 40, of which 20 were waited for; matrix products, arithmetic and copies ran while one was open for 3% of the time, Pallas kernels for 34%

profile of v5, /device:TPU:0, one launch (start us, length us, event | category | flops | bytes accessed | tf_op | source)
XLA Modules:
  0.0 224.0 jit_solution(7737238435613947295)
XLA Ops:
  0.6 0.9 copy-done.32
  1.6 4.0 %collective-permute-start.2 = (bf16[32,1024]{1,0:T(8,128)(2,1)S(1)}, bf16[32,1024]{1,0:T(8,128)(2,1)S(1)}, u32[]{:S(2)}, u32[]{:S(2)}) collective-permute-start(bf16[32,1024]{1,0:T(8,128)(2,1)S(1)} %get-tuple-element.90), channel_id=1, source_target_pairs={{0,24},{8,16},{16,8},{24,0},{1,25},{9,17},{17,9},{25,1},{2,26},{10... | collective-permute-start | bytes 196616 | tf_op jit(solution)/shard_map/ppermute | solution.py:20
  6.2 1.6 collective-permute-done.2
  7.8 2.0 collective-permute-done.1
  10.5 1.6 collective-permute-start.3
  12.1 2.6 %collective-permute-start.4 = (bf16[4,32,1024]{2,1,0:T(8,128)(2,1)S(1)}, bf16[4,32,1024]{2,1,0:T(8,128)(2,1)S(1)}, u32[]{:S(2)}, u32[]{:S(2)}) collective-permute-start(bf16[4,32,1024]{2,1,0:T(8,128)(2,1)S(1)} %pad_maximum_fusion.1.refs_0_.refs_2_), channel_id=1, source_target_pairs={{0,4},{1,5},{2,6},{3,7},{4,0},{5,1},{6,2},{7,3},{8,12},{9,13},{10,... | collective-permute-start | bytes 786440 | tf_op jit(solution)/shard_map/ppermute | solution.py:25
  14.7 1.3 collective-permute-start.5
  16.9 5.9 %partial_pre.3 = (bf16[2,256,256]{2,1,0:T(8,128)(2,1)}, f32[3,2,256,256]{3,2,1,0:T(8,128)}, f32[8,128]{1,0:T(8,128)}) custom-call(bf16[256,1024]{1,0:T(8,128)(2,1)} %bitcast.129, bf16[2,1024,1792]{2,1,0:T(8,128)(2,1)} %refs_2_.3), custom_call_target="tpu_custom_call" | custom-call | flops 1 | bytes 1 | tf_op jit(solution)/shard_map/partial_pre/pallas_call | solution.py:114
  22.8 0.9 copy-done.33
  25.0 1.5 collective-permute-start.8
  26.5 3.0 %collective-permute-done.7.refs_1_ = bf16[256,256]{1,0:T(8,128)(2,1)S(1)} collective-permute-done((bf16[256,256]{1,0:T(8,128)(2,1)S(1)}, bf16[256,256]{1,0:T(8,128)(2,1)S(1)}, u32[]{:S(2)}, u32[]{:S(2)}) %collective-permute-start.7) | collective-permute-done | bytes 131104 | tf_op jit(solution)/shard_map/ppermute | solution.py:20
  30.0 1.4 copy-done.16
  33.6 1.5 collective-permute-start.12
  35.2 7.0 %hidden_grad.2 = (f32[256,256]{1,0:T(8,128)S(1)}, f32[192,256]{1,0:T(8,128)S(1)}, f32[8,128]{1,0:T(8,128)S(1)}) custom-call(bf16[64,4096]{1,0:T(8,128)(2,1)S(1)} %pack.11.refs_0_, bf16[1792,4096]{1,0:T(8,128)(2,1)} %refs_1_.9, f32[8,128]{1,0:T(8,128)S(1)} %get-tuple-element.97.refs_3_.refs_2_), custom_call_target="tpu_custom_call" | custom-call | flops 1 | bytes 1 | tf_op jit(solution)/shard_map/hidden_grad/pallas_call | solution.py:114
  42.6 5.1 %partial_pre.4 = (bf16[2,768,256]{2,1,0:T(8,128)(2,1)S(1)}, f32[3,2,768,256]{3,2,1,0:T(8,128)S(1)}, f32[8,128]{1,0:T(8,128)S(1)}) custom-call(bf16[768,1024]{1,0:T(8,128)(2,1)S(1)} %bitcast.123, bf16[2,1024,1792]{2,1,0:T(8,128)(2,1)S(1)} %bitcast.116, f32[8,128]{1,0:T(8,128)S(1)} %get-tuple-element.98.refs_2_), custom_call_target="tpu_custom_call" | custom-call | flops 1 | bytes 1 | tf_op jit(solution)/shard_map/partial_pre/pallas_call | solution.py:114
  48.0 1.5 collective-permute-start.13
  50.3 6.1 %collective-permute-start.17 = (bf16[32,4096]{1,0:T(8,128)(2,1)S(1)}, bf16[32,4096]{1,0:T(8,128)(2,1)S(1)}, u32[]{:S(2)}, u32[]{:S(2)}) collective-permute-start(bf16[32,4096]{1,0:T(8,128)(2,1)S(1)} %hold.1), channel_id=1, source_target_pairs={{0,2},{1,3},{2,4},{3,5},{4,6},{5,7},{6,0},{7,1},{8,10},{9,11},{10,... | collective-permute-start | bytes 786440 | tf_op jit(solution)/shard_map/ppermute | solution.py:25
  56.4 1.6 collective-permute-start.18
  58.8 6.1 %collective-permute-done.13.refs_1_.refs_3_ = bf16[1280,256]{1,0:T(8,128)(2,1)S(1)} collective-permute-done((bf16[1280,256]{1,0:T(8,128)(2,1)S(1)}, bf16[1280,256]{1,0:T(8,128)(2,1)S(1)}, u32[]{:S(2)}, u32[]{:S(2)}) %collective-permute-start.13) | collective-permute-done | bytes 655392 | tf_op jit(solution)/shard_map/ppermute | solution.py:20
  65.4 1.1 exchange_step.13
  66.5 1.2 collective-permute-start.15
  67.8 1.5 collective-permute-start.16
  69.4 4.7 %partial_pre.5 = (bf16[2,768,256]{2,1,0:T(8,128)(2,1)S(1)}, f32[3,2,768,256]{3,2,1,0:T(8,128)S(1)}, f32[8,128]{1,0:T(8,128)S(1)}) custom-call(bf16[1024,1024]{1,0:T(8,128)(2,1)S(1)} %bitcast.126, bf16[2,1024,1792]{2,1,0:T(8,128)(2,1)S(1)} %bitcast.116, f32[8,128]{1,0:T(8,128)S(1)} %get-tuple-element.111.refs_2_), custom_call_target="tpu_custom_call" | custom-call | flops 1 | bytes 1 | tf_op jit(solution)/shard_map/partial_pre/pallas_call | solution.py:114
  74.1 1.1 exchange_step.14
  75.4 1.1 collective-permute-start.21
  76.5 1.2 collective-permute-done.20.refs_1_.refs_3_.refs_5_
  78.3 5.2 %copy-done.3 = bf16[1792,4096]{1,0:T(8,128)(2,1)S(1)} copy-done((bf16[1792,4096]{1,0:T(8,128)(2,1)S(1)}, bf16[1792,4096]{1,0:T(8,128)(2,1)}, u32[]{:S(2)}) %copy-start.3) | copy-done | bytes 14680088
  83.5 6.7 %hidden_grad.3 = (f32[768,256]{1,0:T(8,128)S(1)}, f32[576,256]{1,0:T(8,128)S(1)}, f32[8,128]{1,0:T(8,128)S(1)}) custom-call(bf16[192,4096]{1,0:T(8,128)(2,1)S(1)} %pack.14.refs_0_, bf16[1792,4096]{1,0:T(8,128)(2,1)S(1)} %copy-done.3, f32[8,128]{1,0:T(8,128)S(1)} %get-tuple-element.114.refs_3_.refs_2_), custom_call_target="tpu_custom_call" | custom-call | flops 1 | bytes 1 | tf_op jit(solution)/shard_map/hidden_grad/pallas_call | solution.py:114
  92.6 1.3 collective-permute-start.26
  94.1 1.3 fusion.2
  95.4 3.0 %collective-permute-done.21.refs_1_ = bf16[768,256]{1,0:T(8,128)(2,1)S(1)} collective-permute-done((bf16[768,256]{1,0:T(8,128)(2,1)}, bf16[768,256]{1,0:T(8,128)(2,1)S(1)}, u32[]{:S(2)}, u32[]{:S(2)}) %collective-permute-start.21) | collective-permute-done | bytes 393248 | tf_op jit(solution)/shard_map/ppermute | solution.py:20
  98.5 1.0 collective-permute-done.22.refs_2_
  99.5 1.3 exchange_step.16
  101.6 1.3 collective-permute-start.24
  103.0 12.4 %collective-permute-done.25.refs_0_.refs_1_ = bf16[1536,256]{1,0:T(8,128)(2,1)S(1)} collective-permute-done((bf16[1536,256]{1,0:T(8,128)(2,1)S(1)}, bf16[1536,256]{1,0:T(8,128)(2,1)S(1)}, u32[]{:S(2)}, u32[]{:S(2)}) %collective-permute-start.25) | collective-permute-done | bytes 786464 | tf_op jit(solution)/shard_map/ppermute | solution.py:20
  115.3 1.0 collective-permute-done.26.refs_1_.refs_2_
  116.3 0.9 exchange_step.17
  119.2 1.3 collective-permute-start.30
  120.7 1.1 copy-done.31
  121.8 10.4 %collective-permute-done.23.refs_2_ = bf16[1536,256]{1,0:T(8,128)(2,1)} collective-permute-done((bf16[1536,256]{1,0:T(8,128)(2,1)}, bf16[1536,256]{1,0:T(8,128)(2,1)}, u32[]{:S(2)}, u32[]{:S(2)}) %collective-permute-start.23) | collective-permute-done | bytes 786464 | tf_op jit(solution)/shard_map/ppermute | solution.py:20
  132.3 1.0 collective-permute-done.24.refs_3_
  133.3 2.3 %copy-done.7 = f32[3,2,768,256]{3,2,1,0:T(8,128)S(1)} copy-done((f32[3,2,768,256]{3,2,1,0:T(8,128)S(1)}, f32[3,2,768,256]{3,2,1,0:T(8,128)}, u32[]{:S(2)}) %copy-start.7) | copy-done | bytes 4718616
  135.6 2.9 %exchange_step.18 = (bf16[1536,256]{1,0:T(8,128)(2,1)}, bf16[1536,256]{1,0:T(8,128)(2,1)S(1)}, bf16[2,768,256]{2,1,0:T(8,128)(2,1)S(1)}, f32[8,128]{1,0:T(8,128)S(1)}) custom-call(f32[3,2,768,256]{3,2,1,0:T(8,128)S(1)} %copy-done.7, f32[768,256]{1,0:T(8,128)S(1)} %bitcast.136, bf16[1536,256]{1,0:T(8,128)(2,1)} %collective-permute-done.23.refs_2_, ...), custom_call_target="tpu_custom_call" | custom-call | flops 1 | bytes 1 | tf_op jit(solution)/shard_map/exchange_step/pallas_call | solution.py:114
  139.4 1.3 collective-permute-start.28
  141.5 1.5 pre_grad.4
  143.2 3.4 %fusion = f32[768,1024,1]{1,0,2:T(8,128)S(1)} fusion(bf16[2,768,1024]{2,1,0:T(8,128)(2,1)S(1)} %get-tuple-element.138.refs_3_, bf16[2,1024,1792]{2,1,0:T(8,128)(2,1)S(1)} %bitcast.118), kind=kOutput, calls=%fused_computation | convolution fusion | flops 3221225472 | bytes 10485760 | tf_op jit(solution)/shard_map/ktf,kdf->td/dot_general | solution.py:606
  146.6 1.0 slice-done.6
  148.5 0.9 slice-done.7
  150.3 9.6 %weight_step.4 = (bf16[2,1024,1792]{2,1,0:T(8,128)(2,1)}, bf16[2,1024,1792]{2,1,0:T(8,128)(2,1)}, bf16[2,1024,1792]{2,1,0:T(8,128)(2,1)}, f32[4,2,64]{2,1,0:T(2,...) custom-call(bf16[256,1024]{1,0:T(8,128)(2,1)S(1)} %bitcast.130, bf16[768,1024]{1,0:T(8,128)(2,1)S(1)} %bitcast.124, ...), custom_call_target="tpu_custom_call" | custom-call | flops 1 | bytes 1 | tf_op jit(solution)/shard_map/weight_step/pallas_call | solution.py:114
  160.7 1.3 collective-permute-start.32
  162.2 5.6 %collective-permute-done.31.refs_3_ = bf16[768,256]{1,0:T(8,128)(2,1)S(1)} collective-permute-done((bf16[768,256]{1,0:T(8,128)(2,1)S(1)}, bf16[768,256]{1,0:T(8,128)(2,1)S(1)}, u32[]{:S(2)}, u32[]{:S(2)}) %collective-permute-start.31) | collective-permute-done | bytes 393248 | tf_op jit(solution)/shard_map/ppermute | solution.py:20
  168.7 3.4 %fusion.4 = f32[1024,1024,1]{1,0,2:T(8,128)S(1)} fusion(bf16[2,1024,768]{2,1,0:T(8,128)(2,1)S(1)} %get-tuple-element.144.refs_1_, bf16[2,1024,1792]{2,1,0:T(8,128)(2,1)S(1)} %bitcast.118), kind=kOutput, calls=%fused_computation.4 | convolution fusion | flops 3221225472 | bytes 10485760 | tf_op jit(solution)/shard_map/ktf,kdf->td/dot_general | solution.py:606
  172.6 1.5 copy-done.35
  175.6 1.0 copy-done.36
  176.8 2.6 %collective-permute-done.33 = bf16[4,4,32,1024]{3,2,1,0:T(8,128)(2,1)S(1)} collective-permute-done((bf16[4,4,32,1024]{3,2,1,0:T(8,128)(2,1)S(1)}, bf16[4,4,32,1024]{3,2,1,0:T(8,128)(2,1)S(1)}, u32[]{:S(2)}, u32[]{:S(2)}) %collective-permute-start.33) | collective-permute-done | bytes 1048608 | tf_op jit(solution)/shard_map/ppermute | solution.py:37
  179.5 1.1 fusion.15
  180.6 6.1 %collective-permute-start.36 = (bf16[4,32,1024]{2,1,0:T(8,128)(2,1)}, bf16[4,32,1024]{2,1,0:T(8,128)(2,1)}, u32[]{:S(2)}, u32[]{:S(2)}) collective-permute-start(bf16[4,32,1024]{2,1,0:T(8,128)(2,1)} %get-tuple-element.176), channel_id=1, source_target_pairs={{0,2},{1,3},{2,4},{3,5},{4,6},{5,7},{6,0},{7,1},{8,10},{9,11},{10,... | collective-permute-start | bytes 786440 | tf_op jit(solution)/shard_map/ppermute | solution.py:25
  186.7 1.6 collective-permute-start.35
  189.1 1.9 copy-done.15
  191.0 9.7 %weight_step.5 = (bf16[2,1024,1792]{2,1,0:T(8,128)(2,1)}, bf16[2,1024,1792]{2,1,0:T(8,128)(2,1)}, bf16[2,1024,1792]{2,1,0:T(8,128)(2,1)}, f32[4,2,64]{2,1,0:T(2,...) custom-call(bf16[256,1024]{1,0:T(8,128)(2,1)S(1)} %bitcast.131, ...), custom_call_target="tpu_custom_call", output_to_operand_aliasing={{0}: (9, {}), {1}: (10, {}), {2}: (11, {})} | custom-call | flops 1 | bytes 1 | tf_op jit(solution)/shard_map/weight_step/pallas_call | solution.py:114
  200.7 9.6 %weight_step.6 = (bf16[2,1024,1792]{2,1,0:T(8,128)(2,1)}, bf16[2,1024,1792]{2,1,0:T(8,128)(2,1)}, bf16[2,1024,1792]{2,1,0:T(8,128)(2,1)}, f32[4,2,64]{2,1,0:T(2,...) custom-call(bf16[1024,1024]{1,0:T(8,128)(2,1)S(1)} %bitcast.127, ...), custom_call_target="tpu_custom_call", output_to_operand_aliasing={{0}: (7, {}), {1}: (8, {}), {2}: (9, {})} | custom-call | flops 1 | bytes 1 | tf_op jit(solution)/shard_map/weight_step/pallas_call | solution.py:114
  210.4 1.4 fusion.20.refs_11_
  211.8 2.4 %collective-permute-start.39 = (bf16[32,1024]{1,0:T(8,128)(2,1)S(1)}, bf16[32,1024]{1,0:T(8,128)(2,1)S(1)}, u32[]{:S(2)}, u32[]{:S(2)}) collective-permute-start(bf16[32,1024]{1,0:T(8,128)(2,1)S(1)} %get-tuple-element.183), channel_id=1, source_target_pairs={{0,24},{8,16},{16,8},{24,0},{1,25},{9,17},{17,9},{25,1},{2,26},{10... | collective-permute-start | bytes 196616 | tf_op jit(solution)/shard_map/ppermute | solution.py:20
  215.4 7.2 %weight_step.7 = (bf16[2,1024,1792]{2,1,0:T(8,128)(2,1)}, bf16[2,1024,1792]{2,1,0:T(8,128)(2,1)}, bf16[2,1024,1792]{2,1,0:T(8,128)(2,1)}, f32[2,2,64]{2,1,0:T(2,...) custom-call(bf16[1024,1024]{1,0:T(8,128)(2,1)S(1)} %bitcast.128, ...), custom_call_target="tpu_custom_call", output_to_operand_aliasing={{0}: (7, {}), {1}: (8, {}), {2}: (9, {})} | custom-call | flops 1 | bytes 1 | tf_op jit(solution)/shard_map/weight_step/pallas_call | solution.py:114
  (175 shorter events, 26.0 us)
Async XLA Ops:
  1.6 6.2 %collective-permute-start.2 = (bf16[32,1024]{1,0:T(8,128)(2,1)S(1)}, bf16[32,1024]{1,0:T(8,128)(2,1)S(1)}, u32[]{:S(2)}, u32[]{:S(2)}) collective-permute-start(bf16[32,1024]{1,0:T(8,128)(2,1)S(1)} %get-tuple-element.90), channel_id=1, source_target_pairs={{0,24},{8,16},{16,8},{24,0},{1,25},{9,17},{17,9},{25,1},{2,26},{10... | collective-permute-start | bytes 196616 | tf_op jit(solution)/shard_map/ppermute | solution.py:20
  5.6 4.3 %collective-permute-start.1 = (bf16[32,1024]{1,0:T(8,128)(2,1)S(1)}, bf16[32,1024]{1,0:T(8,128)(2,1)S(1)}, u32[]{:S(2)}, u32[]{:S(2)}) collective-permute-start(bf16[32,1024]{1,0:T(8,128)(2,1)S(1)} %get-tuple-element.89), channel_id=1, source_target_pairs={{0,16},{8,24},{16,0},{24,8},{1,17},{9,25},{17,1},{25,9},{2,18},{10... | collective-permute-start | bytes 196616 | tf_op jit(solution)/shard_map/ppermute | solution.py:20
  6.1 4.3 %collective-permute-start = (bf16[32,1024]{1,0:T(8,128)(2,1)S(1)}, bf16[32,1024]{1,0:T(8,128)(2,1)S(1)}, u32[]{:S(2)}, u32[]{:S(2)}) collective-permute-start(bf16[32,1024]{1,0:T(8,128)(2,1)S(1)} %get-tuple-element.88), channel_id=1, source_target_pairs={{0,8},{8,0},{16,24},{24,16},{1,9},{9,1},{17,25},{25,17},{2,10},{10... | collective-permute-start | bytes 196616 | tf_op jit(solution)/shard_map/ppermute | solution.py:20
  10.4 5.6 %collective-permute-start.6 = (bf16[4,32,1024]{2,1,0:T(8,128)(2,1)S(1)}, bf16[4,32,1024]{2,1,0:T(8,128)(2,1)S(1)}, u32[]{:S(2)}, u32[]{:S(2)}) collective-permute-start(bf16[4,32,1024]{2,1,0:T(8,128)(2,1)S(1)} %pad_maximum_fusion.1.refs_0_.refs_2_), channel_id=1, source_target_pairs={{0,1},{1,0},{2,3},{3,2},{4,5},{5,4},{6,7},{7,6},{8,9},{9,8},{10,11... | collective-permute-start | bytes 786440 | tf_op jit(solution)/shard_map/ppermute | solution.py:37
  10.5 21.0 %collective-permute-start.3 = (bf16[4,32,1024]{2,1,0:T(8,128)(2,1)S(1)}, bf16[4,32,1024]{2,1,0:T(8,128)(2,1)S(1)}, u32[]{:S(2)}, u32[]{:S(2)}) collective-permute-start(bf16[4,32,1024]{2,1,0:T(8,128)(2,1)S(1)} %pad_maximum_fusion.1.refs_0_.refs_2_), channel_id=1, source_target_pairs={{0,2},{1,3},{2,4},{3,5},{4,6},{5,7},{6,0},{7,1},{8,10},{9,11},{10,... | collective-permute-start | bytes 786440 | tf_op jit(solution)/shard_map/ppermute | solution.py:25
  12.1 20.3 %collective-permute-start.4 = (bf16[4,32,1024]{2,1,0:T(8,128)(2,1)S(1)}, bf16[4,32,1024]{2,1,0:T(8,128)(2,1)S(1)}, u32[]{:S(2)}, u32[]{:S(2)}) collective-permute-start(bf16[4,32,1024]{2,1,0:T(8,128)(2,1)S(1)} %pad_maximum_fusion.1.refs_0_.refs_2_), channel_id=1, source_target_pairs={{0,4},{1,5},{2,6},{3,7},{4,0},{5,1},{6,2},{7,3},{8,12},{9,13},{10,... | collective-permute-start | bytes 786440 | tf_op jit(solution)/shard_map/ppermute | solution.py:25
  14.7 17.7 %collective-permute-start.5 = (bf16[4,32,1024]{2,1,0:T(8,128)(2,1)S(1)}, bf16[4,32,1024]{2,1,0:T(8,128)(2,1)S(1)}, u32[]{:S(2)}, u32[]{:S(2)}) collective-permute-start(bf16[4,32,1024]{2,1,0:T(8,128)(2,1)S(1)} %pad_maximum_fusion.1.refs_0_.refs_2_), channel_id=1, source_target_pairs={{0,6},{1,7},{2,0},{3,1},{4,2},{5,3},{6,4},{7,5},{8,14},{9,15},{10,... | collective-permute-start | bytes 786440 | tf_op jit(solution)/shard_map/ppermute | solution.py:25
  16.9 15.6 %copy-start.27 = (bf16[32,4096]{1,0:T(8,128)(2,1)S(1)}, bf16[32,4096]{1,0:T(8,128)(2,1)}, u32[]{:S(2)}) copy-start(bf16[32,4096]{1,0:T(8,128)(2,1)} %value_ref.1) | copy-start | bytes 786436
  24.4 5.1 %collective-permute-start.7 = (bf16[256,256]{1,0:T(8,128)(2,1)S(1)}, bf16[256,256]{1,0:T(8,128)(2,1)S(1)}, u32[]{:S(2)}, u32[]{:S(2)}) collective-permute-start(bf16[256,256]{1,0:T(8,128)(2,1)S(1)} %get-tuple-element.94), channel_id=1, source_target_pairs={{0,8},{8,0},{16,24},{24,16},{1,9},{9,1},{17,25},{25,17},{2,10},{10... | collective-permute-start | bytes 393224 | tf_op jit(solution)/shard_map/ppermute | solution.py:20
  25.0 5.0 %collective-permute-start.8 = (bf16[256,256]{1,0:T(8,128)(2,1)S(1)}, bf16[256,256]{1,0:T(8,128)(2,1)S(1)}, u32[]{:S(2)}, u32[]{:S(2)}) collective-permute-start(bf16[256,256]{1,0:T(8,128)(2,1)S(1)} %get-tuple-element.95), channel_id=1, source_target_pairs={{0,16},{8,24},{16,0},{24,8},{1,17},{9,25},{17,1},{25,9},{2,18},{10... | collective-permute-start | bytes 393224 | tf_op jit(solution)/shard_map/ppermute | solution.py:20
  32.4 9.8 %collective-permute-start.9 = (bf16[4,96,1024]{2,1,0:T(8,128)(2,1)S(1)}, bf16[4,96,1024]{2,1,0:T(8,128)(2,1)S(1)}, u32[]{:S(2)}, u32[]{:S(2)}) collective-permute-start(bf16[4,96,1024]{2,1,0:T(8,128)(2,1)S(1)} %pack.9), channel_id=1, source_target_pairs={{0,1},{1,0},{2,3},{3,2},{4,5},{5,4},{6,7},{7,6},{8,9},{9,8},{10,11... | collective-permute-start | bytes 2359304 | tf_op jit(solution)/shard_map/ppermute | solution.py:37
  32.5 2.6 %collective-permute-start.10 = (bf16[32,4096]{1,0:T(8,128)(2,1)S(1)}, bf16[32,4096]{1,0:T(8,128)(2,1)S(1)}, u32[]{:S(2)}, u32[]{:S(2)}) collective-permute-start(bf16[32,4096]{1,0:T(8,128)(2,1)S(1)} %copy-done.27), channel_id=1, source_target_pairs={{0,1},{1,0},{2,3},{3,2},{4,5},{5,4},{6,7},{7,6},{8,9},{9,8},{10,11... | collective-permute-start | bytes 786440 | tf_op jit(solution)/shard_map/ppermute | solution.py:37
  33.0 14.7 %collective-permute-start.11 = (bf16[512,256]{1,0:T(8,128)(2,1)S(1)}, bf16[512,256]{1,0:T(8,128)(2,1)S(1)}, u32[]{:S(2)}, u32[]{:S(2)}) collective-permute-start(bf16[512,256]{1,0:T(8,128)(2,1)S(1)} %get-tuple-element.101), channel_id=1, source_target_pairs={{0,8},{8,0},{16,24},{24,16},{1,9},{9,1},{17,25},{25,17},{2,10},{10... | collective-permute-start | bytes 786440 | tf_op jit(solution)/shard_map/ppermute | solution.py:20
  33.6 14.1 %collective-permute-start.12 = (bf16[512,256]{1,0:T(8,128)(2,1)S(1)}, bf16[512,256]{1,0:T(8,128)(2,1)S(1)}, u32[]{:S(2)}, u32[]{:S(2)}) collective-permute-start(bf16[512,256]{1,0:T(8,128)(2,1)S(1)} %get-tuple-element.102), channel_id=1, source_target_pairs={{0,16},{8,24},{16,0},{24,8},{1,17},{9,25},{17,1},{25,9},{2,18},{10... | collective-permute-start | bytes 786440 | tf_op jit(solution)/shard_map/ppermute | solution.py:20
  35.2 7.2 %slice-start = ((s8[7340032]{0:T(1024)(128)(4,1)}), s8[4194304]{0:T(1024)(128)(4,1)S(1)}, s32[]{:S(2)}) async-start(s8[7340032]{0:T(1024)(128)(4,1)} %bitcast.115), calls=%async_computation | async-start | bytes 8388608
  35.2 7.4 %slice-start.1 = ((s8[7340032]{0:T(1024)(128)(4,1)}), s8[3145728]{0:T(1024)(128)(4,1)S(1)}, s32[]{:S(2)}) async-start(s8[7340032]{0:T(1024)(128)(4,1)} %bitcast.115), calls=%async_computation.1 | async-start | bytes 6291456
  42.4 26.9 %copy-start = (bf16[4,192,1024]{2,1,0:T(8,128)(2,1)}, bf16[4,192,1024]{2,1,0:T(8,128)(2,1)S(1)}, u32[]{:S(2)}) copy-start(bf16[4,192,1024]{2,1,0:T(8,128)(2,1)S(1)} %pack.10.refs_1_.refs_2_.refs_3_) | copy-start | bytes 4718596
  48.0 21.3 %copy-start.9 = (bf16[4,64,1024]{2,1,0:T(8,128)(2,1)S(1)}, bf16[4,64,1024]{2,1,0:T(8,128)(2,1)}, u32[]{:S(2)}) copy-start(bf16[4,64,1024]{2,1,0:T(8,128)(2,1)} %copy-done.8) | copy-start | bytes 1572868
  48.0 16.8 %collective-permute-start.13 = (bf16[1280,256]{1,0:T(8,128)(2,1)S(1)}, bf16[1280,256]{1,0:T(8,128)(2,1)S(1)}, u32[]{:S(2)}, u32[]{:S(2)}) collective-permute-start(bf16[1280,256]{1,0:T(8,128)(2,1)S(1)} %get-tuple-element.105), channel_id=1, source_target_pairs={{0,8},{8,0},{16,24},{24,16},{1,9},{9,1},{17,25},{25,17},{2,10},{10... | collective-permute-start | bytes 1966088 | tf_op jit(solution)/shard_map/ppermute | solution.py:20
  49.5 15.9 %collective-permute-start.14 = (bf16[1280,256]{1,0:T(8,128)(2,1)S(1)}, bf16[1280,256]{1,0:T(8,128)(2,1)S(1)}, u32[]{:S(2)}, u32[]{:S(2)}) collective-permute-start(bf16[1280,256]{1,0:T(8,128)(2,1)S(1)} %get-tuple-element.106), channel_id=1, source_target_pairs={{0,16},{8,24},{16,0},{24,8},{1,17},{9,25},{17,1},{25,9},{2,18},{10... | collective-permute-start | bytes 1966088 | tf_op jit(solution)/shard_map/ppermute | solution.py:20
  50.3 25.0 %collective-permute-start.17 = (bf16[32,4096]{1,0:T(8,128)(2,1)S(1)}, bf16[32,4096]{1,0:T(8,128)(2,1)S(1)}, u32[]{:S(2)}, u32[]{:S(2)}) collective-permute-start(bf16[32,4096]{1,0:T(8,128)(2,1)S(1)} %hold.1), channel_id=1, source_target_pairs={{0,2},{1,3},{2,4},{3,5},{4,6},{5,7},{6,0},{7,1},{8,10},{9,11},{10,... | collective-permute-start | bytes 786440 | tf_op jit(solution)/shard_map/ppermute | solution.py:25
  56.4 18.9 %collective-permute-start.18 = (bf16[32,4096]{1,0:T(8,128)(2,1)S(1)}, bf16[32,4096]{1,0:T(8,128)(2,1)S(1)}, u32[]{:S(2)}, u32[]{:S(2)}) collective-permute-start(bf16[32,4096]{1,0:T(8,128)(2,1)S(1)} %hold.1), channel_id=1, source_target_pairs={{0,4},{1,5},{2,6},{3,7},{4,0},{5,1},{6,2},{7,3},{8,12},{9,13},{10,... | collective-permute-start | bytes 786440 | tf_op jit(solution)/shard_map/ppermute | solution.py:25
  57.9 17.3 %collective-permute-start.19 = (bf16[32,4096]{1,0:T(8,128)(2,1)S(1)}, bf16[32,4096]{1,0:T(8,128)(2,1)S(1)}, u32[]{:S(2)}, u32[]{:S(2)}) collective-permute-start(bf16[32,4096]{1,0:T(8,128)(2,1)S(1)} %hold.1), channel_id=1, source_target_pairs={{0,6},{1,7},{2,0},{3,1},{4,2},{5,3},{6,4},{7,5},{8,14},{9,15},{10,... | collective-permute-start | bytes 786440 | tf_op jit(solution)/shard_map/ppermute | solution.py:25
  66.5 23.7 %collective-permute-start.15 = (bf16[1792,256]{1,0:T(8,128)(2,1)}, bf16[1792,256]{1,0:T(8,128)(2,1)S(1)}, u32[]{:S(2)}, u32[]{:S(2)}) collective-permute-start(bf16[1792,256]{1,0:T(8,128)(2,1)} %get-tuple-element.109), channel_id=1, source_target_pairs={{0,8},{8,0},{16,24},{24,16},{1,9},{9,1},{17,25},{25,17},{2,10},{10... | collective-permute-start | bytes 2752520 | tf_op jit(solution)/shard_map/ppermute | solution.py:20
  67.8 23.3 %collective-permute-start.16 = (bf16[1792,256]{1,0:T(8,128)(2,1)S(1)}, bf16[1792,256]{1,0:T(8,128)(2,1)S(1)}, u32[]{:S(2)}, u32[]{:S(2)}) collective-permute-start(bf16[1792,256]{1,0:T(8,128)(2,1)S(1)} %get-tuple-element.110), channel_id=1, source_target_pairs={{0,16},{8,24},{16,0},{24,8},{1,17},{9,25},{17,1},{25,9},{2,18},{10... | collective-permute-start | bytes 2752520 | tf_op jit(solution)/shard_map/ppermute | solution.py:20
  74.1 25.4 %copy-start.6 = (f32[3,2,768,256]{3,2,1,0:T(8,128)}, f32[3,2,768,256]{3,2,1,0:T(8,128)S(1)}, u32[]{:S(2)}) copy-start(f32[3,2,768,256]{3,2,1,0:T(8,128)S(1)} %get-tuple-element.119.refs_0_) | copy-start | bytes 14155780
  75.3 2.4 %collective-permute-start.20 = (bf16[96,4096]{1,0:T(8,128)(2,1)S(1)}, bf16[96,4096]{1,0:T(8,128)(2,1)S(1)}, u32[]{:S(2)}, u32[]{:S(2)}) collective-permute-start(bf16[96,4096]{1,0:T(8,128)(2,1)S(1)} %pack.13), channel_id=1, source_target_pairs={{0,1},{1,0},{2,3},{3,2},{4,5},{5,4},{6,7},{7,6},{8,9},{9,8},{10,11... | collective-permute-start | bytes 2359304 | tf_op jit(solution)/shard_map/ppermute | solution.py:37
  75.4 23.1 %collective-permute-start.21 = (bf16[768,256]{1,0:T(8,128)(2,1)}, bf16[768,256]{1,0:T(8,128)(2,1)S(1)}, u32[]{:S(2)}, u32[]{:S(2)}) collective-permute-start(bf16[768,256]{1,0:T(8,128)(2,1)} %get-tuple-element.122), channel_id=1, source_target_pairs={{0,8},{8,0},{16,24},{24,16},{1,9},{9,1},{17,25},{25,17},{2,10},{10... | collective-permute-start | bytes 1179656 | tf_op jit(solution)/shard_map/ppermute | solution.py:20
  77.8 21.7 %collective-permute-start.22 = (bf16[768,256]{1,0:T(8,128)(2,1)}, bf16[768,256]{1,0:T(8,128)(2,1)S(1)}, u32[]{:S(2)}, u32[]{:S(2)}) collective-permute-start(bf16[768,256]{1,0:T(8,128)(2,1)} %get-tuple-element.123), channel_id=1, source_target_pairs={{0,16},{8,24},{16,0},{24,8},{1,17},{9,25},{17,1},{25,9},{2,18},{10... | collective-permute-start | bytes 1179656 | tf_op jit(solution)/shard_map/ppermute | solution.py:20
  91.7 23.6 %collective-permute-start.25 = (bf16[1536,256]{1,0:T(8,128)(2,1)S(1)}, bf16[1536,256]{1,0:T(8,128)(2,1)S(1)}, u32[]{:S(2)}, u32[]{:S(2)}) collective-permute-start(bf16[1536,256]{1,0:T(8,128)(2,1)S(1)} %get-tuple-element.127), channel_id=1, source_target_pairs={{0,8},{8,0},{16,24},{24,16},{1,9},{9,1},{17,25},{25,17},{2,10},{10... | collective-permute-start | bytes 2359304 | tf_op jit(solution)/shard_map/ppermute | solution.py:20
  92.6 23.8 %collective-permute-start.26 = (bf16[1536,256]{1,0:T(8,128)(2,1)S(1)}, bf16[1536,256]{1,0:T(8,128)(2,1)S(1)}, u32[]{:S(2)}, u32[]{:S(2)}) collective-permute-start(bf16[1536,256]{1,0:T(8,128)(2,1)S(1)} %get-tuple-element.128), channel_id=1, source_target_pairs={{0,16},{8,24},{16,0},{24,8},{1,17},{9,25},{17,1},{25,9},{2,18},{10... | collective-permute-start | bytes 2359304 | tf_op jit(solution)/shard_map/ppermute | solution.py:20
  94.1 6.7 %copy-start.18 = (bf16[2,256,1024]{2,1,0:T(8,128)(2,1)}, bf16[2,256,1024]{2,1,0:T(8,128)(2,1)S(1)}, u32[]{:S(2)}) copy-start(bf16[2,256,1024]{2,1,0:T(8,128)(2,1)S(1)} %get-tuple-element.118.refs_2_) | copy-start | bytes 3145732
  95.4 21.0 %copy-start.21 = (f32[256,1024,1]{1,0,2:T(8,128)}, f32[256,1024,1]{1,0,2:T(8,128)S(1)}, u32[]{:S(2)}) copy-start(f32[256,1024,1]{1,0,2:T(8,128)S(1)} %fusion.2) | copy-start | bytes 3145732
  95.4 25.1 %copy-start.39 = (f32[2,64,14]{1,0,2:T(2,128)S(1)}, f32[2,64,14]{1,0,2:T(2,128)}, u32[]{:S(2)}) copy-start(f32[2,64,14]{1,0,2:T(2,128)} %param.13) | copy-start | bytes 21508
  95.4 25.2 %copy-start.40 = (f32[2,64,14]{1,0,2:T(2,128)S(1)}, f32[2,64,14]{1,0,2:T(2,128)}, u32[]{:S(2)}) copy-start(f32[2,64,14]{1,0,2:T(2,128)} %param.15) | copy-start | bytes 21508
  100.8 31.4 %collective-permute-start.23 = (bf16[1536,256]{1,0:T(8,128)(2,1)}, bf16[1536,256]{1,0:T(8,128)(2,1)}, u32[]{:S(2)}, u32[]{:S(2)}) collective-permute-start(bf16[1536,256]{1,0:T(8,128)(2,1)} %get-tuple-element.125), channel_id=1, source_target_pairs={{0,8},{8,0},{16,24},{24,16},{1,9},{9,1},{17,25},{25,17},{2,10},{10... | collective-permute-start | bytes 2359304 | tf_op jit(solution)/shard_map/ppermute | solution.py:20
  101.6 31.7 %collective-permute-start.24 = (bf16[1536,256]{1,0:T(8,128)(2,1)}, bf16[1536,256]{1,0:T(8,128)(2,1)}, u32[]{:S(2)}, u32[]{:S(2)}) collective-permute-start(bf16[1536,256]{1,0:T(8,128)(2,1)} %get-tuple-element.126), channel_id=1, source_target_pairs={{0,16},{8,24},{16,0},{24,8},{1,17},{9,25},{17,1},{25,9},{2,18},{10... | collective-permute-start | bytes 2359304 | tf_op jit(solution)/shard_map/ppermute | solution.py:20
  116.3 26.7 %slice-start.2 = ((s8[7340032]{0:T(1024)(128)(4,1)}), s8[3145728]{0:T(1024)(128)(4,1)S(1)}, s32[]{:S(2)}) async-start(s8[7340032]{0:T(1024)(128)(4,1)} %bitcast.117), calls=%async_computation.2 | async-start | bytes 6291456
  118.4 22.4 %collective-permute-start.29 = (bf16[768,256]{1,0:T(8,128)(2,1)}, bf16[768,256]{1,0:T(8,128)(2,1)}, u32[]{:S(2)}, u32[]{:S(2)}) collective-permute-start(bf16[768,256]{1,0:T(8,128)(2,1)} %get-tuple-element.135), channel_id=1, source_target_pairs={{0,8},{8,0},{16,24},{24,16},{1,9},{9,1},{17,25},{25,17},{2,10},{10... | collective-permute-start | bytes 1179656 | tf_op jit(solution)/shard_map/ppermute | solution.py:20
  119.2 22.3 %collective-permute-start.30 = (bf16[768,256]{1,0:T(8,128)(2,1)}, bf16[768,256]{1,0:T(8,128)(2,1)}, u32[]{:S(2)}, u32[]{:S(2)}) collective-permute-start(bf16[768,256]{1,0:T(8,128)(2,1)} %get-tuple-element.136), channel_id=1, source_target_pairs={{0,16},{8,24},{16,0},{24,8},{1,17},{9,25},{17,1},{25,9},{2,18},{10... | collective-permute-start | bytes 1179656 | tf_op jit(solution)/shard_map/ppermute | solution.py:20
  135.6 5.8 %copy-start.26 = (bf16[1536,256]{1,0:T(8,128)(2,1)S(1)}, bf16[1536,256]{1,0:T(8,128)(2,1)}, u32[]{:S(2)}) copy-start(bf16[1536,256]{1,0:T(8,128)(2,1)} %copy-done.25) | copy-start | bytes 2359300
  135.6 5.9 %copy-start.29 = (bf16[2,768,256]{2,1,0:T(8,128)(2,1)S(1)}, bf16[2,768,256]{2,1,0:T(8,128)(2,1)}, u32[]{:S(2)}) copy-start(bf16[2,768,256]{2,1,0:T(8,128)(2,1)} %copy-done.28) | copy-start | bytes 2359300
  135.6 7.5 %slice-start.3 = ((s8[7340032]{0:T(1024)(128)(4,1)}), s8[4194304]{0:T(1024)(128)(4,1)S(1)}, s32[]{:S(2)}) async-start(s8[7340032]{0:T(1024)(128)(4,1)} %bitcast.117), calls=%async_computation.3 | async-start | bytes 8388608
  138.6 21.3 %collective-permute-start.27 = (bf16[1536,256]{1,0:T(8,128)(2,1)}, bf16[1536,256]{1,0:T(8,128)(2,1)S(1)}, u32[]{:S(2)}, u32[]{:S(2)}) collective-permute-start(bf16[1536,256]{1,0:T(8,128)(2,1)} %get-tuple-element.132), channel_id=1, source_target_pairs={{0,8},{8,0},{16,24},{24,16},{1,9},{9,1},{17,25},{25,17},{2,10},{10... | collective-permute-start | bytes 2359304 | tf_op jit(solution)/shard_map/ppermute | solution.py:20
  139.4 20.5 %collective-permute-start.28 = (bf16[1536,256]{1,0:T(8,128)(2,1)S(1)}, bf16[1536,256]{1,0:T(8,128)(2,1)S(1)}, u32[]{:S(2)}, u32[]{:S(2)}) collective-permute-start(bf16[1536,256]{1,0:T(8,128)(2,1)S(1)} %get-tuple-element.133), channel_id=1, source_target_pairs={{0,16},{8,24},{16,0},{24,8},{1,17},{9,25},{17,1},{25,9},{2,18},{10... | collective-permute-start | bytes 2359304 | tf_op jit(solution)/shard_map/ppermute | solution.py:20
  143.1 6.3 %slice-start.7 = ((s8[7340032]{0:T(1024)(128)(4,1)}), s8[3145728]{0:T(1024)(128)(4,1)S(1)}, s32[]{:S(2)}) async-start(s8[7340032]{0:T(1024)(128)(4,1)} %bitcast.121), calls=%async_computation.7 | async-start | bytes 6291456
  143.1 6.7 %copy-start.1 = (bf16[4,192,1024]{2,1,0:T(8,128)(2,1)S(1)}, bf16[4,192,1024]{2,1,0:T(8,128)(2,1)}, u32[]{:S(2)}) copy-start(bf16[4,192,1024]{2,1,0:T(8,128)(2,1)} %copy-done) | copy-start | bytes 4718596
  143.1 6.8 %copy-start.10 = (bf16[4,64,1024]{2,1,0:T(8,128)(2,1)S(1)}, bf16[4,64,1024]{2,1,0:T(8,128)(2,1)}, u32[]{:S(2)}) copy-start(bf16[4,64,1024]{2,1,0:T(8,128)(2,1)} %copy-done.8) | copy-start | bytes 1572868
  143.2 7.1 %copy-start.19 = (bf16[2,256,1024]{2,1,0:T(8,128)(2,1)S(1)}, bf16[2,256,1024]{2,1,0:T(8,128)(2,1)}, u32[]{:S(2)}) copy-start(bf16[2,256,1024]{2,1,0:T(8,128)(2,1)} %copy-done.18) | copy-start | bytes 3145732
  160.0 7.8 %collective-permute-start.31 = (bf16[768,256]{1,0:T(8,128)(2,1)S(1)}, bf16[768,256]{1,0:T(8,128)(2,1)S(1)}, u32[]{:S(2)}, u32[]{:S(2)}) collective-permute-start(bf16[768,256]{1,0:T(8,128)(2,1)S(1)} %get-tuple-element.141), channel_id=1, source_target_pairs={{0,8},{8,0},{16,24},{24,16},{1,9},{9,1},{17,25},{25,17},{2,10},{10... | collective-permute-start | bytes 1179656 | tf_op jit(solution)/shard_map/ppermute | solution.py:20
  160.7 7.8 %collective-permute-start.32 = (bf16[768,256]{1,0:T(8,128)(2,1)S(1)}, bf16[768,256]{1,0:T(8,128)(2,1)S(1)}, u32[]{:S(2)}, u32[]{:S(2)}) collective-permute-start(bf16[768,256]{1,0:T(8,128)(2,1)S(1)} %get-tuple-element.142), channel_id=1, source_target_pairs={{0,16},{8,24},{16,0},{24,8},{1,17},{9,25},{17,1},{25,9},{2,18},{10... | collective-permute-start | bytes 1179656 | tf_op jit(solution)/shard_map/ppermute | solution.py:20
  174.6 14.5 %copy-start.2 = (bf16[4,192,1024]{2,1,0:T(8,128)(2,1)S(1)}, bf16[4,192,1024]{2,1,0:T(8,128)(2,1)}, u32[]{:S(2)}) copy-start(bf16[4,192,1024]{2,1,0:T(8,128)(2,1)} %copy-done) | copy-start | bytes 4718596
  174.6 14.5 %copy-start.11 = (bf16[4,64,1024]{2,1,0:T(8,128)(2,1)S(1)}, bf16[4,64,1024]{2,1,0:T(8,128)(2,1)}, u32[]{:S(2)}) copy-start(bf16[4,64,1024]{2,1,0:T(8,128)(2,1)} %copy-done.8) | copy-start | bytes 1572868
  174.6 14.5 %copy-start.20 = (bf16[2,256,1024]{2,1,0:T(8,128)(2,1)S(1)}, bf16[2,256,1024]{2,1,0:T(8,128)(2,1)}, u32[]{:S(2)}) copy-start(bf16[2,256,1024]{2,1,0:T(8,128)(2,1)} %copy-done.18) | copy-start | bytes 3145732
  176.7 2.7 %collective-permute-start.33 = (bf16[4,4,32,1024]{3,2,1,0:T(8,128)(2,1)S(1)}, bf16[4,4,32,1024]{3,2,1,0:T(8,128)(2,1)S(1)}, u32[]{:S(2)}, u32[]{:S(2)}) collective-permute-start(bf16[4,4,32,1024]{3,2,1,0:T(8,128)(2,1)S(1)} %pad_maximum_fusion), channel_id=1, source_target_pairs={{0,1},{1,0},{2,3},{3,2},{4,5},{5,4},{6,7},{7,6},{8,9},{9,8},{10,11... | collective-permute-start | bytes 3145736 | tf_op jit(solution)/shard_map/ppermute | solution.py:37
  180.6 29.7 %collective-permute-start.36 = (bf16[4,32,1024]{2,1,0:T(8,128)(2,1)}, bf16[4,32,1024]{2,1,0:T(8,128)(2,1)}, u32[]{:S(2)}, u32[]{:S(2)}) collective-permute-start(bf16[4,32,1024]{2,1,0:T(8,128)(2,1)} %get-tuple-element.176), channel_id=1, source_target_pairs={{0,2},{1,3},{2,4},{3,5},{4,6},{5,7},{6,0},{7,1},{8,10},{9,11},{10,... | collective-permute-start | bytes 786440 | tf_op jit(solution)/shard_map/ppermute | solution.py:25
  186.7 23.7 %collective-permute-start.35 = (bf16[4,32,1024]{2,1,0:T(8,128)(2,1)}, bf16[4,32,1024]{2,1,0:T(8,128)(2,1)}, u32[]{:S(2)}, u32[]{:S(2)}) collective-permute-start(bf16[4,32,1024]{2,1,0:T(8,128)(2,1)} %get-tuple-element.177), channel_id=1, source_target_pairs={{0,4},{1,5},{2,6},{3,7},{4,0},{5,1},{6,2},{7,3},{8,12},{9,13},{10,... | collective-permute-start | bytes 786440 | tf_op jit(solution)/shard_map/ppermute | solution.py:25
  188.3 22.1 %collective-permute-start.34 = (bf16[4,32,1024]{2,1,0:T(8,128)(2,1)S(1)}, bf16[4,32,1024]{2,1,0:T(8,128)(2,1)}, u32[]{:S(2)}, u32[]{:S(2)}) collective-permute-start(bf16[4,32,1024]{2,1,0:T(8,128)(2,1)S(1)} %get-tuple-element.175), channel_id=1, source_target_pairs={{0,6},{1,7},{2,0},{3,1},{4,2},{5,3},{6,4},{7,5},{8,14},{9,15},{10,... | collective-permute-start | bytes 786440 | tf_op jit(solution)/shard_map/ppermute | solution.py:25
  191.0 9.7 %copy-start.5 = (bf16[4,256,1024]{2,1,0:T(8,128)(2,1)S(1)}, bf16[4,256,1024]{2,1,0:T(8,128)(2,1)}, u32[]{:S(2)}) copy-start(bf16[4,256,1024]{2,1,0:T(8,128)(2,1)} %copy-done.4) | copy-start | bytes 6291460
  191.0 9.7 %copy-start.13 = (bf16[2,1024,768]{2,1,0:T(8,128)(2,1)S(1)}, bf16[2,1024,768]{2,1,0:T(8,128)(2,1)}, u32[]{:S(2)}) copy-start(bf16[2,1024,768]{2,1,0:T(8,128)(2,1)} %copy-done.12) | copy-start | bytes 9437188
  200.7 9.7 %copy-start.37 = (f32[4,2,32,1024]{3,2,0,1:T(8,128)S(1)}, f32[4,2,32,1024]{3,2,0,1:T(8,128)}, u32[]{:S(2)}) copy-start(f32[4,2,32,1024]{3,2,0,1:T(8,128)} %copy-done.36) | copy-start | bytes 3145732
  211.8 11.3 %collective-permute-start.39 = (bf16[32,1024]{1,0:T(8,128)(2,1)S(1)}, bf16[32,1024]{1,0:T(8,128)(2,1)S(1)}, u32[]{:S(2)}, u32[]{:S(2)}) collective-permute-start(bf16[32,1024]{1,0:T(8,128)(2,1)S(1)} %get-tuple-element.183), channel_id=1, source_target_pairs={{0,24},{8,16},{16,8},{24,0},{1,25},{9,17},{17,9},{25,1},{2,26},{10... | collective-permute-start | bytes 196616 | tf_op jit(solution)/shard_map/ppermute | solution.py:20
  214.2 9.0 %collective-permute-start.38 = (bf16[32,1024]{1,0:T(8,128)(2,1)S(1)}, bf16[32,1024]{1,0:T(8,128)(2,1)S(1)}, u32[]{:S(2)}, u32[]{:S(2)}) collective-permute-start(bf16[32,1024]{1,0:T(8,128)(2,1)S(1)} %get-tuple-element.184), channel_id=1, source_target_pairs={{0,16},{8,24},{16,0},{24,8},{1,17},{9,25},{17,1},{25,9},{2,18},{10... | collective-permute-start | bytes 196616 | tf_op jit(solution)/shard_map/ppermute | solution.py:20
  214.7 8.4 %collective-permute-start.37 = (bf16[32,1024]{1,0:T(8,128)(2,1)S(1)}, bf16[32,1024]{1,0:T(8,128)(2,1)S(1)}, u32[]{:S(2)}, u32[]{:S(2)}) collective-permute-start(bf16[32,1024]{1,0:T(8,128)(2,1)S(1)} %get-tuple-element.185), channel_id=1, source_target_pairs={{0,8},{8,0},{16,24},{24,16},{1,9},{9,1},{17,25},{25,17},{2,10},{10... | collective-permute-start | bytes 196616 | tf_op jit(solution)/shard_map/ppermute | solution.py:20
  (25 other events, 65.4 us)
